TPU v7x, 32 devices: a whole 2x2x4 slice. The times are simulated.
32 devices in a mesh: batch: 4 (over y, x), seq: 4 (over z), chip: 2 (over core).
Axes of the slice: x: 2, y: 2, z: 4, core: 2. Of those that a mesh axis runs over, the one named last changes fastest.
Arguments:
- tokens: bfloat16 [4096, 2048], P(('batch', 'seq', 'chip')), may hold values from -6 to 6
- starts: int32 [4096], P(('batch', 'seq', 'chip')), may hold values from 0 to 1, as said below
- w_query: bfloat16 [2048, 2048], P(('batch', 'seq', 'chip')), may hold values from -0.125 to 0.125
- w_forget: bfloat16 [2048, 2048], P(('batch', 'seq', 'chip')), may hold values from -0.125 to 0.125
- w_input: bfloat16 [2048, 2048], P(('batch', 'seq', 'chip')), may hold values from -0.125 to 0.125
- w_output: bfloat16 [2048, 2048], P(('batch', 'seq', 'chip')), may hold values from -0.125 to 0.125
- gain_mix: float32 [2048], P(('batch', 'seq', 'chip')), may hold values from 0.5 to 1.5
- lower_bound: float32 [2048], P(('batch', 'seq', 'chip')), may hold values from 0.9 to 0.9995
- gain_state: float32 [2048], P(('batch', 'seq', 'chip')), may hold values from 0.5 to 1.5
- w_gate: bfloat16 [2048, 5632], P(('batch', 'seq', 'chip')), may hold values from -0.125 to 0.125
- w_up: bfloat16 [2048, 5632], P(('batch', 'seq', 'chip')), may hold values from -0.125 to 0.125
- w_down: bfloat16 [5632, 2048], P(('batch', 'seq', 'chip')), may hold values from -0.078125 to 0.078125
- gain_ffn: float32 [2048], P(('batch', 'seq', 'chip')), may hold values from 0.5 to 1.5
- cotangent: bfloat16 [4096, 2048], P(('batch', 'seq', 'chip')), may hold values from -6 to 6
Outputs:
- output: bfloat16 [4096, 2048], P(('batch', 'seq', 'chip'))
- grad_tokens: float32 [4096, 2048], P(('batch', 'seq', 'chip'))
- grad_query: float32 [2048, 2048], P(('batch', 'seq', 'chip'))
- grad_forget: float32 [2048, 2048], P(('batch', 'seq', 'chip'))
- grad_input: float32 [2048, 2048], P(('batch', 'seq', 'chip'))
- grad_output: float32 [2048, 2048], P(('batch', 'seq', 'chip'))
- grad_gain_mix: float32 [2048], P(('batch', 'seq', 'chip'))
- grad_lower: float32 [2048], P(('batch', 'seq', 'chip'))
- grad_gain_state: float32 [2048], P(('batch', 'seq', 'chip'))
- grad_gate: float32 [2048, 5632], P(('batch', 'seq', 'chip'))
- grad_up: float32 [2048, 5632], P(('batch', 'seq', 'chip'))
- grad_down: float32 [5632, 2048], P(('batch', 'seq', 'chip'))
- grad_gain_ffn: float32 [2048], P(('batch', 'seq', 'chip'))
Inputs may be any that keep to these rules, and one draw needn't show every extreme that they name: `starts`: in each group's 1024 rows (counted from 0) a document begins at row 0 and at exactly two more rows: one at a row from 1 to 127, one at a row from 896 to 1023.
All inputs are finite; a program needn't handle non-finite values.
Results may differ from a plain program's by a relative error of at most 0.0095.
Values may be sent and summed in bfloat16 or wider, within the bound.
No kernel may reach another device: no remote copies, remote signals or barrier semaphores. Data moves between devices by JAX's collectives and lax.ppermute only.
A program may use at most 448 MiB of HBM per device.

v0:
```python
from functools import partial

import jax
import jax.numpy as jnp
from jax import lax
from jax.sharding import PartitionSpec as P

HDIM = 128
BLOCK = 64


EPSILON = 1e-06
RESET_LOG = -30.0
EXACT_PRECISION = lax.Precision.HIGHEST


def shifted(x, axis, by):
    count = lax.axis_size(axis)
    pairs = [(i, i + by) for i in range(count) if 0 <= i + by < count]
    return lax.ppermute(x, axis, pairs)


def root_norm(values, gain):
    return values * lax.rsqrt(jnp.mean(values * values, axis=-1, keepdims=True) + EPSILON) * gain


def matmul(left, right):
    return jnp.dot(left, right, preferred_element_type=jnp.float32)


def weight_grad(left, right):
    return lax.dot_general(
        left, right, (((0,), (0,)), ((), ())), preferred_element_type=jnp.float32
    )


def input_grad(upstream, weight):
    return lax.dot_general(
        upstream, weight, (((1,), (1,)), ((), ())), preferred_element_type=jnp.float32
    )


def block_step(incoming_state, pieces):
    query_act, key_act, value_activation, log_decay = pieces
    cumulative = jnp.cumsum(log_decay, axis=0)
    query_expansion = query_act * jnp.exp(cumulative)
    key_shrink = key_act * jnp.exp(-cumulative)
    scores = jnp.einsum("thk,shk->hts", query_expansion, key_shrink, precision=EXACT_PRECISION)
    block_rows = query_act.shape[0]
    causal = jnp.arange(block_rows)[:, None] >= jnp.arange(block_rows)[None, :]
    scores = jnp.where(causal[None], scores, 0.0)
    output_values = jnp.einsum("hts,shv->thv", scores, value_activation, precision=EXACT_PRECISION)
    output_values = output_values + jnp.einsum(
        "aju,jup->ajp", query_expansion, incoming_state, precision=EXACT_PRECISION
    )
    block_count_total = cumulative[-1]
    key_suffix_factor = key_act * jnp.exp(block_count_total[None] - cumulative)
    outgoing_state = jnp.exp(block_count_total)[..., None] * incoming_state + jnp.einsum(
        "lcg,lcw->cgw", key_suffix_factor, value_activation, precision=EXACT_PRECISION
    )
    return (outgoing_state, output_values)


def local_mix(query_act, key_act, value_activation, log_decay):
    row_count = query_act.shape[0]
    head_count = query_act.shape[1] // HDIM
    shaped = tuple(
        (
            array.reshape(row_count // BLOCK, BLOCK, head_count, HDIM)
            for array in (query_act, key_act, value_activation, log_decay)
        )
    )
    zero_state = jnp.zeros((head_count, HDIM, HDIM), jnp.float32)
    end_state, block_outs = lax.scan(block_step, zero_state, shaped)
    reach = jnp.exp(jnp.cumsum(log_decay.reshape(row_count, head_count, HDIM), axis=0))
    query_extent = query_act.reshape(row_count, head_count, HDIM) * reach
    return (block_outs.reshape(row_count, head_count, HDIM), reach[-1], end_state, query_extent)


def gate_piece(forget_pre, lower_bound, starts):
    forget_gate = lower_bound + (1.0 - lower_bound) * jax.nn.sigmoid(forget_pre)
    log_decay = jnp.where(starts[:, None] == 1, RESET_LOG, jnp.log(forget_gate))
    return (1.0 - forget_gate, log_decay)


def swiglu_piece(gate_act, up_act):
    return jax.nn.silu(gate_act) * up_act


def carry_forward(total_decay, end_state):

    def turn(turn_index, incoming):
        return shifted(
            (total_decay[..., None] * incoming + end_state).astype(jnp.bfloat16), ("seq", "chip"), 1
        ).astype(jnp.float32)

    return lax.fori_loop(0, lax.axis_size(("seq", "chip")) - 1, turn, jnp.zeros_like(end_state))


def carry_backward(total_decay, device_gradient):

    def turn(turn_index, incoming):
        return shifted(
            (total_decay[..., None] * incoming + device_gradient).astype(jnp.bfloat16),
            ("seq", "chip"),
            -1,
        ).astype(jnp.float32)

    return lax.fori_loop(
        0, lax.axis_size(("seq", "chip")) - 1, turn, jnp.zeros_like(device_gradient)
    )


def body(
    tokens,
    starts,
    w_query,
    w_forget,
    w_input,
    w_output,
    gain_mix,
    lower_bound,
    gain_state,
    w_gate,
    w_up,
    w_down,
    gain_ffn,
    cotangent,
):
    full_query, full_forget, full_input, full_output = (
        lax.all_gather(w_query, ("batch", "seq", "chip"), axis=0, tiled=True),
        lax.all_gather(w_forget, ("batch", "seq", "chip"), axis=0, tiled=True),
        lax.all_gather(w_input, ("batch", "seq", "chip"), axis=0, tiled=True),
        lax.all_gather(w_output, ("batch", "seq", "chip"), axis=0, tiled=True),
    )
    full_gain_mix, full_lower, full_gain_state, full_gain_ffn = (
        lax.all_gather(gain_mix, ("batch", "seq", "chip"), axis=0, tiled=True),
        lax.all_gather(lower_bound, ("batch", "seq", "chip"), axis=0, tiled=True),
        lax.all_gather(gain_state, ("batch", "seq", "chip"), axis=0, tiled=True),
        lax.all_gather(gain_ffn, ("batch", "seq", "chip"), axis=0, tiled=True),
    )
    full_gate, full_up, full_down = (
        lax.all_gather(w_gate, ("batch", "seq", "chip"), axis=0, tiled=True),
        lax.all_gather(w_up, ("batch", "seq", "chip"), axis=0, tiled=True),
        lax.all_gather(w_down, ("batch", "seq", "chip"), axis=0, tiled=True),
    )
    row_count = tokens.shape[0]
    inputs = tokens.astype(jnp.float32)
    normed_in, norm_in_pull = jax.vjp(root_norm, inputs, full_gain_mix)
    normed_in_low = normed_in.astype(jnp.bfloat16)
    query_pre = matmul(normed_in_low, full_query)
    forget_pre = matmul(normed_in_low, full_forget)
    value_activation = matmul(normed_in_low, full_input)
    query_act, query_pull = jax.vjp(jax.nn.silu, query_pre)
    (key_act, log_decay), gate_pull = jax.vjp(
        partial(gate_piece, starts=starts), forget_pre, full_lower
    )
    (device_output, total_decay, end_state, query_extent), mix_pull = jax.vjp(
        local_mix, query_act, key_act, value_activation, log_decay
    )
    incoming_state = carry_forward(total_decay, end_state)
    mixed = (
        device_output
        + jnp.einsum("aju,jup->ajp", query_extent, incoming_state, precision=EXACT_PRECISION)
    ).reshape(row_count, -1)
    normed_mix, norm_mix_pull = jax.vjp(root_norm, mixed, full_gain_state)
    normed_mix_low = normed_mix.astype(jnp.bfloat16)
    residual = inputs + matmul(normed_mix_low, full_output)
    normed_ffn, norm_ffn_pull = jax.vjp(root_norm, residual, full_gain_ffn)
    normed_ffn_low = normed_ffn.astype(jnp.bfloat16)
    gate_act = matmul(normed_ffn_low, full_gate)
    up_act = matmul(normed_ffn_low, full_up)
    hidden, swiglu_pull = jax.vjp(swiglu_piece, gate_act, up_act)
    hidden_low = hidden.astype(jnp.bfloat16)
    output = (residual + matmul(hidden_low, full_down)).astype(jnp.bfloat16)
    full_gate, full_up, full_down = (
        lax.all_gather(w_gate, ("batch", "seq", "chip"), axis=0, tiled=True),
        lax.all_gather(w_up, ("batch", "seq", "chip"), axis=0, tiled=True),
        lax.all_gather(w_down, ("batch", "seq", "chip"), axis=0, tiled=True),
    )
    grad_down_full = weight_grad(hidden_low, cotangent)
    grad_hidden = input_grad(cotangent, full_down)
    grad_gate_act, grad_up_act = swiglu_pull(grad_hidden)
    grad_gate_low = grad_gate_act.astype(jnp.bfloat16)
    grad_up_low = grad_up_act.astype(jnp.bfloat16)
    grad_normed_ffn = input_grad(grad_gate_low, full_gate) + input_grad(grad_up_low, full_up)
    grad_residual_part, grad_gain_ffn_full = norm_ffn_pull(grad_normed_ffn)
    grad_gate_full = weight_grad(normed_ffn_low, grad_gate_low)
    grad_up_full = weight_grad(normed_ffn_low, grad_up_low)
    grad_down, grad_gate, grad_up, grad_gain_ffn = (
        lax.psum_scatter(grad_down_full, ("batch", "seq", "chip"), scatter_dimension=0, tiled=True),
        lax.psum_scatter(grad_gate_full, ("batch", "seq", "chip"), scatter_dimension=0, tiled=True),
        lax.psum_scatter(grad_up_full, ("batch", "seq", "chip"), scatter_dimension=0, tiled=True),
        lax.psum_scatter(
            grad_gain_ffn_full, ("batch", "seq", "chip"), scatter_dimension=0, tiled=True
        ),
    )
    grad_residual = cotangent.astype(jnp.float32) + grad_residual_part
    full_query, full_forget, full_input, full_output = (
        lax.all_gather(w_query, ("batch", "seq", "chip"), axis=0, tiled=True),
        lax.all_gather(w_forget, ("batch", "seq", "chip"), axis=0, tiled=True),
        lax.all_gather(w_input, ("batch", "seq", "chip"), axis=0, tiled=True),
        lax.all_gather(w_output, ("batch", "seq", "chip"), axis=0, tiled=True),
    )
    grad_branch = grad_residual.astype(jnp.bfloat16)
    grad_output_full = weight_grad(normed_mix_low, grad_branch)
    grad_normed_mix = input_grad(grad_branch, full_output)
    grad_mixed, grad_gain_state_full = norm_mix_pull(grad_normed_mix)
    gradient_mixed_per_head = grad_mixed.reshape(query_extent.shape)
    gradient_query_extent = jnp.einsum(
        "bup,usp->bus", gradient_mixed_per_head, incoming_state, precision=EXACT_PRECISION
    )
    device_gradient = jnp.einsum(
        "ojp,ojd->jpd", query_extent, gradient_mixed_per_head, precision=EXACT_PRECISION
    )
    grad_next = carry_backward(total_decay, device_gradient)
    grad_total = jnp.sum(grad_next * incoming_state, axis=-1)
    grad_query_act, grad_key_act, grad_value_act, grad_log_decay = mix_pull(
        (gradient_mixed_per_head, grad_total, grad_next, gradient_query_extent)
    )
    (grad_query_pre,) = query_pull(grad_query_act)
    grad_forget_pre, grad_lower_full = gate_pull((grad_key_act, grad_log_decay))
    grad_query_low = grad_query_pre.astype(jnp.bfloat16)
    grad_forget_low = grad_forget_pre.astype(jnp.bfloat16)
    grad_value_low = grad_value_act.astype(jnp.bfloat16)
    grad_normed_in = (
        input_grad(grad_query_low, full_query)
        + input_grad(grad_forget_low, full_forget)
        + input_grad(grad_value_low, full_input)
    )
    grad_inputs_part, grad_gain_mix_full = norm_in_pull(grad_normed_in)
    grad_tokens = grad_residual + grad_inputs_part
    grad_query, grad_forget, grad_input, grad_output, grad_gain_mix, grad_lower, grad_gain_state = (
        lax.psum_scatter(
            weight_grad(normed_in_low, grad_query_low),
            ("batch", "seq", "chip"),
            scatter_dimension=0,
            tiled=True,
        ),
        lax.psum_scatter(
            weight_grad(normed_in_low, grad_forget_low),
            ("batch", "seq", "chip"),
            scatter_dimension=0,
            tiled=True,
        ),
        lax.psum_scatter(
            weight_grad(normed_in_low, grad_value_low),
            ("batch", "seq", "chip"),
            scatter_dimension=0,
            tiled=True,
        ),
        lax.psum_scatter(
            grad_output_full, ("batch", "seq", "chip"), scatter_dimension=0, tiled=True
        ),
        lax.psum_scatter(
            grad_gain_mix_full, ("batch", "seq", "chip"), scatter_dimension=0, tiled=True
        ),
        lax.psum_scatter(
            grad_lower_full, ("batch", "seq", "chip"), scatter_dimension=0, tiled=True
        ),
        lax.psum_scatter(
            grad_gain_state_full, ("batch", "seq", "chip"), scatter_dimension=0, tiled=True
        ),
    )
    return (
        output,
        grad_tokens,
        grad_query,
        grad_forget,
        grad_input,
        grad_output,
        grad_gain_mix,
        grad_lower,
        grad_gain_state,
        grad_gate,
        grad_up,
        grad_down,
        grad_gain_ffn,
    )


def solution(mesh):
    return jax.shard_map(
        body,
        mesh=mesh,
        in_specs=(
            P(("batch", "seq", "chip"), None),
            P(("batch", "seq", "chip")),
            P(("batch", "seq", "chip"), None),
            P(("batch", "seq", "chip"), None),
            P(("batch", "seq", "chip"), None),
            P(("batch", "seq", "chip"), None),
            P(("batch", "seq", "chip")),
            P(("batch", "seq", "chip")),
            P(("batch", "seq", "chip")),
            P(("batch", "seq", "chip"), None),
            P(("batch", "seq", "chip"), None),
            P(("batch", "seq", "chip"), None),
            P(("batch", "seq", "chip")),
            P(("batch", "seq", "chip"), None),
        ),
        out_specs=(
            P(("batch", "seq", "chip"), None),
            P(("batch", "seq", "chip"), None),
            P(("batch", "seq", "chip"), None),
            P(("batch", "seq", "chip"), None),
            P(("batch", "seq", "chip"), None),
            P(("batch", "seq", "chip"), None),
            P(("batch", "seq", "chip")),
            P(("batch", "seq", "chip")),
            P(("batch", "seq", "chip")),
            P(("batch", "seq", "chip"), None),
            P(("batch", "seq", "chip"), None),
            P(("batch", "seq", "chip"), None),
            P(("batch", "seq", "chip")),
        ),
        check_vma=False,
    )
```

profile of v0, /device:TPU:2, one launch (start us, length us, event | category | flops | bytes accessed | tf_op | source)
XLA Modules:
  0.0 3168.4 jit_solution(5561142566020601937)
XLA Ops:
  15.4 42.1 %all-reduce.11 = (f32[2048]{0:T(1024)S(1)}, f32[2048]{0:T(1024)S(1)}, f32[2048]{0:T(1024)S(1)}, f32[2048]{0:T(1024)S(1)}) all-reduce(f32[2048]{0:T(1024)S(1)} %dynamic-update-slice.1, f32[2048]{0:T(1024)S(1)} %dynamic-update-slice, f32[2048]{0:T(1024)S(1)} %dynamic-update-slice.2, ...), channel_id=1, replica_groups=mesh['batch'=4,'seq'=4,'chip'=2] {'batch','seq','chip'}, use_global_device_ids=true, to_apply=%add.3 | all-reduce | flops 8192 | bytes 65536
  60.0 29.7 all-gather.8.cloned.1.call-done
  97.3 71.4 %all-gather.12.cloned.1.call-done = bf16[2048,2048]{1,0:T(8,128)(2,1)} async-done(((bf16[64,2048]{1,0:T(8,128)(2,1)}), bf16[2048,2048]{1,0:T(8,128)(2,1)}) %all-gather.12.cloned.1.call-update) | async-done | bytes 8388624 | tf_op jit(solution)/shard_map/all_gather | solution.py:131
  176.9 70.8 %all-gather.10.cloned.1.call-done = bf16[2048,2048]{1,0:T(8,128)(2,1)} async-done(((bf16[64,2048]{1,0:T(8,128)(2,1)}), bf16[2048,2048]{1,0:T(8,128)(2,1)}) %all-gather.10.cloned.1.call-update) | async-done | bytes 8388624 | tf_op jit(solution)/shard_map/all_gather | solution.py:133
  266.1 29.9 while.80
  301.1 142.6 %while.81 = (s32[]{:T(128)}, f32[16,128,128]{2,1,0:T(8,128)}, f32[1,16,128]{2,1,0:T(8,128)S(1)}, f32[16,128,128]{2,1,0:T(8,128)S(1)}, s32[]{:T(128)}, /*index=5*/s32[]{:T(128)}) while((s32[]{:T(128)}, f32[16,128,128]{2,1,0:T(8,128)}, f32[1,16,128]{2,1,0:T(8,128)S(1)}, f32[16,128,128]{2,1,0:T(8,128)S(1)}, s32[]{:T(128)}, ...), condition=%wide.region_6.7_spmd.clone, body=%wide.region_5.6_spmd.clone.sunk | while | flops 1310723 | bytes 6299767 | solution.py:97
  309.6 19.1 collective-permute-start
  348.2 18.7 collective-permute-start
  372.0 20.2 collective-permute-start
  420.9 19.4 collective-permute-start
  456.3 31.7 %all-gather.16.cloned.1.call-done = bf16[2048,5632]{1,0:T(8,128)(2,1)} async-done(((bf16[64,5632]{1,0:T(8,128)(2,1)}), bf16[2048,5632]{1,0:T(8,128)(2,1)}) %all-gather.16.cloned.1.call-update) | async-done | bytes 23068688 | tf_op jit(solution)/shard_map/all_gather | solution.py:143
  500.5 139.3 %all-gather.18.cloned.1.call-done = bf16[2048,5632]{1,0:T(8,128)(2,1)} async-done(((bf16[64,5632]{1,0:T(8,128)(2,1)}), bf16[2048,5632]{1,0:T(8,128)(2,1)}) %all-gather.18.cloned.1.call-update) | async-done | bytes 23068688 | tf_op jit(solution)/shard_map/all_gather | solution.py:144
  652.1 133.4 %all-gather.20.cloned.1.call-done = bf16[5632,2048]{1,0:T(8,128)(2,1)} async-done(((bf16[176,2048]{1,0:T(8,128)(2,1)}), bf16[5632,2048]{1,0:T(8,128)(2,1)}) %all-gather.20.cloned.1.call-update) | async-done | bytes 23068688 | tf_op jit(solution)/shard_map/all_gather | solution.py:145
  849.4 164.2 %while.82 = (s32[]{:T(128)}, f32[16,128,128]{2,1,0:T(8,128)S(1)}, f32[1,16,128]{2,1,0:T(8,128)S(1)}, f32[16,128,128]{2,1,0:T(8,128)}, s32[]{:T(128)}, /*index=5*/s32[]{:T(128)}) while((s32[]{:T(128)}, f32[16,128,128]{2,1,0:T(8,128)S(1)}, f32[1,16,128]{2,1,0:T(8,128)S(1)}, f32[16,128,128]{2,1,0:T(8,128)}, s32[]{:T(128)}, ...), condition=%wide.region_12.13_spmd.clone, body=%wide.region_11.12_spmd.clone.sunk | while | flops 1310723 | bytes 6299767 | solution.py:109
  860.8 21.2 collective-permute-done.1
  886.8 21.3 collective-permute-done.1
  913.0 21.3 collective-permute-done.1
  939.1 21.3 collective-permute-done.1
  965.2 21.1 collective-permute-done.1
  991.1 21.3 collective-permute-done.1
  1021.5 41.2 %while.79 = (s32[]{:T(128)}, f32[16,128,128]{2,1,0:T(8,128)S(1)}, f32[2,64,16,128]{3,2,1,0:T(8,128)}, f32[2,64,16,128]{3,1,2,0:T(8,128)}, bf16[2,64,16,128]{3,1,...) while((s32[]{:T(128)}, f32[16,128,128]{2,1,0:T(8,128)S(1)}, ...), condition=%wide.region_17.18_spmd.clone, body=%wide.region_13.17_spmd.clone.sunk | while | flops 1219952640 | bytes 89498256 | solution.py:74
  1077.4 20.0 reduce_window_sum.54
  1133.2 18.3 fusion.123
  1152.9 18.6 fusion.124
  1173.0 18.3 fusion.125
  1209.6 60.2 %all-reduce.10 = (f32[2048]{0:T(1024)S(1)}, f32[2048]{0:T(1024)S(1)}, f32[2048]{0:T(1024)S(1)}, f32[2048]{0:T(1024)S(1)}) all-reduce(f32[2048]{0:T(1024)S(1)} %get-tuple-element.927, f32[2048]{0:T(1024)S(1)} %negate_add_fusion, f32[2048]{0:T(1024)S(1)} %copy-done.68, ...), channel_id=6, replica_groups=mesh['batch'=4,'seq'=4,'chip'=2] {'batch','seq','chip'}, use_global_device_ids=true, to_apply=%region_26.27.clone | all-reduce | flops 8192 | bytes 65536
  1286.9 25.6 reduce-scatter.10.cloned.1.call-done
  1312.4 187.1 %reduce-scatter.12.cloned.1.call-done = f32[64,2048]{1,0:T(8,128)} async-done(((f32[2048,2048]{1,0:T(8,128)}), f32[64,2048]{1,0:T(8,128)}) %reduce-scatter.12.cloned.1.call-update) | async-done | bytes 524304 | tf_op jit(solution)/shard_map/reduce_scatter | solution.py:246
  1499.5 187.3 %reduce-scatter.8.cloned.1.call-done = f32[64,2048]{1,0:T(8,128)} async-done(((f32[2048,2048]{1,0:T(8,128)}), f32[64,2048]{1,0:T(8,128)}) %reduce-scatter.8.cloned.1.call-update) | async-done | bytes 524304 | tf_op jit(solution)/shard_map/reduce_scatter | solution.py:234
  1686.8 492.4 %reduce-scatter.16.cloned.1.call-done = f32[64,5632]{1,0:T(8,128)} async-done(((f32[2048,5632]{1,0:T(8,128)}), f32[64,5632]{1,0:T(8,128)}) %reduce-scatter.16.cloned.1.call-update) | async-done | bytes 1441808 | tf_op jit(solution)/shard_map/reduce_scatter | solution.py:192
  2179.2 491.3 %reduce-scatter.18.cloned.1.call-done = f32[64,5632]{1,0:T(8,128)} async-done(((f32[2048,5632]{1,0:T(8,128)}), f32[64,5632]{1,0:T(8,128)}) %reduce-scatter.18.cloned.1.call-update) | async-done | bytes 1441808 | tf_op jit(solution)/shard_map/reduce_scatter | solution.py:193
  2670.5 491.2 %reduce-scatter.20.cloned.1.call-done = f32[176,2048]{1,0:T(8,128)} async-done(((f32[5632,2048]{1,0:T(8,128)}), f32[176,2048]{1,0:T(8,128)}) %reduce-scatter.20.cloned.1.call-update) | async-done | bytes 1441808 | tf_op jit(solution)/shard_map/reduce_scatter | solution.py:191
  (436 shorter events, 417.4 us)
Async XLA Ops:
  7.2 82.5 %all-gather.8.cloned.1.call-start = ((), (), s32[]{:S(2)}) async-start(), calls=%async_computation.7 | async-start | bytes 8650752 | tf_op jit(solution)/shard_map/all_gather | solution.py:132
  7.9 160.8 %all-gather.12.cloned.1.call-start = ((), (), s32[]{:S(2)}) async-start(), calls=%async_computation.9 | async-start | bytes 8650752 | tf_op jit(solution)/shard_map/all_gather | solution.py:131
  8.7 239.1 %all-gather.10.cloned.1.call-start = ((), (), s32[]{:S(2)}) async-start(), calls=%async_computation.8 | async-start | bytes 8650752 | tf_op jit(solution)/shard_map/all_gather | solution.py:133
  9.4 440.9 %all-gather.14.cloned.1.call-start = ((), (), s32[]{:S(2)}) async-start(), calls=%async_computation.10 | async-start | bytes 8650752 | tf_op jit(solution)/shard_map/all_gather | solution.py:134
  10.0 478.1 %all-gather.16.cloned.1.call-start = ((), (), s32[]{:S(2)}) async-start(), calls=%async_computation.11 | async-start | bytes 23789568 | tf_op jit(solution)/shard_map/all_gather | solution.py:143
  10.6 629.2 %all-gather.18.cloned.1.call-start = ((), (), s32[]{:S(2)}) async-start(), calls=%async_computation.12 | async-start | bytes 23789568 | tf_op jit(solution)/shard_map/all_gather | solution.py:144
  11.1 774.3 %all-gather.20.cloned.1.call-start = ((), (), s32[]{:S(2)}) async-start(), calls=%async_computation.13 | async-start | bytes 23789568 | tf_op jit(solution)/shard_map/all_gather | solution.py:145
  11.9 1275.0 %reduce-scatter.14.cloned.1.call-start = ((), (), s32[]{:S(2)}) async-start(), calls=%async_computation.17 | async-start | bytes 17301504 | tf_op jit(solution)/shard_map/reduce_scatter | solution.py:252
  57.5 190.2 %copy-start.50 = (f32[2048]{0:T(1024)}, f32[2048]{0:T(1024)S(1)}, u32[]{:S(2)}) copy-start(f32[2048]{0:T(1024)S(1)} %get-tuple-element.1029) | copy-start | bytes 24580
  57.5 392.8 %copy-start.52 = (f32[2048]{0:T(1024)}, f32[2048]{0:T(1024)S(1)}, u32[]{:S(2)}) copy-start(f32[2048]{0:T(1024)S(1)} %get-tuple-element.1031) | copy-start | bytes 24580
  57.5 397.7 %copy-start.64 = (f32[2048]{0:T(1024)}, f32[2048]{0:T(1024)S(1)}, u32[]{:S(2)}) copy-start(f32[2048]{0:T(1024)S(1)} %get-tuple-element.1032) | copy-start | bytes 24580
  59.3 188.4 %copy-start.60 = (f32[128]{0:T(128)}, f32[128]{0:T(128)S(1)}, u32[]{:S(2)}) copy-start(f32[128]{0:T(128)S(1)} %fusion.100) | copy-start | bytes 1540
  302.2 3.9 collective-permute-start
  309.6 20.8 collective-permute-start
  333.8 10.9 collective-permute-start
  348.2 20.4 collective-permute-start
  372.0 21.9 collective-permute-start
  397.4 20.1 collective-permute-start
  420.9 21.2 collective-permute-start
  837.3 475.1 %reduce-scatter.10.cloned.1.call-start = ((), (), s32[]{:S(2)}) async-start(), calls=%async_computation.15 | async-start | bytes 17301504 | tf_op jit(solution)/shard_map/reduce_scatter | solution.py:240
  851.8 4.1 collective-permute-start.1
  859.5 22.5 collective-permute-start.1
  885.5 22.6 collective-permute-start.1
  911.7 22.6 collective-permute-start.1
  937.8 22.6 collective-permute-start.1
  963.9 22.4 collective-permute-start.1
  989.9 22.6 collective-permute-start.1
  1110.0 389.5 %reduce-scatter.12.cloned.1.call-start = ((), (), s32[]{:S(2)}) async-start(), calls=%async_computation.16 | async-start | bytes 17301504 | tf_op jit(solution)/shard_map/reduce_scatter | solution.py:246
  1119.7 567.1 %reduce-scatter.8.cloned.1.call-start = ((), (), s32[]{:S(2)}) async-start(), calls=%async_computation.14 | async-start | bytes 17301504 | tf_op jit(solution)/shard_map/reduce_scatter | solution.py:234
  1131.5 1047.6 %reduce-scatter.16.cloned.1.call-start = ((), (), s32[]{:S(2)}) async-start(), calls=%async_computation.18 | async-start | bytes 47579136 | tf_op jit(solution)/shard_map/reduce_scatter | solution.py:192
  1151.5 1519.0 %reduce-scatter.18.cloned.1.call-start = ((), (), s32[]{:S(2)}) async-start(), calls=%async_computation.19 | async-start | bytes 47579136 | tf_op jit(solution)/shard_map/reduce_scatter | solution.py:193
  1171.5 1990.1 %reduce-scatter.20.cloned.1.call-start = ((), (), s32[]{:S(2)}) async-start(), calls=%async_computation.20 | async-start | bytes 47579136 | tf_op jit(solution)/shard_map/reduce_scatter | solution.py:191
  (96 other events, 2157.8 us)
Sparse Core Ops, SparseCore 0:
  11.0 78.6 all-gather.7
  92.7 75.9 all-gather.11
  171.7 75.9 all-gather.9
  250.6 75.9 all-gather.13
  329.3 158.7 all-gather.15
  490.8 148.9 all-gather.17
  642.6 142.7 all-gather.19
  837.4 222.5 reduce-scatter.13
  1110.1 202.2 reduce-scatter.9
  1315.2 184.3 reduce-scatter.11
  1502.4 184.3 reduce-scatter.7
  1689.5 489.5 reduce-scatter.15
  2182.0 488.4 reduce-scatter.17
  2673.2 488.4 reduce-scatter.19
where the time goes:
time: 3180 us; the launch traced here: 3170 us
  waiting for transfers between devices  2500 us (79%)
  matrix products  268 us (8%)
  starting transfers between devices  116 us (4%)
  other arithmetic  102 us (3%)
  blocking collectives  102 us (3%)
  local copies, waits for them, and re-layouts  63.5 us (2%)
    reduce_scatter x1, waiting for transfers between devices, body(): lax.psum_scatter(grad_gate_full, ('batch', 'seq', 'chip'), scatter_dimens...  492 us
    reduce_scatter x1, waiting for transfers between devices, body(): lax.psum_scatter(grad_up_full, ('batch', 'seq', 'chip'), scatter_dimensio...  491 us
    reduce_scatter x1, waiting for transfers between devices, body(): lax.psum_scatter(grad_down_full, ('batch', 'seq', 'chip'), scatter_dimens...  491 us
    reduce_scatter x1, waiting for transfers between devices, body(): lax.psum_scatter(weight_grad(normed_in_low, grad_query_low), ('batch', 's...  187 us
    reduce_scatter x1, waiting for transfers between devices, body(): lax.psum_scatter(weight_grad(normed_in_low, grad_value_low), ('batch', 's...  187 us
    ppermute x14, waiting for transfers between devices, shifted(): return lax.ppermute(x, axis, pairs)  143 us
    all_gather x1, waiting for transfers between devices, body(): lax.all_gather(w_up, ('batch', 'seq', 'chip'), axis=0, tiled=True)  139 us
    all_gather x1, waiting for transfers between devices, body(): lax.all_gather(w_down, ('batch', 'seq', 'chip'), axis=0, tiled=True)  133 us
  transfers between devices with their start and end apart: 28, of which 26 were waited for; matrix products, arithmetic and copies ran while one was open for 12% of the time, Pallas kernels for 0%

commit v1 on v0

v1 whole, which is shorter than its diff:
```python
import jax
import jax.numpy as jnp
from jax import lax
from jax.sharding import PartitionSpec as P

HDIM = 128
EPSILON = 1e-06
RESET_LOG = -30.0
EXACT = lax.Precision.HIGHEST
F32 = jnp.float32
LOW = jnp.bfloat16
AXES = ("batch", "seq", "chip")


def dot(left, right):
    return jnp.dot(left, right, preferred_element_type=F32)


def dot_tn(left, right):
    return lax.dot_general(left, right, (((0,), (0,)), ((), ())), preferred_element_type=F32)


def dot_nt(left, right):
    return lax.dot_general(left, right, (((1,), (1,)), ((), ())), preferred_element_type=F32)


def inverse_rms(values):
    return lax.rsqrt(jnp.mean(values * values, axis=-1, keepdims=True) + EPSILON)


def norm_back(values, rms, scaled):
    inner = jnp.mean(scaled * values, axis=-1, keepdims=True)
    return rms * scaled - values * (rms * rms * rms * inner)


def pick(flag, first, second):
    return jnp.where(flag, first, second)


def body(
    tokens, starts, w_query, w_forget, w_input, w_output, gain_mix, lower_bound, gain_state,
    w_gate, w_up, w_down, gain_ffn, cotangent,
):
    nb, ns, nc = (lax.axis_size(a) for a in AXES)
    b, s, c = (lax.axis_index(a) for a in AXES)
    rows, width = tokens.shape
    r = w_query.shape[0]
    part = width // (nb * nc)
    ffr = w_down.shape[0]
    heads = part // HDIM
    span = nc * rows

    def from_batch(x, k):
        return lax.ppermute(x, "batch", [(i, i ^ k) for i in range(nb)])

    def from_core(x):
        return lax.ppermute(x, "chip", [(i, i ^ 1) for i in range(nc)])

    def turn(x):
        return lax.ppermute(x, "seq", [(i, (i + 1) % ns) for i in range(ns)])

    def unmixed(blocks):
        out = [list(row) for row in blocks]
        bit = 1
        while bit < nb:
            on = (b & bit) != 0
            out = [[pick(on, out[i ^ bit][j], out[i][j]) for j in range(nc)] for i in range(nb)]
            bit *= 2
        on = c != 0
        return [[pick(on, out[i][j ^ 1], out[i][j]) for j in range(nc)] for i in range(nb)]

    def gather_plane(x):
        mine = jnp.stack([x] + [from_batch(x, k) for k in range(1, nb)])
        return jnp.stack([mine, from_core(mine)], axis=1)

    def scatter_plane(x):
        both = x[:, 0] + from_core(x[:, 1].astype(LOW)).astype(F32)
        total = both[0]
        sent = both[1:].astype(LOW)
        for k in range(1, nb):
            total = total + from_batch(sent[k - 1], k).astype(F32)
        return total

    def spread_columns(x):
        own = lax.dynamic_index_in_dim(x, c, 2, keepdims=False)
        other = from_core(lax.dynamic_index_in_dim(x, c ^ 1, 2, keepdims=False))
        got = []
        for k in range(nb):
            pair = jnp.stack([lax.dynamic_index_in_dim(y, b ^ k, 1, keepdims=False) for y in (own, other)])
            pair = from_batch(pair, k) if k else pair
            got.append([pair[0], pair[1]])
        return jnp.stack([jnp.stack(row) for row in unmixed(got)])

    def collect_columns(x):
        x = x.astype(LOW)
        got = []
        for k in range(nb):
            y = lax.dynamic_index_in_dim(x, b ^ k, 0, keepdims=False)
            got.append(from_batch(y, k) if k else y)
        got = jnp.stack(got)
        own = lax.dynamic_index_in_dim(got, c, 1, keepdims=False)
        other = from_core(lax.dynamic_index_in_dim(got, c ^ 1, 1, keepdims=False))
        return unmixed([[own[k], other[k]] for k in range(nb)])

    def ring_gather(x, axis):
        shape = x.shape[:axis] + (ns,) + x.shape[axis:]
        out = jnp.zeros(shape, x.dtype)
        for k in range(ns):
            if k:
                x = turn(x)
            out = lax.dynamic_update_index_in_dim(out, x, (s - k) % ns, axis)
        return out

    def ring_scatter(x, axis):
        def block(k):
            return lax.dynamic_index_in_dim(x, (s - k) % ns, axis, keepdims=False)

        total = block(1 % ns)
        for k in range(2, ns + 1):
            total = turn(total.astype(LOW)).astype(F32) + block(k % ns)
        return total

    by_part = lambda w: w.reshape(r, nb, nc, part)
    by_unit = lambda w: w.reshape(r, nb, ns, nc, ffr).transpose(0, 1, 3, 2, 4).reshape(r, nb, nc, ns * ffr)
    forget_value = spread_columns(jnp.concatenate([by_part(w_forget), by_part(w_input)], axis=3))
    small = jnp.concatenate(
        [gain_mix, gain_state, gain_ffn, lower_bound, starts.astype(F32)]
    ).reshape(1, -1)
    plane_small = gather_plane(small)[:, :, 0]
    plane_starts = plane_small[:, :, 4 * r :].reshape(nb, span)
    vectors = [[plane_small[i, j, : 4 * r].reshape(4, r) for j in range(nc)] for i in range(nb)]
    vectors = jnp.stack([jnp.stack(row, axis=1) for row in unmixed(vectors)], axis=1)
    vectors = ring_gather(vectors, 2).reshape(4, width)
    full_gain_mix, full_gain_state, full_gain_ffn, full_lower = (vectors[i] for i in range(4))
    lower_part = lax.dynamic_slice_in_dim(full_lower, (b * nc + c) * part, part)

    plane_tokens = gather_plane(tokens).reshape(nb * span, width)
    forget_value = ring_gather(forget_value, 1).reshape(width, 2 * part)
    query_low = spread_columns(by_part(w_query))
    query_low = ring_gather(query_low, 1).reshape(width, part)
    gate_up = spread_columns(jnp.concatenate([by_unit(w_gate), by_unit(w_up)], axis=3))
    full_output = lax.all_gather(w_output, AXES, axis=0, tiled=True)
    units = ns * ffr
    gate_up = ring_gather(gate_up, 1).reshape(width, 2 * units)
    down = ring_gather(w_down, 0).reshape(units, width)
    plane_cotangent = gather_plane(cotangent).reshape(nb * span, width)

    values = plane_tokens.astype(F32)
    normed_in = (values * inverse_rms(values) * full_gain_mix).astype(LOW)
    forget_value_pre = dot(normed_in, forget_value)
    query_pre = dot(normed_in, query_low)
    split = lambda x: x.reshape(nb, span, heads, HDIM)
    lower = lower_part.reshape(heads, HDIM)
    forget_sig = jax.nn.sigmoid(split(forget_value_pre[:, :part]))
    value_act = split(forget_value_pre[:, part:])
    query_pre = split(query_pre)
    query_sig = jax.nn.sigmoid(query_pre)
    query_act = query_pre * query_sig
    forget_gate = lower + (1.0 - lower) * forget_sig
    key_act = 1.0 - forget_gate
    is_start = plane_starts[:, :, None, None] == 1.0
    log_decay = jnp.where(is_start, 0.0, jnp.log(forget_gate))

    place = jnp.arange(span)
    place = ((place // rows) ^ c) * rows + place % rows
    causal = (place[:, None] >= place[None, :]).astype(F32)
    cumulative = jnp.einsum("ts,gshk->gthk", causal, log_decay, precision=EXACT)
    count = jnp.einsum("ts,gs->gt", causal, plane_starts, precision=EXACT)
    total = jnp.sum(log_decay, axis=1)
    total_count = jnp.sum(plane_starts, axis=1)
    reach = jnp.exp(RESET_LOG * count)[:, :, None, None]
    left = jnp.exp(RESET_LOG * (total_count[:, None] - count))[:, :, None, None]
    mask = causal[None] * jnp.exp(RESET_LOG * jnp.maximum(count[:, :, None] - count[:, None, :], 0.0))
    mask = mask[:, None]
    grow = jnp.exp(cumulative)
    shrink = jnp.exp(-cumulative)
    suffix = jnp.exp(total[:, None] - cumulative) * left
    decay = jnp.exp(total + RESET_LOG * total_count[:, None, None])[..., None]
    query_ext = (query_act * grow).astype(LOW)
    key_shrink = (key_act * shrink).astype(LOW)
    key_suffix = (key_act * suffix).astype(LOW)
    value_low = value_act.astype(LOW)
    es = lambda spec, x, y: jnp.einsum(spec, x, y, preferred_element_type=F32)
    end_state = es("gthk,gthv->ghkv", key_suffix, value_low)

    def carry(local, step):
        incoming = jnp.zeros_like(local)
        for _ in range(ns - 1):
            pairs = [(i, i + step) for i in range(ns) if 0 <= i + step < ns]
            incoming = lax.ppermute((decay * incoming + local).astype(LOW), "seq", pairs).astype(F32)
        return incoming

    incoming = carry(end_state, 1)
    incoming_low = incoming.astype(LOW)
    scores = (es("gthk,gshk->ghts", query_ext, key_shrink) * mask).astype(LOW)
    mixed = es("ghts,gshv->gthv", scores, value_low)
    mixed = mixed + reach * es("gthk,ghkv->gthv", query_ext, incoming_low)

    def to_tokens(x):
        x = x.reshape(nb, nc, rows, part)
        got = jnp.stack([x[0]] + [from_batch(x[k], k) for k in range(1, nb)])
        other = from_core(got[:, 1])
        blocks = unmixed([[got[k, 0], other[k]] for k in range(nb)])
        return jnp.concatenate([y for row in blocks for y in row], axis=1)

    def to_parts(x):
        blocks = unmixed(
            [[x[:, (i * nc + j) * part : (i * nc + j + 1) * part] for j in range(nc)] for i in range(nb)]
        )
        own = jnp.stack([row[0] for row in blocks])
        other = from_core(jnp.stack([row[1] for row in blocks]))
        both = jnp.stack([own, other], axis=1)
        return jnp.stack([both[0]] + [from_batch(both[k], k) for k in range(1, nb)])

    mixed_own = to_tokens(mixed.astype(LOW)).astype(F32)
    own_tokens = tokens.astype(F32)
    mix_rms = inverse_rms(mixed_own)
    normed_mix = (mixed_own * mix_rms * full_gain_state).astype(LOW)
    residual = own_tokens + dot(normed_mix, full_output)
    ffn_rms = inverse_rms(residual)
    normed_ffn = (residual * ffn_rms * full_gain_ffn).astype(LOW)

    plane_ffn = gather_plane(normed_ffn).reshape(nb * span, width)
    gate_up_act = dot(plane_ffn, gate_up)
    gate_act, up_act = gate_up_act[:, :units], gate_up_act[:, units:]
    gate_sig = jax.nn.sigmoid(gate_act)
    gate_silu = gate_act * gate_sig
    hidden = (gate_silu * up_act).astype(LOW)
    grad_hidden = dot_nt(plane_cotangent, down)
    grad_gate_act = (grad_hidden * up_act * gate_sig * (1.0 + gate_act * (1.0 - gate_sig))).astype(LOW)
    grad_up_act = (grad_hidden * gate_silu).astype(LOW)
    grad_gate_up = jnp.concatenate([grad_gate_act, grad_up_act], axis=1)
    by_plane = lambda x: x.reshape(nb, nc, rows, width)
    grad_normed_ffn = scatter_plane(by_plane(dot_nt(grad_gate_up, gate_up)))
    output = (residual + scatter_plane(by_plane(dot(hidden, down)))).astype(LOW)

    grad_residual = cotangent.astype(F32) + norm_back(residual, ffn_rms, grad_normed_ffn * full_gain_ffn)
    grad_branch = grad_residual.astype(LOW)
    grad_mixed = norm_back(mixed_own, mix_rms, dot_nt(grad_branch, full_output) * full_gain_state)
    grad_mixed = to_parts(grad_mixed.astype(LOW)).reshape(nb, span, heads, HDIM)

    grad_down = ring_scatter(dot_tn(hidden, plane_cotangent).reshape(ns, ffr, width), 0)
    grad_gate_up = ring_scatter(dot_tn(plane_ffn, grad_gate_up).reshape(nb, ns, nc * r, 2 * units), 1)

    grad_reach = (reach * grad_mixed.astype(F32)).astype(LOW)
    grad_next = carry(es("gthk,gthv->ghkv", query_ext, grad_reach), -1)
    next_low = grad_next.astype(LOW)
    grad_scores = (es("gthv,gshv->ghts", grad_mixed, value_low) * mask).astype(LOW)
    grad_ext = es("ghts,gshk->gthk", grad_scores, key_shrink) + es("gthv,ghkv->gthk", grad_reach, incoming_low)
    grad_shrink = es("ghts,gthk->gshk", grad_scores, query_ext)
    grad_suffix = es("gthv,ghkv->gthk", value_low, next_low)
    grad_value = es("ghts,gthv->gshv", scores, grad_mixed) + es("gthk,ghkv->gthv", key_suffix, next_low)
    grad_query = grad_ext * grow
    grad_key = grad_shrink * shrink + grad_suffix * suffix
    suffix_term = key_suffix.astype(F32) * grad_suffix
    grad_cumulative = query_ext.astype(F32) * grad_ext - key_shrink.astype(F32) * grad_shrink - suffix_term
    grad_total = jnp.sum(suffix_term, axis=1) + jnp.sum(decay * incoming * grad_next, axis=-1)
    grad_log = jnp.einsum("ts,gthk->gshk", causal, grad_cumulative, precision=EXACT) + grad_total[:, None]
    grad_forget = jnp.where(is_start, 0.0, grad_log / forget_gate) - grad_key
    grad_lower = jnp.sum(grad_forget * (1.0 - forget_sig), axis=(0, 1)).reshape(1, part)
    grad_query_pre = grad_query * query_sig * (1.0 + query_pre * (1.0 - query_sig))
    grad_forget_pre = grad_forget * (1.0 - lower) * forget_sig * (1.0 - forget_sig)
    flat = lambda x: x.reshape(nb * span, part).astype(LOW)
    grad_pre = jnp.concatenate([flat(grad_forget_pre), flat(grad_value), flat(grad_query_pre)], axis=1)
    projections = jnp.concatenate([forget_value, query_low], axis=1)
    grad_normed_in = scatter_plane(by_plane(dot_nt(grad_pre, projections)))
    grad_tokens = grad_residual + norm_back(own_tokens, inverse_rms(own_tokens), grad_normed_in * full_gain_mix)
    grad_projections = ring_scatter(dot_tn(normed_in, grad_pre).reshape(nb, ns, nc * r, 3 * part), 1)

    plane_mix = to_parts(normed_mix).reshape(nb * span, part)
    plane_branch = gather_plane(grad_branch).reshape(nb * span, width)
    grad_out = dot_tn(plane_mix, plane_branch).reshape(ns // nc, nc, r, width)
    own = lax.dynamic_index_in_dim(grad_out, c, 1, keepdims=False)
    other = from_core(lax.dynamic_index_in_dim(grad_out, c ^ 1, 1, keepdims=False).astype(LOW)).astype(F32)
    grad_out = pick(c == 0, jnp.concatenate([own, other]), jnp.concatenate([other, own]))
    grad_output = ring_scatter(grad_out, 0)

    blocks = collect_columns(grad_projections.reshape(nb, nc, r, 3 * part))
    columns = lambda i: jnp.concatenate(
        [y[:, i * part : (i + 1) * part] for row in blocks for y in row], axis=1
    ).astype(F32)
    grad_w_forget, grad_w_input, grad_w_query = columns(0), columns(1), columns(2)
    blocks = collect_columns(grad_gate_up.reshape(nb, nc, r, 2 * units))
    blocks = jnp.stack([jnp.stack(row) for row in blocks]).reshape(nb, nc, r, 2, ns, ffr)
    grad_w_gate, grad_w_up = (
        blocks[:, :, :, i].transpose(2, 0, 3, 1, 4).reshape(r, w_gate.shape[1]).astype(F32) for i in range(2)
    )
    shifts = [grad_lower] + [
        lax.ppermute(grad_lower, "seq", [(i, (i + k) % ns) for i in range(ns)]) for k in range(1, ns)
    ]
    grad_lower = sum(shifts)
    other = from_core(grad_lower)
    grad_lower = pick(c == 0, jnp.concatenate([grad_lower, other], 1), jnp.concatenate([other, grad_lower], 1))[0]
    grad_lower = lax.dynamic_slice_in_dim(grad_lower, (s * nc + c) * r, r)

    def along(*pairs):
        return sum(jnp.sum(w.astype(F32) * g, axis=1) for w, g in pairs)

    grad_gain_mix = along((w_query, grad_w_query), (w_forget, grad_w_forget), (w_input, grad_w_input)) / gain_mix
    grad_gain_state = along((w_output, grad_output)) / gain_state
    grad_gain_ffn = along((w_gate, grad_w_gate), (w_up, grad_w_up)) / gain_ffn
    return (
        output, grad_tokens, grad_w_query, grad_w_forget, grad_w_input, grad_output, grad_gain_mix, grad_lower,
        grad_gain_state, grad_w_gate, grad_w_up, grad_down, grad_gain_ffn,
    )


def solution(mesh):
    flat, matrix = P(AXES), P(AXES, None)
    return jax.shard_map(
        body,
        mesh=mesh,
        in_specs=(
            matrix, flat, matrix, matrix, matrix, matrix, flat, flat, flat, matrix, matrix, matrix, flat, matrix,
        ),
        out_specs=(
            matrix, matrix, matrix, matrix, matrix, matrix, flat, flat, flat, matrix, matrix, matrix, flat,
        ),
        check_vma=False,
    )
```

time: 3180 us -> 807 us (0.25)
  waiting for transfers between devices: 2500 us -> 362 us
  matrix products: 268 us -> 93.5 us
  blocking collectives: 102 us -> 0 us
  local copies, waits for them, and re-layouts: 63.5 us -> 118 us
    reduce_scatter x7 -> x0, waiting for transfers between devices: 1870 us -> none  [the longest x1 492 us: body(): lax.psum_scatter(grad_gate_full, ('batch', 'seq', 'chip'), scatter_dimens...]
    all_gather x7 -> x1, waiting for transfers between devices: 476 us -> 0.02 us  [body(): full_output = lax.all_gather(w_output, AXES, axis=0, tiled=True)]
    ppermute x14 -> x102, waiting for transfers between devices: 143 us -> 362 us  [the longest x27 198 us: turn(): return lax.ppermute(x, 'seq', [(i, (i + 1) % ns) for i in range(ns)])]
    dot_general x48 -> x28, matrix products: 268 us -> 93.5 us  [the longest x5 29.9 us: dot(): return jnp.dot(left, right, preferred_element_type=F32)]
    unnamed x2 -> x0, blocking collectives: 102 us -> none
    ppermute x14 -> x102, starting transfers between devices: 115 us -> 92.6 us  [the longest x48 55.1 us: from_batch(): return lax.ppermute(x, 'batch', [(i, i ^ k) for i in range(nb)])]
  transfers between devices with their start and end apart: 28 -> 103, of which waited for: 26 -> 46; matrix products, arithmetic and copies ran while one was open for 12% -> 34% of each run, Pallas kernels for 0% -> 0%
where the time goes in v1:
time: 807 us; the launch traced here: 794 us
  waiting for transfers between devices  362 us (45%)
  local copies, waits for them, and re-layouts  118 us (15%)
  other arithmetic  110 us (14%)
  matrix products  93.5 us (12%)
  starting transfers between devices  92.6 us (11%)
  between operations  17.2 us (2%)
    ppermute x27, waiting for transfers between devices, turn(): return lax.ppermute(x, 'seq', [(i, (i + 1) % ns) for i in range(ns)])  198 us
    ppermute x48, waiting for transfers between devices, from_batch(): return lax.ppermute(x, 'batch', [(i, i ^ k) for i in range(nb)])  108 us
    ppermute x48, starting transfers between devices, from_batch(): return lax.ppermute(x, 'batch', [(i, i ^ k) for i in range(nb)])  55.1 us
    ppermute x6, waiting for transfers between devices, carry(): lax.ppermute((decay * incoming + local).astype(LOW), 'seq', pairs)  54.9 us
    dot_general x5, matrix products, dot(): return jnp.dot(left, right, preferred_element_type=F32)  29.9 us
    dot_general x4, matrix products, dot_nt(): lax.dot_general(left, right, (((1,), (1,)), ((), ())), preferred_element_...  28 us
    dot_general x4, matrix products, dot_tn(): lax.dot_general(left, right, (((0,), (0,)), ((), ())), preferred_element_...  18.9 us
    ppermute x27, starting transfers between devices, turn(): return lax.ppermute(x, 'seq', [(i, (i + 1) % ns) for i in range(ns)])  18.3 us
  transfers between devices with their start and end apart: 103, of which 46 were waited for; matrix products, arithmetic and copies ran while one was open for 34% of the time, Pallas kernels for 0%

profile of v1, /device:TPU:2, one launch (start us, length us, event | category | flops | bytes accessed | tf_op | source)
XLA Modules:
  0.0 794.2 jit_solution(338791755327913402)
XLA Ops:
  55.3 5.8 collective-permute-done.10
  84.9 10.6 %collective-permute-done.22 = bf16[4,2,64,256]{3,2,1,0:T(8,128)(2,1)S(1)} collective-permute-done((bf16[4,2,64,256]{3,2,1,0:T(8,128)(2,1)S(1)}, bf16[4,2,64,256]{3,2,1,0:T(8,128)(2,1)S(1)}, u32[]{:S(2)}, u32[]{:S(2)}) %collective-permute-start.22) | collective-permute-done | bytes 262176 | tf_op jit(solution)/shard_map/ppermute | solution.py:60
  99.7 11.6 %collective-permute-done.1 = bf16[128,2048]{1,0:T(8,128)(2,1)S(1)} collective-permute-done((bf16[128,2048]{1,0:T(8,128)(2,1)S(1)}, bf16[128,2048]{1,0:T(8,128)(2,1)S(1)}, u32[]{:S(2)}, u32[]{:S(2)}) %collective-permute-start.1) | collective-permute-done | bytes 524320 | tf_op jit(solution)/shard_map/ppermute | solution.py:54
  126.6 5.8 collective-permute-done.43
  135.0 9.7 %collective-permute-done.23 = bf16[4,2,64,256]{3,2,1,0:T(8,128)(2,1)S(1)} collective-permute-done((bf16[4,2,64,256]{3,2,1,0:T(8,128)(2,1)S(1)}, bf16[4,2,64,256]{3,2,1,0:T(8,128)(2,1)S(1)}, u32[]{:S(2)}, u32[]{:S(2)}) %collective-permute-start.23) | collective-permute-done | bytes 262176 | tf_op jit(solution)/shard_map/ppermute | solution.py:60
  147.0 5.8 collective-permute-done.24
  161.9 14.9 %collective-permute-done.44 = bf16[176,2048]{1,0:T(8,128)(2,1)S(1)} collective-permute-done((bf16[176,2048]{1,0:T(8,128)(2,1)}, bf16[176,2048]{1,0:T(8,128)(2,1)S(1)}, u32[]{:S(2)}, u32[]{:S(2)}) %collective-permute-start.44) | collective-permute-done | bytes 720928 | tf_op jit(solution)/shard_map/ppermute | solution.py:60
  176.8 11.2 %collective-permute-done.16 = bf16[4,2,64,512]{3,2,1,0:T(8,128)(2,1)S(1)} collective-permute-done((bf16[4,2,64,512]{3,2,1,0:T(8,128)(2,1)}, bf16[4,2,64,512]{3,2,1,0:T(8,128)(2,1)S(1)}, u32[]{:S(2)}, u32[]{:S(2)}) %collective-permute-start.16) | collective-permute-done | bytes 524320 | tf_op jit(solution)/shard_map/ppermute | solution.py:60
  189.8 55.4 %collective-permute-done.17 = bf16[4,2,64,512]{3,2,1,0:T(8,128)(2,1)S(1)} collective-permute-done((bf16[4,2,64,512]{3,2,1,0:T(8,128)(2,1)S(1)}, bf16[4,2,64,512]{3,2,1,0:T(8,128)(2,1)S(1)}, u32[]{:S(2)}, u32[]{:S(2)}) %collective-permute-start.17) | collective-permute-done | bytes 524320 | tf_op jit(solution)/shard_map/ppermute | solution.py:60
  318.7 6.2 fusion.1
  338.9 7.9 collective-permute-done.33
  348.1 11.1 %collective-permute-done.34 = bf16[128,2048]{1,0:T(8,128)(2,1)S(1)} collective-permute-done((bf16[128,2048]{1,0:T(8,128)(2,1)S(1)}, bf16[128,2048]{1,0:T(8,128)(2,1)S(1)}, u32[]{:S(2)}, u32[]{:S(2)}) %collective-permute-start.34) | collective-permute-done | bytes 524320 | tf_op jit(solution)/shard_map/ppermute | solution.py:54
  366.5 6.4 copy.300
  391.2 6.4 copy.267
  397.6 10.6 %fusion.168 = f32[1024,1408]{1,0:T(8,128)S(1)} fusion(bf16[1024,2048]{1,0:T(8,128)(2,1)} %bitcast.795, bf16[2048,1408]{1,0:T(8,128)(2,1)} %bitcast.798), kind=kOutput, calls=%fused_computation.694 | convolution fusion | flops 5905580032 | bytes 15728640 | tf_op jit(solution)/shard_map/dot_general | solution.py:16
  408.2 7.9 multiply_convert_fusion.2
  427.9 9.8 %fusion.15 = f32[4,2,128,2048]{3,2,0,1:T(8,128)S(1)} fusion(bf16[2048,1408,1,1]{1,0,2,3:T(8,128)(2,1)} %bitcast.799, bf16[4,2,128,1408]{3,2,1,0:T(8,128)(2,1)S(1)} %bitcast.812), kind=kOutput, calls=%fused_computation.36 | convolution fusion | flops 5905580032 | bytes 17039360 | tf_op jit(solution)/shard_map/dot_general | solution.py:24
  449.2 8.6 %fusion.10 = f32[4,4,128,1408]{3,2,1,0:T(8,128)S(1)} fusion(bf16[4,4,128,1024]{3,2,1,0:T(8,128)(2,1)S(1)} %bitcast.808, bf16[1024,1408]{1,0:T(8,128)(2,1)} %copy-done.30), kind=kOutput, calls=%fused_computation.28 | convolution fusion | flops 5905580032 | bytes 18612224 | tf_op jit(solution)/shard_map/dot_general | solution.py:20
  461.2 7.8 collective-permute-done.100
  483.8 15.8 %collective-permute-done.92 = bf16[4,128,1408]{2,1,0:T(8,128)(2,1)} collective-permute-done((bf16[4,128,1408]{2,1,0:T(8,128)(2,1)}, bf16[4,128,1408]{2,1,0:T(8,128)(2,1)}, u32[]{:S(2)}, u32[]{:S(2)}) %collective-permute-start.92) | collective-permute-done | bytes 1441824 | tf_op jit(solution)/shard_map/ppermute | solution.py:60
  505.7 6.9 collective-permute-done.47
  512.6 10.3 %collective-permute-done.49 = bf16[128,2048]{1,0:T(8,128)(2,1)S(1)} collective-permute-done((bf16[128,2048]{1,0:T(8,128)(2,1)S(1)}, bf16[128,2048]{1,0:T(8,128)(2,1)S(1)}, u32[]{:S(2)}, u32[]{:S(2)}) %collective-permute-start.49) | collective-permute-done | bytes 524320 | tf_op jit(solution)/shard_map/ppermute | solution.py:54
  541.7 12.9 %collective-permute-done.93 = bf16[4,128,1408]{2,1,0:T(8,128)(2,1)} collective-permute-done((bf16[4,128,1408]{2,1,0:T(8,128)(2,1)}, bf16[4,128,1408]{2,1,0:T(8,128)(2,1)}, u32[]{:S(2)}, u32[]{:S(2)}) %collective-permute-start.93) | collective-permute-done | bytes 1441824 | tf_op jit(solution)/shard_map/ppermute | solution.py:60
  559.8 7.3 collective-permute-done.59
  581.9 30.2 %collective-permute-done.62 = bf16[4,2,128,128]{3,2,1,0:T(8,128)(2,1)S(1)} collective-permute-done((bf16[4,2,128,128]{3,2,1,0:T(8,128)(2,1)S(1)}, bf16[4,2,128,128]{3,2,1,0:T(8,128)(2,1)S(1)}, u32[]{:S(2)}, u32[]{:S(2)}) %collective-permute-start.62) | collective-permute-done | bytes 262176 | tf_op jit(solution)/shard_map/ppermute | solution.py:190
  614.1 8.3 %collective-permute-done.63 = bf16[4,2,128,128]{3,2,1,0:T(8,128)(2,1)S(1)} collective-permute-done((bf16[4,2,128,128]{3,2,1,0:T(8,128)(2,1)S(1)}, bf16[4,2,128,128]{3,2,1,0:T(8,128)(2,1)S(1)}, u32[]{:S(2)}, u32[]{:S(2)}) %collective-permute-start.63) | collective-permute-done | bytes 262176 | tf_op jit(solution)/shard_map/ppermute | solution.py:190
  647.3 6.3 fusion.5
  663.8 10.9 %collective-permute-done.69 = bf16[4,128,768]{2,1,0:T(8,128)(2,1)S(1)} collective-permute-done((bf16[4,128,768]{2,1,0:T(8,128)(2,1)S(1)}, bf16[4,128,768]{2,1,0:T(8,128)(2,1)S(1)}, u32[]{:S(2)}, u32[]{:S(2)}) %collective-permute-start.69) | collective-permute-done | bytes 786464 | tf_op jit(solution)/shard_map/ppermute | solution.py:60
  686.2 10.7 %collective-permute-done.70 = bf16[4,128,768]{2,1,0:T(8,128)(2,1)S(1)} collective-permute-done((bf16[4,128,768]{2,1,0:T(8,128)(2,1)S(1)}, bf16[4,128,768]{2,1,0:T(8,128)(2,1)S(1)}, u32[]{:S(2)}, u32[]{:S(2)}) %collective-permute-start.70) | collective-permute-done | bytes 786464 | tf_op jit(solution)/shard_map/ppermute | solution.py:60
  730.6 6.0 collective-permute-done.85
  749.1 23.3 %collective-permute-done.73 = bf16[2,64,768]{2,1,0:T(8,128)(2,1)S(1)} collective-permute-done((bf16[2,64,768]{2,1,0:T(8,128)(2,1)S(1)}, bf16[2,64,768]{2,1,0:T(8,128)(2,1)S(1)}, u32[]{:S(2)}, u32[]{:S(2)}) %collective-permute-start.73) | collective-permute-done | bytes 196640 | tf_op jit(solution)/shard_map/ppermute | solution.py:54
  775.3 5.7 collective-permute-done.87
  (679 shorter events, 409.2 us)
Async XLA Ops:
  7.2 320.3 %all-gather.2.cloned.1.call-start = ((), (), s32[]{:S(2)}) async-start(), calls=%async_computation | async-start | bytes 8650752 | tf_op jit(solution)/shard_map/all_gather | solution.py:142
  9.3 29.9 %collective-permute-start.6 = (f32[1,384]{1,0:T(1,128)}, f32[1,384]{1,0:T(1,128)S(1)}, u32[]{:S(2)}, u32[]{:S(2)}) collective-permute-start(f32[1,384]{1,0:T(1,128)} %reshape.1234), channel_id=1, source_target_pairs={{0,24},{8,16},{16,8},{24,0},{1,25},{9,17},{17,9},{25,1},{2,26},{10... | collective-permute-start | bytes 4616 | tf_op jit(solution)/shard_map/ppermute | solution.py:54
  12.7 82.8 %collective-permute-start = (bf16[128,2048]{1,0:T(8,128)(2,1)}, bf16[128,2048]{1,0:T(8,128)(2,1)}, u32[]{:S(2)}, u32[]{:S(2)}) collective-permute-start(bf16[128,2048]{1,0:T(8,128)(2,1)} %param.14), channel_id=1, source_target_pairs={{0,8},{8,0},{16,24},{24,16},{1,9},{9,1},{17,25},{25,17},{2,10},{10... | collective-permute-start | bytes 1572872 | tf_op jit(solution)/shard_map/ppermute | solution.py:54
  12.8 86.2 %collective-permute-start.2 = (bf16[128,2048]{1,0:T(8,128)(2,1)}, bf16[128,2048]{1,0:T(8,128)(2,1)}, u32[]{:S(2)}, u32[]{:S(2)}) collective-permute-start(bf16[128,2048]{1,0:T(8,128)(2,1)} %param.14), channel_id=1, source_target_pairs={{0,24},{8,16},{16,8},{24,0},{1,25},{9,17},{17,9},{25,1},{2,26},{10... | collective-permute-start | bytes 1572872 | tf_op jit(solution)/shard_map/ppermute | solution.py:54
  80.0 31.3 %collective-permute-start.1 = (bf16[128,2048]{1,0:T(8,128)(2,1)S(1)}, bf16[128,2048]{1,0:T(8,128)(2,1)S(1)}, u32[]{:S(2)}, u32[]{:S(2)}) collective-permute-start(bf16[128,2048]{1,0:T(8,128)(2,1)S(1)} %copy-done.6), channel_id=1, source_target_pairs={{0,16},{8,24},{16,0},{24,8},{1,17},{9,25},{17,1},{25,9},{2,18},{10... | collective-permute-start | bytes 1572872 | tf_op jit(solution)/shard_map/ppermute | solution.py:54
  82.2 33.3 %collective-permute-start.50 = (bf16[128,2048]{1,0:T(8,128)(2,1)S(1)}, bf16[128,2048]{1,0:T(8,128)(2,1)S(1)}, u32[]{:S(2)}, u32[]{:S(2)}) collective-permute-start(bf16[128,2048]{1,0:T(8,128)(2,1)S(1)} %copy-done.35), channel_id=1, source_target_pairs={{0,8},{8,0},{16,24},{24,16},{1,9},{9,1},{17,25},{25,17},{2,10},{10... | collective-permute-start | bytes 1572872 | tf_op jit(solution)/shard_map/ppermute | solution.py:54
  115.5 29.9 %collective-permute-start.15 = (bf16[4,2,64,512]{3,2,1,0:T(8,128)(2,1)S(1)}, bf16[4,2,64,512]{3,2,1,0:T(8,128)(2,1)S(1)}, u32[]{:S(2)}, u32[]{:S(2)}) collective-permute-start(bf16[4,2,64,512]{3,2,1,0:T(8,128)(2,1)S(1)} %pad_maximum_fusion.11), channel_id=1, source_target_pairs={{0,2},{2,4},{4,6},{6,0},{1,3},{3,5},{5,7},{7,1},{8,10},{10,12},{12... | collective-permute-start | bytes 1572872 | tf_op jit(solution)/shard_map/ppermute | solution.py:60
  121.7 125.6 %collective-permute-start.3 = (bf16[4,128,2048]{2,1,0:T(8,128)(2,1)}, bf16[4,128,2048]{2,1,0:T(8,128)(2,1)}, u32[]{:S(2)}, u32[]{:S(2)}) collective-permute-start(bf16[4,128,2048]{2,1,0:T(8,128)(2,1)} %get-tuple-element.154), channel_id=1, source_target_pairs={{0,1},{1,0},{2,3},{3,2},{4,5},{5,4},{6,7},{7,6},{8,9},{9,8},{10,11... | collective-permute-start | bytes 6291464 | tf_op jit(solution)/shard_map/ppermute | solution.py:57
  124.8 31.0 %collective-permute-start.37 = (bf16[2,64,1408]{2,1,0:T(8,128)(2,1)}, bf16[2,64,1408]{2,1,0:T(8,128)(2,1)}, u32[]{:S(2)}, u32[]{:S(2)}) collective-permute-start(bf16[2,64,1408]{2,1,0:T(8,128)(2,1)} %pad_maximum_fusion.13), channel_id=1, source_target_pairs={{0,24},{8,16},{16,8},{24,0},{1,25},{9,17},{17,9},{25,1},{2,26},{10... | collective-permute-start | bytes 1081352 | tf_op jit(solution)/shard_map/ppermute | solution.py:54
  152.9 209.4 %collective-permute-start.53 = (bf16[4,128,2048]{2,1,0:T(8,128)(2,1)}, bf16[4,128,2048]{2,1,0:T(8,128)(2,1)}, u32[]{:S(2)}, u32[]{:S(2)}) collective-permute-start(bf16[4,128,2048]{2,1,0:T(8,128)(2,1)} %get-tuple-element.147), channel_id=1, source_target_pairs={{0,1},{1,0},{2,3},{3,2},{4,5},{5,4},{6,7},{7,6},{8,9},{9,8},{10,11... | collective-permute-start | bytes 6291464 | tf_op jit(solution)/shard_map/ppermute | solution.py:57
  155.9 32.2 %collective-permute-start.16 = (bf16[4,2,64,512]{3,2,1,0:T(8,128)(2,1)}, bf16[4,2,64,512]{3,2,1,0:T(8,128)(2,1)S(1)}, u32[]{:S(2)}, u32[]{:S(2)}) collective-permute-start(bf16[4,2,64,512]{3,2,1,0:T(8,128)(2,1)} %copy-done.54), channel_id=1, source_target_pairs={{0,2},{2,4},{4,6},{6,0},{1,3},{3,5},{5,7},{7,1},{8,10},{10,12},{12... | collective-permute-start | bytes 1572872 | tf_op jit(solution)/shard_map/ppermute | solution.py:60
  159.6 87.4 %collective-permute-start.40 = (bf16[4,2,64,1408]{3,2,1,0:T(8,128)(2,1)S(1)}, bf16[4,2,64,1408]{3,2,1,0:T(8,128)(2,1)}, u32[]{:S(2)}, u32[]{:S(2)}) collective-permute-start(bf16[4,2,64,1408]{3,2,1,0:T(8,128)(2,1)S(1)} %pad_maximum_fusion.8), channel_id=1, source_target_pairs={{0,2},{2,4},{4,6},{6,0},{1,3},{3,5},{5,7},{7,1},{8,10},{10,12},{12... | collective-permute-start | bytes 4325384 | tf_op jit(solution)/shard_map/ppermute | solution.py:60
  176.8 69.3 %collective-permute-start.45 = (bf16[176,2048]{1,0:T(8,128)(2,1)S(1)}, bf16[176,2048]{1,0:T(8,128)(2,1)S(1)}, u32[]{:S(2)}, u32[]{:S(2)}) collective-permute-start(bf16[176,2048]{1,0:T(8,128)(2,1)S(1)} %collective-permute-done.44), channel_id=1, source_target_pairs={{0,2},{2,4},{4,6},{6,0},{1,3},{3,5},{5,7},{7,1},{8,10},{10,12},{12... | collective-permute-start | bytes 2162696 | tf_op jit(solution)/shard_map/ppermute | solution.py:60
  188.0 57.2 %collective-permute-start.17 = (bf16[4,2,64,512]{3,2,1,0:T(8,128)(2,1)S(1)}, bf16[4,2,64,512]{3,2,1,0:T(8,128)(2,1)S(1)}, u32[]{:S(2)}, u32[]{:S(2)}) collective-permute-start(bf16[4,2,64,512]{3,2,1,0:T(8,128)(2,1)S(1)} %collective-permute-done.16), channel_id=1, source_target_pairs={{0,2},{2,4},{4,6},{6,0},{1,3},{3,5},{5,7},{7,1},{8,10},{10,12},{12... | collective-permute-start | bytes 1572872 | tf_op jit(solution)/shard_map/ppermute | solution.py:60
  247.0 89.0 %collective-permute-start.41 = (bf16[4,2,64,1408]{3,2,1,0:T(8,128)(2,1)}, bf16[4,2,64,1408]{3,2,1,0:T(8,128)(2,1)}, u32[]{:S(2)}, u32[]{:S(2)}) collective-permute-start(bf16[4,2,64,1408]{3,2,1,0:T(8,128)(2,1)} %collective-permute-done.40), channel_id=1, source_target_pairs={{0,2},{2,4},{4,6},{6,0},{1,3},{3,5},{5,7},{7,1},{8,10},{10,12},{12... | collective-permute-start | bytes 4325384 | tf_op jit(solution)/shard_map/ppermute | solution.py:60
  336.1 48.1 %collective-permute-start.42 = (bf16[4,2,64,1408]{3,2,1,0:T(8,128)(2,1)}, bf16[4,2,64,1408]{3,2,1,0:T(8,128)(2,1)}, u32[]{:S(2)}, u32[]{:S(2)}) collective-permute-start(bf16[4,2,64,1408]{3,2,1,0:T(8,128)(2,1)} %collective-permute-done.41), channel_id=1, source_target_pairs={{0,2},{2,4},{4,6},{6,0},{1,3},{3,5},{5,7},{7,1},{8,10},{10,12},{12... | collective-permute-start | bytes 4325384 | tf_op jit(solution)/shard_map/ppermute | solution.py:60
  438.0 33.3 %collective-permute-start.54 = (bf16[4,128,2048]{2,1,0:T(8,128)(2,1)S(1)}, bf16[4,128,2048]{2,1,0:T(8,128)(2,1)}, u32[]{:S(2)}, u32[]{:S(2)}) collective-permute-start(bf16[4,128,2048]{2,1,0:T(8,128)(2,1)S(1)} %fusion.18), channel_id=1, source_target_pairs={{0,1},{1,0},{2,3},{3,2},{4,5},{5,4},{6,7},{7,6},{8,9},{9,8},{10,11... | collective-permute-start | bytes 6291464 | tf_op jit(solution)/shard_map/ppermute | solution.py:57
  447.9 30.8 %collective-permute-start.46 = (bf16[4,128,2048]{2,1,0:T(8,128)(2,1)}, bf16[4,128,2048]{2,1,0:T(8,128)(2,1)}, u32[]{:S(2)}, u32[]{:S(2)}) collective-permute-start(bf16[4,128,2048]{2,1,0:T(8,128)(2,1)} %fusion.17), channel_id=1, source_target_pairs={{0,1},{1,0},{2,3},{3,2},{4,5},{5,4},{6,7},{7,6},{8,9},{9,8},{10,11... | collective-permute-start | bytes 6291464 | tf_op jit(solution)/shard_map/ppermute | solution.py:57
  459.2 40.3 %collective-permute-start.92 = (bf16[4,128,1408]{2,1,0:T(8,128)(2,1)}, bf16[4,128,1408]{2,1,0:T(8,128)(2,1)}, u32[]{:S(2)}, u32[]{:S(2)}) collective-permute-start(bf16[4,128,1408]{2,1,0:T(8,128)(2,1)} %fusion.27), channel_id=1, source_target_pairs={{0,2},{2,4},{4,6},{6,0},{1,3},{3,5},{5,7},{7,1},{8,10},{10,12},{12... | collective-permute-start | bytes 4325384 | tf_op jit(solution)/shard_map/ppermute | solution.py:60
  504.4 50.2 %collective-permute-start.93 = (bf16[4,128,1408]{2,1,0:T(8,128)(2,1)}, bf16[4,128,1408]{2,1,0:T(8,128)(2,1)}, u32[]{:S(2)}, u32[]{:S(2)}) collective-permute-start(bf16[4,128,1408]{2,1,0:T(8,128)(2,1)} %fusion.14), channel_id=1, source_target_pairs={{0,2},{2,4},{4,6},{6,0},{1,3},{3,5},{5,7},{7,1},{8,10},{10,12},{12... | collective-permute-start | bytes 4325384 | tf_op jit(solution)/shard_map/ppermute | solution.py:60
  535.4 88.7 %collective-permute-start.82 = (bf16[128,2048]{1,0:T(8,128)(2,1)}, bf16[128,2048]{1,0:T(8,128)(2,1)}, u32[]{:S(2)}, u32[]{:S(2)}) collective-permute-start(bf16[128,2048]{1,0:T(8,128)(2,1)} %get-tuple-element.73), channel_id=1, source_target_pairs={{0,24},{8,16},{16,8},{24,0},{1,25},{9,17},{17,9},{25,1},{2,26},{10... | collective-permute-start | bytes 1572872 | tf_op jit(solution)/shard_map/ppermute | solution.py:54
  537.3 86.8 %collective-permute-start.81 = (bf16[128,2048]{1,0:T(8,128)(2,1)}, bf16[128,2048]{1,0:T(8,128)(2,1)}, u32[]{:S(2)}, u32[]{:S(2)}) collective-permute-start(bf16[128,2048]{1,0:T(8,128)(2,1)} %get-tuple-element.73), channel_id=1, source_target_pairs={{0,16},{8,24},{16,0},{24,8},{1,17},{9,25},{17,1},{25,9},{2,18},{10... | collective-permute-start | bytes 1572872 | tf_op jit(solution)/shard_map/ppermute | solution.py:54
  538.5 85.6 %collective-permute-start.80 = (bf16[128,2048]{1,0:T(8,128)(2,1)}, bf16[128,2048]{1,0:T(8,128)(2,1)}, u32[]{:S(2)}, u32[]{:S(2)}) collective-permute-start(bf16[128,2048]{1,0:T(8,128)(2,1)} %get-tuple-element.73), channel_id=1, source_target_pairs={{0,8},{8,0},{16,24},{24,16},{1,9},{9,1},{17,25},{25,17},{2,10},{10... | collective-permute-start | bytes 1572872 | tf_op jit(solution)/shard_map/ppermute | solution.py:54
  539.0 33.9 %collective-permute-start.61 = (bf16[2,128,256]{2,1,0:T(8,128)(2,1)S(1)}, bf16[2,128,256]{2,1,0:T(8,128)(2,1)S(1)}, u32[]{:S(2)}, u32[]{:S(2)}) collective-permute-start(bf16[2,128,256]{2,1,0:T(8,128)(2,1)S(1)} %get-tuple-element.202), channel_id=1, source_target_pairs={{0,24},{8,16},{16,8},{24,0},{1,25},{9,17},{17,9},{25,1},{2,26},{10... | collective-permute-start | bytes 393224 | tf_op jit(solution)/shard_map/ppermute | solution.py:54
  572.2 84.8 %collective-permute-start.94 = (bf16[4,128,1408]{2,1,0:T(8,128)(2,1)}, bf16[4,128,1408]{2,1,0:T(8,128)(2,1)}, u32[]{:S(2)}, u32[]{:S(2)}) collective-permute-start(bf16[4,128,1408]{2,1,0:T(8,128)(2,1)} %fusion.13), channel_id=1, source_target_pairs={{0,2},{2,4},{4,6},{6,0},{1,3},{3,5},{5,7},{7,1},{8,10},{10,12},{12... | collective-permute-start | bytes 4325384 | tf_op jit(solution)/shard_map/ppermute | solution.py:60
  577.0 35.1 %collective-permute-start.62 = (bf16[4,2,128,128]{3,2,1,0:T(8,128)(2,1)S(1)}, bf16[4,2,128,128]{3,2,1,0:T(8,128)(2,1)S(1)}, u32[]{:S(2)}, u32[]{:S(2)}) collective-permute-start(bf16[4,2,128,128]{3,2,1,0:T(8,128)(2,1)S(1)} %get-tuple-element.314), channel_id=1, source_target_pairs={{2,0},{4,2},{6,4},{3,1},{5,3},{7,5},{10,8},{12,10},{14,12},{11,9},... | collective-permute-start | bytes 786440 | tf_op jit(solution)/shard_map/ppermute | solution.py:190
  627.4 52.1 %collective-permute-start.83 = (bf16[4,128,2048]{2,1,0:T(8,128)(2,1)}, bf16[4,128,2048]{2,1,0:T(8,128)(2,1)}, u32[]{:S(2)}, u32[]{:S(2)}) collective-permute-start(bf16[4,128,2048]{2,1,0:T(8,128)(2,1)} %get-tuple-element.139), channel_id=1, source_target_pairs={{0,1},{1,0},{2,3},{3,2},{4,5},{5,4},{6,7},{7,6},{8,9},{9,8},{10,11... | collective-permute-start | bytes 6291464 | tf_op jit(solution)/shard_map/ppermute | solution.py:57
  674.6 52.2 %collective-permute-start.65 = (bf16[4,128,2048]{2,1,0:T(8,128)(2,1)}, bf16[4,128,2048]{2,1,0:T(8,128)(2,1)}, u32[]{:S(2)}, u32[]{:S(2)}) collective-permute-start(bf16[4,128,2048]{2,1,0:T(8,128)(2,1)} %fusion.19), channel_id=1, source_target_pairs={{0,1},{1,0},{2,3},{3,2},{4,5},{5,4},{6,7},{7,6},{8,9},{9,8},{10,11... | collective-permute-start | bytes 6291464 | tf_op jit(solution)/shard_map/ppermute | solution.py:57
  684.7 40.8 %collective-permute-start.84 = (bf16[2,64,2048]{2,1,0:T(8,128)(2,1)}, bf16[2,64,2048]{2,1,0:T(8,128)(2,1)}, u32[]{:S(2)}, u32[]{:S(2)}) collective-permute-start(bf16[2,64,2048]{2,1,0:T(8,128)(2,1)} %fusion.85), channel_id=1, source_target_pairs={{0,1},{1,0},{2,3},{3,2},{4,5},{5,4},{6,7},{7,6},{8,9},{9,8},{10,11... | collective-permute-start | bytes 1572872 | tf_op jit(solution)/shard_map/ppermute | solution.py:57
  697.9 38.8 %collective-permute-start.71 = (bf16[4,128,768]{2,1,0:T(8,128)(2,1)}, bf16[4,128,768]{2,1,0:T(8,128)(2,1)}, u32[]{:S(2)}, u32[]{:S(2)}) collective-permute-start(bf16[4,128,768]{2,1,0:T(8,128)(2,1)} %fusion.23), channel_id=1, source_target_pairs={{0,2},{2,4},{4,6},{6,0},{1,3},{3,5},{5,7},{7,1},{8,10},{10,12},{12... | collective-permute-start | bytes 2359304 | tf_op jit(solution)/shard_map/ppermute | solution.py:60
  741.1 31.6 %collective-permute-start.66 = (bf16[128,2048]{1,0:T(8,128)(2,1)S(1)}, bf16[128,2048]{1,0:T(8,128)(2,1)S(1)}, u32[]{:S(2)}, u32[]{:S(2)}) collective-permute-start(bf16[128,2048]{1,0:T(8,128)(2,1)S(1)} %get-tuple-element.140), channel_id=1, source_target_pairs={{0,8},{8,0},{16,24},{24,16},{1,9},{9,1},{17,25},{25,17},{2,10},{10... | collective-permute-start | bytes 1572872 | tf_op jit(solution)/shard_map/ppermute | solution.py:54
  741.6 31.2 %collective-permute-start.68 = (bf16[128,2048]{1,0:T(8,128)(2,1)S(1)}, bf16[128,2048]{1,0:T(8,128)(2,1)S(1)}, u32[]{:S(2)}, u32[]{:S(2)}) collective-permute-start(bf16[128,2048]{1,0:T(8,128)(2,1)S(1)} %get-tuple-element.141), channel_id=1, source_target_pairs={{0,24},{8,16},{16,8},{24,0},{1,25},{9,17},{17,9},{25,1},{2,26},{10... | collective-permute-start | bytes 1572872 | tf_op jit(solution)/shard_map/ppermute | solution.py:54
  (166 other events, 2255.0 us)
Sparse Core Ops, SparseCore 0:
  15.9 131.7 all-gather.1

commit v2 on v1

v2 whole, which is shorter than its diff:
```python
import math
from functools import partial

import jax
import jax.numpy as jnp
from jax import lax
from jax.experimental import pallas as pl
from jax.experimental.pallas import tpu as pltpu
from jax.sharding import PartitionSpec as P

HDIM = 128
EPSILON = 1e-06
RESET_LOG = -30.0
F32 = jnp.float32
LOW = jnp.bfloat16
AXES = ("y", "x", "h", "l", "chip")
LIMIT = 56 * 2**20
VMEM = pl.BlockSpec(memory_space=pltpu.VMEM)
SMEM = pl.BlockSpec(memory_space=pltpu.SMEM)
ANY = pl.BlockSpec(memory_space=pl.ANY)


def dot(left, right):
    return jnp.dot(left, right, preferred_element_type=F32)


def dot_tn(left, right):
    return lax.dot_general(left, right, (((0,), (0,)), ((), ())), preferred_element_type=F32)


def dot_nt(left, right):
    return lax.dot_general(left, right, (((1,), (1,)), ((), ())), preferred_element_type=F32)


def inverse_rms(values):
    return lax.rsqrt(jnp.mean(values * values, axis=-1, keepdims=True) + EPSILON)


def norm_back(values, rms, scaled):
    inner = jnp.mean(scaled * values, axis=-1, keepdims=True)
    return rms * scaled - values * (rms * rms * rms * inner)


def sigmoid(a):
    return 1.0 / (1.0 + jnp.exp(-a))


def pick(flag, first, second):
    return jnp.where(flag, first, second)


def after(x, *deps):
    return lax.optimization_barrier((x, deps))[0]


def shape(dims, dtype=F32):
    return jax.ShapeDtypeStruct(tuple(dims), dtype)


def call(kernel, outs, *args, specs=None, out_specs=None, grid=(), scratch=(), flops=0):
    outs = tuple(outs)
    specs = [VMEM] * len(args) if specs is None else specs
    out_specs = tuple([VMEM] * len(outs)) if out_specs is None else tuple(out_specs)
    moved = sum(math.prod(a.shape) * a.dtype.itemsize for a in (*args, *outs))
    return pl.pallas_call(
        kernel,
        out_shape=outs,
        grid=grid,
        in_specs=specs,
        out_specs=out_specs,
        scratch_shapes=list(scratch),
        compiler_params=pltpu.CompilerParams(vmem_limit_bytes=LIMIT),
        cost_estimate=pl.CostEstimate(flops=int(flops), bytes_accessed=int(moved), transcendentals=0),
    )(*args)


class Plan:
    def __init__(self, sizes):
        self.ny, self.nx, self.nh, self.nl, self.nc = sizes
        self.plane = self.nx * self.nl
        self.copies = self.ny * self.nh
        self.devices = self.copies * self.plane * self.nc

    def owner(self, y, p, h, c):
        return (((y * self.nx + p // self.nl) * self.nh + h) * self.nl + p % self.nl) * self.nc + c


def fetch(plan, where, blocks, target, sems, start=True):
    y, h, here = (where[i] for i in range(3))
    moves = []
    for t, (source, i, j, k, e) in enumerate(blocks):
        yy = lax.rem(y + (plan.ny - j), plan.ny)
        hh = lax.rem(h + (plan.nh - i), plan.nh)
        place = plan.owner(yy, here ^ k, hh, e)
        move = pltpu.make_async_copy(source, target.at[place], sems.at[t])
        if start:
            move.start()
        moves.append(move)
    return moves


def pack_kernel(plan, ffr, gate, up, out):
    units = plan.copies * ffr
    for e in range(plan.nc):
        for p in range(plan.plane):
            for w, base in ((gate, 0), (up, units)):
                for m in range(plan.copies):
                    at = plan.owner(m // plan.nh, p, m % plan.nh, e) * ffr
                    to = base + m * ffr
                    out[e, p, :, to : to + ffr] = w[:, at : at + ffr]


def unpack_kernel(plan, ffr, where, blocks, gate, up, grad_gate, grad_up, along, ordered):
    here = where[2]
    units = plan.copies * ffr
    for k in range(plan.plane):
        for e in range(plan.nc):
            ordered[e, here ^ k] = blocks[e, k]
    for e in range(plan.nc):
        for p in range(plan.plane):
            block = ordered[e, p].astype(F32)
            for g, base in ((grad_gate, 0), (grad_up, units)):
                for m in range(plan.copies):
                    at = plan.owner(m // plan.nh, p, m % plan.nh, e) * ffr
                    to = base + m * ffr
                    g[:, at : at + ffr] = block[:, to : to + ffr]
    total = jnp.sum(gate[...].astype(F32) * grad_gate[...], axis=1, keepdims=True)
    total = total + jnp.sum(up[...].astype(F32) * grad_up[...], axis=1, keepdims=True)
    along[...] = jnp.broadcast_to(total, along.shape)


def unpack_part_kernel(plan, part, where, blocks, w0, w1, w2, g0, g1, g2, along):
    here = where[2]
    for k in range(plan.plane):
        for e in range(plan.nc):
            at = pl.multiple_of(((here ^ k) * plan.nc + e) * part, part)
            for i, g in enumerate((g0, g1, g2)):
                g[:, pl.ds(at, part)] = blocks[e, k, :, i * part : (i + 1) * part].astype(F32)
    total = 0.0
    for w, g in ((w0, g0), (w1, g1), (w2, g2)):
        total = total + jnp.sum(w[...].astype(F32) * g[...], axis=1, keepdims=True)
    along[...] = jnp.broadcast_to(total, along.shape)


def normalize(x, gain, out, step):
    @pl.loop(0, x.shape[0] // step)
    def _(t):
        at = pl.ds(pl.multiple_of(t * step, step), step)
        values = x[at, :].astype(F32)
        out[at, :] = (values * inverse_rms(values) * gain[...]).astype(LOW)


def project_kernel(plan, names, where, x, gain, *rest):
    blocks, (normed, pre, weight, sems) = rest[: len(names)], rest[len(names) :]
    moves = fetch(
        plan, where,
        [(ref.at[k * plan.nc + e], i, j, k, e) for ref, (i, j) in zip(blocks, names)
         for k in range(plan.plane) for e in range(plan.nc)],
        weight, sems,
    )
    normalize(x, gain, normed, 64)
    for move in moves:
        move.wait()
    pre[...] = dot(normed[...], weight[...].reshape(-1, weight.shape[-1]))


def ffn_kernel(plan, names, where, normed, cotangent, down, *rest):
    blocks, (hidden, grad_gu, part_out, part_grad, weight, sems) = rest[: len(names)], rest[len(names) :]
    first = pl.program_id(0) == 0

    def moves(start):
        return fetch(
            plan, where,
            [(ref.at[i, k * plan.nc + e], i, j, base + k, e) for ref, (j, base) in zip(blocks, names)
             for i in range(plan.nh) for k in range(ref.shape[1] // plan.nc) for e in range(plan.nc)],
            weight, sems, start,
        )

    @pl.when(first)
    def _():
        moves(True)

    units = down.shape[0]
    upstream = dot_nt(cotangent[...], down[...])

    @pl.when(first)
    def _():
        for move in moves(False):
            move.wait()

    full = weight[...].reshape(-1, weight.shape[-1])
    both = dot(normed[...], full)
    gate, up = both[:, :units], both[:, units:]
    sig = sigmoid(gate)
    silu = gate * sig
    hid = (silu * up).astype(LOW)
    hidden[...] = hid
    grad_gu[:, :units] = (upstream * up * sig * (1.0 + gate * (1.0 - sig))).astype(LOW)
    grad_gu[:, units:] = (upstream * silu).astype(LOW)
    part_grad[...] = dot_nt(grad_gu[...], full).astype(part_grad.dtype)
    part_out[...] = dot(hid, down[...]).astype(part_out.dtype)


def columns_grad_kernel(plan, turn, sides, count, where, normed, *rest):
    grads, out = rest[:count], rest[count]
    y = lax.rem(where[0] + (plan.ny - turn), plan.ny)
    step = out.shape[0] * out.shape[2]
    for t, side in enumerate(sides):
        at = pl.multiple_of((y * plan.nx + (where[5] ^ side)) * step, step)
        base = 0
        for a in grads:
            n = a.shape[1]
            value = dot_tn(normed[:, pl.ds(at, step)], a[...])
            for i in range(plan.nh):
                out[i, t, :, base : base + n] = value[i * out.shape[2] : (i + 1) * out.shape[2]].astype(out.dtype)
            base += n


def rows_grad_kernel(left, right, out):
    n = 512
    for t in range(out.shape[1] // n):
        at = slice(t * n, (t + 1) * n)
        out[:, at] = dot_tn(left[...], right[:, at]).astype(out.dtype)


def interleaved(x):
    return jnp.concatenate([x[e, 0, i] for i in range(x.shape[2]) for e in range(x.shape[0])], axis=0)


def separated(x, out):
    nc, _, nl, rows, _ = out.shape
    for i in range(nl):
        for e in range(nc):
            at = (i * nc + e) * rows
            out[e, 0, i] = x[at : at + rows].astype(out.dtype)


def thirds(x):
    first = x.astype(LOW)
    rest = x - first.astype(F32)
    second = rest.astype(LOW)
    return first, second, (rest - second.astype(F32)).astype(LOW)


def causal_of(where, span, rows):
    flip = where[4] * rows
    t = lax.broadcasted_iota(jnp.int32, (span, span), 0) ^ flip
    s = lax.broadcasted_iota(jnp.int32, (span, span), 1) ^ flip
    return (t >= s).astype(F32)


def gate_terms(forget_pre, lower, is_start):
    sig = sigmoid(forget_pre)
    gate = lower + (1.0 - lower) * sig
    return sig, gate, 1.0 - gate, jnp.where(is_start, 0.0, jnp.log(gate))


def decay_terms(causal, starts, starts_row, cumulative, total):
    low = causal.astype(LOW)
    count = dot(low, starts)
    count_row = dot_nt(starts_row, low)[:1]
    ends = jnp.sum(starts.astype(F32), axis=0, keepdims=True)
    reach = jnp.exp(RESET_LOG * count)
    left = jnp.exp(RESET_LOG * (ends - count))
    between = causal * jnp.exp(RESET_LOG * jnp.maximum(count[:, :1] - count_row, 0.0))
    return reach, between, jnp.exp(cumulative), jnp.exp(-cumulative), jnp.exp(total - cumulative) * left, ends


def mix_kernel(
    where, f, v, q, lower, starts, starts_row,
    end_state, decay, local, query_reach, cumulative_out, scores_out,
):
    rows = f.shape[3]
    forget_pre, value, query_pre = interleaved(f), interleaved(v), interleaved(q)
    span = forget_pre.shape[0]
    is_start = starts[0].astype(F32) == 1.0
    _, _, key, log_decay = gate_terms(forget_pre, lower[0], is_start)
    causal = causal_of(where, span, rows)
    low = causal.astype(LOW)
    parts = thirds(log_decay)
    cumulative = dot(low, parts[0]) + dot(low, parts[1]) + dot(low, parts[2])
    total = jnp.sum(log_decay, axis=0, keepdims=True)
    reach, between, grow, shrink, suffix, ends = decay_terms(causal, starts[0], starts_row[0], cumulative, total)
    query = query_pre * sigmoid(query_pre) * grow
    value_low = value.astype(LOW)
    end_state[0, 0] = dot_tn((key * suffix).astype(LOW), value_low)
    ones = jnp.ones((span, HDIM), LOW)
    total_column = dot_tn(parts[0], ones) + dot_tn(parts[1], ones) + dot_tn(parts[2], ones)
    decay[0, 0] = jnp.exp(total_column + RESET_LOG * ends)
    scores = (dot_nt(query.astype(LOW), (key * shrink).astype(LOW)) * between).astype(LOW)
    local[0, 0] = dot(scores, value_low)
    query_reach[0, 0] = (query * reach).astype(LOW)
    cumulative_out[0, 0] = cumulative
    scores_out[0, 0] = scores


def mix_end_kernel(local, query_reach, incoming, out):
    separated(local[0, 0] + dot(query_reach[0, 0], incoming[0, 0]), out)


def mix_state_grad_kernel(query_reach, grads, out):
    out[0, 0] = dot_tn(query_reach[0, 0], interleaved(grads))


def mix_back_kernel(
    where, f, v, q, lower, starts, starts_row, cumulative_in, scores_in, grads, incoming, next_grad, decay,
    df, dv, dq, lower_grad,
):
    rows = f.shape[3]
    forget_pre, value, query_pre, upstream = interleaved(f), interleaved(v), interleaved(q), interleaved(grads)
    span = forget_pre.shape[0]
    is_start = starts[0].astype(F32) == 1.0
    low_bound = lower[0]
    forget_sig, gate, key, log_decay = gate_terms(forget_pre, low_bound, is_start)
    causal = causal_of(where, span, rows)
    low = causal.astype(LOW)
    cumulative = cumulative_in[0, 0]
    total = jnp.sum(log_decay, axis=0, keepdims=True)
    reach, between, grow, shrink, suffix, _ = decay_terms(causal, starts[0], starts_row[0], cumulative, total)
    query_sig = sigmoid(query_pre)
    query_ext = (query_pre * query_sig * grow).astype(LOW)
    key_shrink = (key * shrink).astype(LOW)
    key_suffix = (key * suffix).astype(LOW)
    value_low = value.astype(LOW)
    state, after_state = incoming[0, 0], next_grad[0, 0]
    grad_scores = (dot_nt(upstream, value_low) * between).astype(LOW)
    grad_ext = dot(grad_scores, key_shrink) + reach * dot_nt(upstream, state)
    grad_shrink = dot_tn(grad_scores, query_ext)
    grad_suffix = dot_nt(value_low, after_state)
    grad_value = dot_tn(scores_in[0, 0], upstream) + dot(key_suffix, after_state)
    suffix_term = key_suffix.astype(F32) * grad_suffix
    terms = query_ext.astype(F32) * grad_ext - key_shrink.astype(F32) * grad_shrink - suffix_term
    ones = jnp.ones((8, HDIM), LOW)
    state_term = thirds(decay[0, 0] * state.astype(F32) * after_state.astype(F32))
    state_row = (dot_nt(ones, state_term[0]) + dot_nt(ones, state_term[1]) + dot_nt(ones, state_term[2]))[:1]
    grad_total = jnp.sum(suffix_term, axis=0, keepdims=True) + state_row
    parts = thirds(terms)
    grad_log = dot_tn(low, parts[0]) + dot_tn(low, parts[1]) + dot_tn(low, parts[2]) + grad_total
    grad_key = grad_shrink * shrink + grad_suffix * suffix
    grad_forget = jnp.where(is_start, 0.0, grad_log / gate) - grad_key
    lower_grad[0, 0] = jnp.broadcast_to(
        jnp.sum(grad_forget * (1.0 - forget_sig), axis=0, keepdims=True), lower_grad.shape[2:]
    )
    separated(grad_forget * (1.0 - low_bound) * forget_sig * (1.0 - forget_sig), df)
    separated(grad_value, dv)
    separated(grad_ext * grow * query_sig * (1.0 + query_pre * (1.0 - query_sig)), dq)


def branch_kernel(plan, names, part, where, tokens, gain_state, gain_ffn, *rest):
    mixed_in, rest = rest[: plan.plane], rest[plan.plane :]
    own, other, mixed, normed_parts, residual, normed_ffn, weight, sems = rest
    here = where[2]
    moves = fetch(
        plan, where,
        [(ref.at[t, u, m], i, j, k, e) for ref, e in ((own, where[3]), (other, where[3] ^ 1)) for t, u, m, i, j, k in names],
        weight, sems,
    )
    for k in range(plan.plane):
        for e in range(plan.nc):
            at = pl.multiple_of(((here ^ k) * plan.nc + e) * part, part)
            mixed[:, pl.ds(at, part)] = mixed_in[k][e].astype(F32)
    values = mixed[...]
    normed = (values * inverse_rms(values) * gain_state[...]).astype(LOW)
    normed_ffn[...] = normed
    for k in range(plan.plane):
        for e in range(plan.nc):
            at = pl.multiple_of(((here ^ k) * plan.nc + e) * part, part)
            normed_parts[k, e] = normed_ffn[:, pl.ds(at, part)]
    for move in moves:
        move.wait()
    total = tokens[...].astype(F32) + dot(normed, weight[...].reshape(-1, weight.shape[-1]))
    residual[...] = total
    normed_ffn[...] = (total * inverse_rms(total) * gain_ffn[...]).astype(LOW)


def branch_back_kernel(
    plan, part, where, upstream, cotangent, residual, mixed, gain_state, gain_ffn, weight,
    grad_residual, branch, grad_parts, scratch,
):
    here = where[2]
    values = residual[...]
    grad = cotangent[...].astype(F32) + norm_back(values, inverse_rms(values), upstream[...] * gain_ffn[...])
    grad_residual[...] = grad
    low = grad.astype(LOW)
    branch[...] = low
    values = mixed[...]
    scaled = dot_nt(low, weight[...].reshape(-1, weight.shape[-1])) * gain_state[...]
    scratch[...] = norm_back(values, inverse_rms(values), scaled).astype(LOW)
    for k in range(plan.plane):
        for e in range(plan.nc):
            at = pl.multiple_of(((here ^ k) * plan.nc + e) * part, part)
            grad_parts[k, e] = scratch[:, pl.ds(at, part)]


def inputs_grad_kernel(df, dv, dq, weight, out):
    part = df.shape[1]
    full = weight[...].reshape(-1, weight.shape[-1])
    out[...] = (
        dot_nt(df[...], full[:, :part]) + dot_nt(dv[...], full[:, part : 2 * part])
        + dot_nt(dq[...], full[:, 2 * part :])
    ).astype(out.dtype)


def body(
    plan, tokens, starts, w_query, w_forget, w_input, w_output, gain_mix, lower_bound, gain_state,
    w_gate, w_up, w_down, gain_ffn, cotangent,
):
    ny, nx, nh, nl, nc, plane, copies = (
        plan.ny, plan.nx, plan.nh, plan.nl, plan.nc, plan.plane, plan.copies
    )
    y, x_, h, l, c = (lax.axis_index(a) for a in AXES)
    here = x_ * nl + l
    where = jnp.stack([y, h, here, c, l * nc, x_]).astype(jnp.int32)
    rows, width = tokens.shape
    r = w_query.shape[0]
    part = width // (plane * nc)
    ffr = w_down.shape[0]
    units = copies * ffr
    heads = part // HDIM
    span = nl * nc * rows
    half = plane * rows
    names = [(i, j) for i in range(nh) for j in range(ny)]

    def fence(*values):
        return lax.optimization_barrier(values)

    def from_plane(blocks):
        return [blocks[0]] + [
            lax.ppermute(blocks[k], ("x", "l"), [(i, i ^ k) for i in range(plane)]) for k in range(1, plane)
        ]

    def swap(x, axis):
        return lax.ppermute(x, axis, [(0, 1), (1, 0)])

    def to_cores(x):
        return lax.all_to_all(x, "chip", 0, 0, tiled=True)

    def turn(x, axis, n):
        return lax.ppermute(x, axis, [(i, (i + 1) % n) for i in range(n)])

    def turns(x, axis, n):
        out = [x]
        for _ in range(1, n):
            out.append(turn(out[-1], axis, n))
        return out

    def over_plane(pieces):
        mine = jnp.concatenate(pieces)
        return to_cores(jnp.stack([mine, mine])).reshape(nc * mine.shape[0], -1)

    def summed_core(x):
        x = to_cores(x.reshape(nc, half, -1)).astype(F32)
        return x[0] + x[1]

    def summed_plane(both):
        both = both.reshape(plane, rows, -1)
        sent = both[1:].astype(LOW)
        got = from_plane([both[0]] + [sent[k] for k in range(plane - 1)])
        return sum((z.astype(F32) for z in got[1:]), got[0])

    def at_plane(x, axis):
        return [lax.dynamic_index_in_dim(x, here ^ k, axis, keepdims=False) for k in range(plane)]

    def collect(sides):
        got = from_plane(
            [lax.dynamic_index_in_dim(sides[k // nl], l ^ (k % nl), 0, keepdims=False) for k in range(plane)]
        )
        return jnp.stack(got, axis=1)

    def to_parts(x):
        return jnp.stack(from_plane([x[k] for k in range(plane)]), axis=1)

    def scatter_y(sent, kept):
        total = sent
        for i, mine in enumerate(kept):
            total = turn(total, "y", ny).astype(F32) + mine.astype(F32)
            total = total.astype(LOW) if i < len(kept) - 1 else total
        return total

    def scatter_h(x):
        def block(i):
            return lax.dynamic_index_in_dim(x, (h - i) % nh, 0, keepdims=False)

        total = block(1 % nh)
        for i in range(2, nh + 1):
            total = turn(total.astype(LOW), "h", nh).astype(F32) + block(i % nh)
        return total

    def rows_of_y(x):
        out = [lax.dynamic_index_in_dim(x, (y - i) % ny, 0, keepdims=False) for i in range(1, ny + 1)]
        return out[0], out[1:]

    small = jnp.concatenate([gain_mix, gain_state, gain_ffn, lower_bound, starts.astype(F32)]).reshape(1, -1)
    small_mine = jnp.concatenate(from_plane([small] * plane))
    small_other = lax.ppermute(small_mine, "chip", [(i, i ^ 1) for i in range(nc)])
    plane_small = jnp.concatenate([pick(c == 0, small_mine, small_other), pick(c == 0, small_other, small_mine)])
    vectors = jnp.concatenate(
        [z for x in turns(plane_small[:, : 4 * r], "h", nh) for z in turns(x, "y", ny)]
    )
    spread = lambda w: w.reshape(r, plane, nc, part)
    three = jnp.concatenate([spread(w_forget), spread(w_input), spread(w_query)], axis=3).transpose(2, 1, 0, 3)
    three = jnp.concatenate(from_plane(at_plane(to_cores(three), 1)))
    down_line = turns(after(w_down, vectors), "h", nh)
    out_first = turns(w_output, "y", ny)
    tokens_pair = jnp.concatenate([tokens, swap(after(tokens, three), "l")])
    cotangent_x = swap(after(cotangent, three), "x")
    (packed,) = call(partial(pack_kernel, plan, ffr), [shape((nc, plane, r, 2 * units), LOW)], w_gate, w_up)
    packed = to_cores(packed)
    plane_small, vectors, three, down_line, out_first, tokens_pair, cotangent_x, packed, w_output = fence(
        plane_small, vectors, three, down_line, out_first, tokens_pair, cotangent_x, packed, w_output
    )

    three_line = turns(three, "h", nh)
    three_first = turns(three, "y", ny)
    out_line = turns(after(w_output, three_line), "h", nh)
    tokens_far = swap(tokens_pair, "x")
    cotangent_l = swap(jnp.concatenate([cotangent, cotangent_x]), "l")
    gate_up = from_plane(after(at_plane(packed, 1), tokens_far, cotangent_l))
    gate_up = [jnp.concatenate(gate_up[:nl]), jnp.concatenate(gate_up[nl:])]
    three_line, three_first, out_line, tokens_pair, tokens_far, cotangent_l, gate_up, down_line = fence(
        three_line, three_first, out_line, tokens_pair, tokens_far, cotangent_l, gate_up, down_line
    )

    three = three_first + [z for x in three_line[1:] for z in turns(x, "y", ny)]
    out_copies = out_first + [z for x in out_line[1:] for z in turns(x, "y", ny)]
    gu_first = jnp.stack(turns(gate_up[0], "h", nh))
    plane_tokens = over_plane([tokens_pair, tokens_far])
    plane_starts = (
        plane_small[:, 4 * r :].reshape(nc, nx, nl, rows).transpose(1, 2, 0, 3).reshape(nx, span)
    )
    starts_row = jnp.broadcast_to(plane_starts[:, None], (nx, 8, span)).astype(LOW)
    starts_wide = jnp.broadcast_to(plane_starts[:, :, None], (nx, span, HDIM)).astype(LOW)
    places = jnp.stack([
        plan.owner((y - j) % ny, here ^ k, (h - i) % nh, e)
        for i, j in names for e in range(nc) for k in range(plane)
    ])
    ordered = (jnp.arange(plan.devices)[:, None] == places[None, :]).astype(F32)
    vectors = jnp.dot(ordered, vectors, precision=lax.Precision.HIGHEST)
    vectors = vectors.reshape(plan.devices, 4, r).transpose(1, 0, 2).reshape(4, width)
    full_gain_mix, full_gain_state, full_gain_ffn = (vectors[i : i + 1] for i in range(3))
    lower = lax.dynamic_slice_in_dim(vectors[3], (here * nc + c) * part, part).reshape(heads, 1, HDIM)
    count = plan.devices
    total = nc * half
    project_flops = 2 * total * width * 3 * part
    normed_in, pre, w_three = call(
        partial(project_kernel, plan, names),
        [shape((total, width), LOW), shape((total, 3 * part)), shape((count, r, 3 * part), LOW)],
        where, plane_tokens, full_gain_mix, *three,
        specs=[SMEM, VMEM, VMEM] + [ANY] * copies,
        scratch=[pltpu.SemaphoreType.DMA((count,))],
        flops=project_flops,
    )
    down_line, gate_up, pre, out_copies, lower, starts_wide, starts_row, gu_first = fence(
        down_line, gate_up, pre, out_copies, lower, starts_wide, starts_row, gu_first
    )

    by_group = lambda x: x.reshape(nc, nx, nl, rows, -1)
    piece = lambda i: pl.BlockSpec((nc, 1, nl, rows, HDIM), lambda g, a, i=i: (0, g, 0, 0, i * heads + a))
    state_spec = pl.BlockSpec((1, 1, HDIM, HDIM), lambda g, a: (g, a, 0, 0))
    rows_spec = pl.BlockSpec((1, 1, span, HDIM), lambda g, a: (g, a, 0, 0))
    scores_spec = pl.BlockSpec((1, 1, span, span), lambda g, a: (g, a, 0, 0))
    head_spec = pl.BlockSpec((1, 1, HDIM), lambda g, a: (a, 0, 0))
    starts_spec = pl.BlockSpec((1, span, HDIM), lambda g, a: (g, 0, 0))
    starts_row_spec = pl.BlockSpec((1, 8, span), lambda g, a: (g, 0, 0))
    pre_args = (by_group(pre),) * 3
    pre_specs = [piece(0), piece(1), piece(2)]
    states = (nx, heads, HDIM, HDIM)
    by_row = (nx, heads, span, HDIM)
    grouped = (nc, nx, nl, rows, part)
    mix_flops = nx * heads * 2 * span * span * HDIM
    end_state, decay, local, query_reach, cumulative, scores = call(
        mix_kernel,
        [shape(states), shape(states), shape(by_row), shape(by_row, LOW), shape(by_row),
         shape((nx, heads, span, span), LOW)],
        where, *pre_args, lower, starts_wide, starts_row,
        grid=(nx, heads),
        specs=[SMEM] + pre_specs + [head_spec, starts_spec, starts_row_spec],
        out_specs=[state_spec, state_spec, rows_spec, rows_spec, rows_spec, scores_spec],
        flops=8 * mix_flops,
    )
    down_blocks = turns(jnp.stack(down_line), "y", ny)
    gu_second = jnp.stack(turns(gate_up[1], "h", nh))
    cut = copies // 2
    pieces = [jnp.stack(out_copies[:cut]), jnp.stack(out_copies[cut:])]
    moved = [swap(z, axis) for z, axis in zip(pieces, ("l", "x"))]
    pairs = [jnp.stack([a, z]) for a, z in zip(pieces, moved)]
    moved = [swap(z, axis) for z, axis in zip(pairs, ("x", "l"))]
    groups = jnp.stack([pairs[0], moved[0], pairs[1], moved[1]])
    out_names = [
        (t * 2 + distance, u, m, *names[t * cut + m], u * nl + distance if t else distance * nl + u)
        for t in range(2) for distance in range(2) for u in range(2) for m in range(cut)
    ]
    end_state, decay, local, query_reach, down_blocks, gu_first, groups, gu_second = fence(
        end_state, decay, local, query_reach, down_blocks, gu_first, groups, gu_second
    )

    def carry(block, step):
        incoming = jnp.zeros_like(block)
        for t in range(nh - 1):
            pairs = [(i, i + step) for i in range(nh) if 0 <= i + step < nh]
            sent = decay * incoming + block if t else block
            incoming = lax.ppermute(sent.astype(LOW), "h", pairs)
            incoming = incoming if t == nh - 2 else incoming.astype(F32)
        return incoming

    incoming = carry(end_state, 1)
    (mixed,) = call(
        mix_end_kernel, [shape(grouped, LOW)], local, query_reach, incoming,
        grid=(nx, heads), specs=[rows_spec, rows_spec, state_spec], out_specs=[piece(0)], flops=mix_flops // 4,
    )
    mixed = to_cores(mixed.reshape(nc, plane, rows, part))
    mixed_in = from_plane([mixed[:, k] for k in range(plane)])
    gu_first = turns(gu_first, "y", ny)
    groups_other = lax.ppermute(groups, "chip", [(i, i ^ 1) for i in range(nc)])
    mixed_in, gu_first, groups, groups_other, down_blocks, gu_second = fence(
        mixed_in, gu_first, groups, groups_other, down_blocks, gu_second
    )

    parts_shape = (plane, nc, rows, part)
    mixed, normed_parts, residual, normed_ffn, w_out_full = call(
        partial(branch_kernel, plan, out_names, part),
        [shape((rows, width)), shape(parts_shape, LOW), shape((rows, width)), shape((rows, width), LOW),
         shape((count, r, width), LOW)],
        where, tokens, full_gain_state, full_gain_ffn, *mixed_in, groups, groups_other,
        specs=[SMEM] + [VMEM] * (3 + plane) + [ANY] * 2,
        scratch=[pltpu.SemaphoreType.DMA((count,))],
        flops=2 * rows * width * width,
    )
    ffn_pieces = from_plane([normed_ffn] * plane)
    gate_up = gu_first + turns(gu_second, "y", ny)
    plane_cotangent = over_plane([cotangent, cotangent_l[:rows], cotangent_x, cotangent_l[rows:]])
    down = jnp.zeros((ny, nh, ffr, width), LOW)
    for j, blocks in enumerate(down_blocks):
        for i in range(nh):
            down = lax.dynamic_update_slice(down, blocks[i][None, None], ((y - j) % ny, (h - i) % nh, 0, 0))
    down = down.reshape(units, width)
    ffn_pieces, gate_up, down, normed_parts, plane_cotangent = fence(
        ffn_pieces, gate_up, down, normed_parts, plane_cotangent
    )

    plane_ffn = over_plane(ffn_pieces)
    gu_names = [(j, k) for k in (0, nl) for j in range(ny)]
    step = min(256, half)
    row_spec = lambda n: pl.BlockSpec((step, n), lambda t: (t, 0))
    hidden, grad_gu, part_out, part_ffn = call(
        partial(ffn_kernel, plan, gu_names),
        [shape((total, units), LOW), shape((total, 2 * units), LOW), shape((total, width), LOW),
         shape((total, width), LOW)],
        where, plane_ffn, plane_cotangent, down, *gate_up,
        grid=(total // step,),
        specs=[SMEM, row_spec(width), row_spec(width), VMEM] + [ANY] * len(gate_up),
        out_specs=[row_spec(units), row_spec(2 * units), row_spec(width), row_spec(width)],
        scratch=[pltpu.VMEM((count, r, 2 * units), LOW), pltpu.SemaphoreType.DMA((count,))],
        flops=2 * total * width * units * 7,
    )
    mix_parts = to_parts(normed_parts)
    lcr = nl * nc * r

    def columns_grad(turns, dtype, sides, normed, grads):
        n = sum(g.shape[1] for g in grads)
        return call(
            partial(columns_grad_kernel, plan, turns, sides, len(grads)), [shape((nh, len(sides), lcr, n), dtype)],
            where, normed, *grads, specs=[SMEM] + [VMEM] * (1 + len(grads)),
            flops=2 * total * width * n * len(sides) // (ny * nx),
        )[0]

    def columns_kept(sides, *arrays):
        return [columns_grad(i % ny, F32 if i == ny else LOW, sides, *arrays) for i in range(2, ny + 1)]

    both_ffn = summed_core(part_ffn)
    far_sent = columns_grad(1, LOW, (1,), plane_ffn, [grad_gu])
    both_ffn, far_sent, plane_ffn, grad_gu, hidden, mix_parts, plane_cotangent, part_out = fence(
        both_ffn, far_sent, plane_ffn, grad_gu, hidden, mix_parts, plane_cotangent, part_out
    )

    grad_normed_ffn = summed_plane(both_ffn)
    near_sent = columns_grad(1, LOW, (0,), plane_ffn, [grad_gu])
    grad_gu_far = scatter_y(far_sent, columns_kept((1,), plane_ffn, [grad_gu]))
    (grad_down,) = call(
        rows_grad_kernel, [shape((units, width), LOW)], hidden, plane_cotangent, flops=2 * total * units * width,
    )
    both_out = summed_core(after(part_out, near_sent))
    grad_gu_far, grad_normed_ffn, near_sent, grad_down, plane_ffn, grad_gu, both_out = fence(
        grad_gu_far, grad_normed_ffn, near_sent, grad_down, plane_ffn, grad_gu, both_out
    )

    grad_gu_near = scatter_y(near_sent, columns_kept((0,), plane_ffn, [grad_gu]))
    grad_residual, branch, grad_parts = call(
        partial(branch_back_kernel, plan, part),
        [shape((rows, width)), shape((rows, width), LOW), shape(parts_shape, LOW)],
        where, grad_normed_ffn, cotangent, residual, mixed, full_gain_state, full_gain_ffn, w_out_full,
        specs=[SMEM] + [VMEM] * 7,
        scratch=[pltpu.VMEM((rows, width), LOW)],
        flops=2 * rows * width * width,
    )
    grads = to_parts(grad_parts)
    branch_pieces = from_plane([after(branch, grads)] * plane)
    grad_gu_far = scatter_h(grad_gu_far)
    grads = by_group(to_cores(grads))
    (state_grad,) = call(
        mix_state_grad_kernel, [shape(states)], query_reach, grads,
        grid=(nx, heads), specs=[rows_spec, piece(0)], out_specs=[state_spec], flops=mix_flops // 4,
    )
    mix_parts = to_cores(mix_parts)
    grad_gu_near, state_grad, grads, branch_pieces, grad_gu_far, grad_down, both_out, mix_parts = fence(
        grad_gu_near, state_grad, grads, branch_pieces, grad_gu_far, grad_down, both_out, mix_parts
    )

    next_grad = carry(state_grad, -1)
    output = (residual + summed_plane(both_out)).astype(LOW)
    grad_down = scatter_y(*rows_of_y(grad_down.reshape(ny, nh, ffr, width)))
    df, dv, dq, lower_grad = call(
        mix_back_kernel,
        [shape(grouped, LOW)] * 3 + [shape((nx, heads, 8, HDIM))],
        where, *pre_args, lower, starts_wide, starts_row, cumulative, scores, grads, incoming, next_grad, decay,
        grid=(nx, heads),
        specs=[SMEM] + pre_specs + [head_spec, starts_spec, starts_row_spec, rows_spec, scores_spec]
        + [piece(0), state_spec, state_spec, state_spec],
        out_specs=[piece(0)] * 3 + [pl.BlockSpec((1, 1, 8, HDIM), lambda g, a: (g, a, 0, 0))],
        flops=12 * mix_flops,
    )
    pre_grads = [g.reshape(total, part) for g in (df, dv, dq)]
    (part_in,) = call(
        inputs_grad_kernel, [shape((total, width), LOW)], *pre_grads, w_three, flops=project_flops
    )
    both_in = summed_core(part_in)
    three_sent = columns_grad(1, LOW, (0, 1), normed_in, pre_grads)
    both_in, three_sent, pre_grads, branch_pieces, grad_down, grad_gu_near, output = fence(
        both_in, three_sent, pre_grads, branch_pieces, grad_down, grad_gu_near, output
    )

    grad_normed_in = summed_plane(both_in)
    grad_three = scatter_y(three_sent, columns_kept((0, 1), normed_in, pre_grads))
    grad_gu_near = scatter_h(grad_gu_near)
    (grad_out,) = call(
        rows_grad_kernel, [shape((part, width), LOW)], mix_parts.reshape(total, part), over_plane(branch_pieces),
        flops=2 * total * part * width,
    )
    grad_three, grad_normed_in, grad_gu_near, grad_out, grad_down, grad_gu_far = fence(
        grad_three, grad_normed_in, grad_gu_near, grad_out, grad_down, grad_gu_far
    )

    own_tokens = tokens.astype(F32)
    grad_tokens = grad_residual + norm_back(own_tokens, inverse_rms(own_tokens), grad_normed_in * full_gain_mix)
    grad_three = scatter_h(grad_three).astype(LOW).reshape(nx, nl, nc, r, 3 * part)
    grad_output = scatter_y(*rows_of_y(grad_out.reshape(ny, nh, r, width)))
    gu_blocks = collect([z.astype(LOW).reshape(nl, nc, r, 2 * units) for z in (grad_gu_near, grad_gu_far)])
    lower_grad = jnp.sum(lower_grad[:, :, 0], axis=0).reshape(1, part)
    lower_grad = sum(turns(lower_grad, "y", ny))
    grad_three, grad_output, gu_blocks, lower_grad, grad_down = fence(
        grad_three, grad_output, gu_blocks, lower_grad, grad_down
    )

    three_blocks = collect([grad_three[t] for t in range(nx)])
    grad_output = scatter_h(grad_output)
    lower_grad = sum(turns(lower_grad, "h", nh))
    grad_down = scatter_h(after(grad_down, lower_grad))
    owners = []
    for j in range(ny):
        for p in range(nx):
            for i in range(nh):
                for o in range(nl):
                    for e in range(nc):
                        owners.append(((p * nl + o) * nc + e) * copies + j * nh + i)
    pairs = list(enumerate(owners))
    along = shape((r, HDIM))
    grad_w_gate, grad_w_up, along_ffn = call(
        partial(unpack_kernel, plan, ffr), [shape(w_gate.shape), shape(w_up.shape), along],
        where, to_cores(gu_blocks), w_gate, w_up, specs=[SMEM] + [VMEM] * 3,
        scratch=[pltpu.VMEM((nc, plane, r, 2 * units), LOW)],
    )
    grad_w_forget, grad_w_input, grad_w_query, along_mix = call(
        partial(unpack_part_kernel, plan, part), [shape(w_query.shape)] * 3 + [along],
        where, to_cores(three_blocks), w_forget, w_input, w_query, specs=[SMEM] + [VMEM] * 4,
    )
    grad_output = lax.ppermute(grad_output.astype(LOW), AXES, pairs).astype(F32)
    lower_grad = lax.dynamic_index_in_dim(lower_grad.reshape(copies, r), y * nh + h, 0, keepdims=False)
    lower_grad = lax.ppermute(lower_grad, AXES, pairs)
    grad_gain_mix = along_mix[:, 0] / gain_mix
    grad_gain_ffn = along_ffn[:, 0] / gain_ffn
    grad_gain_state = jnp.sum(w_output.astype(F32) * grad_output, axis=1) / gain_state
    return (
        output, grad_tokens, grad_w_query, grad_w_forget, grad_w_input, grad_output, grad_gain_mix, lower_grad,
        grad_gain_state, grad_w_gate, grad_w_up, grad_down, grad_gain_ffn,
    )


def solution(mesh):
    nb, ns, nc = (mesh.shape[a] for a in ("batch", "seq", "chip"))
    sizes = (nb // 2, 2, ns // 2, 2, nc)
    fine = jax.sharding.Mesh(mesh.devices.reshape(sizes), AXES)
    flat, matrix = P(AXES), P(AXES, None)
    return jax.shard_map(
        partial(body, Plan(sizes)),
        mesh=fine,
        in_specs=(
            matrix, flat, matrix, matrix, matrix, matrix, flat, flat, flat, matrix, matrix, matrix, flat, matrix,
        ),
        out_specs=(
            matrix, matrix, matrix, matrix, matrix, matrix, flat, flat, flat, matrix, matrix, matrix, flat,
        ),
        check_vma=False,
    )
```

time: 807 us -> 709 us (0.88)
  Pallas kernels: 0 us -> 154 us
  waiting for transfers between devices: 362 us -> 230 us
  matrix products: 93.5 us -> 0.14 us
  local copies, waits for them, and re-layouts: 118 us -> 38.7 us
  blocking collectives: 0 us -> 55.9 us
  starting transfers between devices: 92.6 us -> 137 us
  other arithmetic: 110 us -> 77.5 us
  between operations: 17.2 us -> 2.2 us
    pallas_call x0 -> x20, Pallas kernels: none -> 154 us  [call(): pl.pallas_call(kernel, out_shape=outs, grid=grid, in_specs=specs, out_spe...]
    ppermute x102 -> x80, waiting for transfers between devices: 362 us -> 225 us  [the longest x39 85.2 us: from_plane(): lax.ppermute(blocks[k], ('x', 'l'), [(i, i ^ k) for i in range(plane)])]
    dot_general x28 -> x1, matrix products: 93.5 us -> 0.14 us  [body(): vectors = jnp.dot(ordered, vectors, precision=lax.Precision.HIGHEST)]
    all_to_all x0 -> x8, blocking collectives: none -> 55.9 us  [to_cores(): return lax.all_to_all(x, 'chip', 0, 0, tiled=True)]
    all_to_all x0 -> x6, starting transfers between devices: none -> 28.1 us  [to_cores(): return lax.all_to_all(x, 'chip', 0, 0, tiled=True)]
    convert_element_type x24 -> x8, other arithmetic: 39.4 us -> 13.9 us  [the longest x3 8.69 us: summed_core(): x = to_cores(x.reshape(nc, half, -1)).astype(F32)]
    add x4 -> x15, other arithmetic: 3.29 us -> 26.4 us  [the longest x5 9.12 us: scatter_y(): total = turn(total, 'y', ny).astype(F32) + mine.astype(F32)]
    dot_general x5 -> x0, local copies, waits for them, and re-layouts: 18.6 us -> none  [the longest x4 16.4 us: dot_tn(): lax.dot_general(left, right, (((0,), (0,)), ((), ())), preferred_element_...]
  transfers between devices with their start and end apart: 103 -> 86, of which waited for: 46 -> 25; matrix products, arithmetic and copies ran while one was open for 34% -> 14% of each run, Pallas kernels for 0% -> 16%
where the time goes in v2:
time: 709 us; the launch traced here: 695 us
  waiting for transfers between devices  230 us (32%)
  Pallas kernels  154 us (22%)
  starting transfers between devices  137 us (19%)
  other arithmetic  77.5 us (11%)
  blocking collectives  55.9 us (8%)
  local copies, waits for them, and re-layouts  38.7 us (5%)
    pallas_call x20, Pallas kernels, call(): pl.pallas_call(kernel, out_shape=outs, grid=grid, in_specs=specs, out_spe...  154 us
    ppermute x39, waiting for transfers between devices, from_plane(): lax.ppermute(blocks[k], ('x', 'l'), [(i, i ^ k) for i in range(plane)])  85.2 us
    ppermute x27, waiting for transfers between devices, turn(): return lax.ppermute(x, axis, [(i, (i + 1) % n) for i in range(n)])  80 us
    ppermute x8, waiting for transfers between devices, swap(): return lax.ppermute(x, axis, [(0, 1), (1, 0)])  57.2 us
    all_to_all x8, blocking collectives, to_cores(): return lax.all_to_all(x, 'chip', 0, 0, tiled=True)  55.9 us
    ppermute x39, starting transfers between devices, from_plane(): lax.ppermute(blocks[k], ('x', 'l'), [(i, i ^ k) for i in range(plane)])  47.5 us
    ppermute x27, starting transfers between devices, turn(): return lax.ppermute(x, axis, [(i, (i + 1) % n) for i in range(n)])  39.1 us
    all_to_all x6, starting transfers between devices, to_cores(): return lax.all_to_all(x, 'chip', 0, 0, tiled=True)  28.1 us
  transfers between devices with their start and end apart: 86, of which 25 were waited for; matrix products, arithmetic and copies ran while one was open for 14% of the time, Pallas kernels for 16%

profile of v2, /device:TPU:2, one launch (start us, length us, event | category | flops | bytes accessed | tf_op | source)
XLA Modules:
  0.0 695.3 jit_solution(1310661096052032522)
XLA Ops:
  43.6 10.4 %collective-permute-done.12 = bf16[128,2048]{1,0:T(8,128)(2,1)} collective-permute-done((bf16[128,2048]{1,0:T(8,128)(2,1)S(1)}, bf16[128,2048]{1,0:T(8,128)(2,1)}, u32[]{:S(2)}, u32[]{:S(2)}) %collective-permute-start.12) | collective-permute-done | bytes 524320 | tf_op jit(solution)/shard_map/ppermute | solution.py:433
  56.2 9.9 %collective-permute-done.10 = bf16[176,2048]{1,0:T(8,128)(2,1)} collective-permute-done((bf16[176,2048]{1,0:T(8,128)(2,1)}, bf16[176,2048]{1,0:T(8,128)(2,1)}, u32[]{:S(2)}, u32[]{:S(2)}) %collective-permute-start.10) | collective-permute-done | bytes 720928 | tf_op jit(solution)/shard_map/ppermute | solution.py:439
  70.7 18.3 %collective-permute-done.17 = bf16[256,2048]{1,0:T(8,128)(2,1)S(1)} collective-permute-done((bf16[256,2048]{1,0:T(8,128)(2,1)}, bf16[256,2048]{1,0:T(8,128)(2,1)S(1)}, u32[]{:S(2)}, u32[]{:S(2)}) %collective-permute-start.17) | collective-permute-done | bytes 1048608 | tf_op jit(solution)/shard_map/ppermute | solution.py:433
  89.0 18.1 %collective-permute-done.18 = bf16[256,2048]{1,0:T(8,128)(2,1)} collective-permute-done((bf16[256,2048]{1,0:T(8,128)(2,1)S(1)}, bf16[256,2048]{1,0:T(8,128)(2,1)}, u32[]{:S(2)}, u32[]{:S(2)}) %collective-permute-start.18) | collective-permute-done | bytes 1048608 | tf_op jit(solution)/shard_map/ppermute | solution.py:433
  114.2 10.1 %collective-permute-done.19 = bf16[2,64,1408]{2,1,0:T(8,128)(2,1)S(1)} collective-permute-done((bf16[2,64,1408]{2,1,0:T(8,128)(2,1)}, bf16[2,64,1408]{2,1,0:T(8,128)(2,1)S(1)}, u32[]{:S(2)}, u32[]{:S(2)}) %collective-permute-start.19) | collective-permute-done | bytes 360480 | tf_op jit(solution)/shard_map/ppermute | solution.py:429
  145.5 18.3 %collective-permute-done.24 = bf16[4,64,1408]{2,1,0:T(8,128)(2,1)S(1)} collective-permute-done((bf16[4,64,1408]{2,1,0:T(8,128)(2,1)S(1)}, bf16[4,64,1408]{2,1,0:T(8,128)(2,1)S(1)}, u32[]{:S(2)}, u32[]{:S(2)}) %collective-permute-start.24) | collective-permute-done | bytes 720928 | tf_op jit(solution)/shard_map/ppermute | solution.py:439
  165.1 11.4 %shard_map.238 = (bf16[1024,2048]{1,0:T(8,128)(2,1)}, f32[1024,768]{1,0:T(8,128)}, bf16[32,64,768]{2,1,0:T(8,128)(2,1)}) custom-call(s32[6]{0:T(128)} %stack.286.where, bf16[1024,2048]{1,0:T(8,128)(2,1)} %bitcast.16.x, f32[1,2048]{1,0:T(1,128)} %slice.184.gain, bf16[8,64,768]{2,1,0:T(8,128)(2,1)} %pad_maximum_fusion.13.rest_0_, ...), custom_call_target="tpu_custom_call" | custom-call | flops 3221225472 | bytes 17834008 | tf_op jit(solution)/shard_map/pallas_call | solution.py:65
  182.5 9.5 %collective-permute-done.28 = bf16[2,64,2048]{2,1,0:T(8,128)(2,1)S(1)} collective-permute-done((bf16[2,64,2048]{2,1,0:T(8,128)(2,1)S(1)}, bf16[2,64,2048]{2,1,0:T(8,128)(2,1)S(1)}, u32[]{:S(2)}, u32[]{:S(2)}) %collective-permute-start.28) | collective-permute-done | bytes 524320 | tf_op jit(solution)/shard_map/ppermute | solution.py:433
  195.8 9.6 %shard_map.239 = (f32[2,2,128,128]{3,2,1,0:T(8,128)}, f32[2,2,128,128]{3,2,1,0:T(8,128)}, f32[2,2,512,128]{3,2,1,0:T(8,128)}, bf16[2,2,512,128]{3,2,1,0:T(8,128)...) custom-call(s32[6]{0:T(128)} %stack.286.where, f32[2,2,2,128,768]{4,3,2,1,0:T(8,128)} %bitcast.225, ...), custom_call_target="tpu_custom_call" | custom-call | flops 2147483648 | bytes 14959640 | tf_op jit(solution)/shard_map/pallas_call | solution.py:65
  205.3 24.4 %collective-permute-done.30 = bf16[4,64,1408]{2,1,0:T(8,128)(2,1)} collective-permute-done((bf16[4,64,1408]{2,1,0:T(8,128)(2,1)S(1)}, bf16[4,64,1408]{2,1,0:T(8,128)(2,1)}, u32[]{:S(2)}, u32[]{:S(2)}) %collective-permute-start.30) | collective-permute-done | bytes 720928 | tf_op jit(solution)/shard_map/ppermute | solution.py:439
  270.9 10.3 %shard_map.241 = (f32[128,2048]{1,0:T(8,128)}, bf16[4,2,128,256]{3,2,1,0:T(8,128)(2,1)}, f32[128,2048]{1,0:T(8,128)}, bf16[128,2048]{1,0:T(8,128)(2,1)}, bf16[32,64,2048]{2,1,0:T(8,128)(2,1)}) custom-call(s32[6]{0:T(128)} %stack.286.where, bf16[128,2048]{1,0:T(8,128)(2,1)} %tokens.1, f32[1,2048]{1,0:T(1,128)} %slice.188.gain_state, ...), custom_call_target="tpu_custom_call" | custom-call | flops 1073741824 | bytes 20987928 | tf_op jit(solution)/shard_map/pallas_call | solution.py:65
  296.4 12.5 %collective-permute-done.38 = bf16[128,2048]{1,0:T(8,128)(2,1)} collective-permute-done((bf16[128,2048]{1,0:T(8,128)(2,1)}, bf16[128,2048]{1,0:T(8,128)(2,1)}, u32[]{:S(2)}, u32[]{:S(2)}) %collective-permute-start.38) | collective-permute-done | bytes 524320 | tf_op jit(solution)/shard_map/ppermute | solution.py:429
  308.9 9.5 %collective-permute-done.40.rest_3_ = bf16[2,4,64,1408]{3,2,1,0:T(8,128)(2,1)} collective-permute-done((bf16[2,4,64,1408]{3,2,1,0:T(8,128)(2,1)S(1)}, bf16[2,4,64,1408]{3,2,1,0:T(8,128)(2,1)}, u32[]{:S(2)}, u32[]{:S(2)}) %collective-permute-start.40) | collective-permute-done | bytes 1441824 | tf_op jit(solution)/shard_map/ppermute | solution.py:439
  320.3 8.5 %all_to_all.71 = bf16[2,512,2048]{2,1,0:T(8,128)(2,1)} all-to-all(bf16[2,512,2048]{2,1,0:T(8,128)(2,1)S(1)} %pad_maximum_fusion.3), channel_id=1, replica_groups=mesh['y'=2,'x'=2,'h'=2,'l'=2,'chip'=2] {'chip'}, dimensions={0} | all-to-all | bytes 8388608 | tf_op jit(solution)/shard_map/all_to_all | solution.py:436
  328.8 29.2 %shard_map.242 = (bf16[1024,704]{1,0:T(8,128)(2,1)}, bf16[1024,1408]{1,0:T(8,128)(2,1)}, bf16[1024,2048]{1,0:T(8,128)(2,1)}, bf16[1024,2048]{1,0:T(8,128)(2,1)}) custom-call(s32[6]{0:T(128)} %stack.286.where, bf16[1024,2048]{1,0:T(8,128)(2,1)} %bitcast.231, bf16[1024,2048]{1,0:T(8,128)(2,1)} %bitcast.83.cotangent.right, bf16[704,2048]{1,0:T(8,128)(2,1)} %bitcast.81.down, ...), custom_call_target="tpu_custom_call" | custom-call | flops 20669530112 | bytes 29753368 | tf_op jit(solution)/shard_map/pallas_call | solution.py:65
  358.0 8.5 %all_to_all.72 = bf16[2,512,2048]{2,1,0:T(8,128)(2,1)S(1)} all-to-all(bf16[2,512,2048]{2,1,0:T(8,128)(2,1)} %bitcast.241), channel_id=1, replica_groups=mesh['y'=2,'x'=2,'h'=2,'l'=2,'chip'=2] {'chip'}, dimensions={0} | all-to-all | bytes 8388608 | tf_op jit(solution)/shard_map/all_to_all | solution.py:436
  378.3 6.5 shard_map.244
  396.7 7.2 %all_to_all.73 = bf16[2,512,2048]{2,1,0:T(8,128)(2,1)S(1)} all-to-all(bf16[2,512,2048]{2,1,0:T(8,128)(2,1)S(1)} %bitcast.239), channel_id=1, replica_groups=mesh['y'=2,'x'=2,'h'=2,'l'=2,'chip'=2] {'chip'}, dimensions={0} | all-to-all | bytes 8388608 | tf_op jit(solution)/shard_map/all_to_all | solution.py:436
  408.3 7.4 %shard_map.246 = bf16[704,2048]{1,0:T(8,128)(2,1)} custom-call(bf16[1024,704]{1,0:T(8,128)(2,1)} %get-tuple-element.259.left, bf16[1024,2048]{1,0:T(8,128)(2,1)} %bitcast.83.cotangent.right), custom_call_target="tpu_custom_call" | custom-call | flops 2952790016 | bytes 8519680 | tf_op jit(solution)/shard_map/pallas_call | solution.py:65
  415.7 6.6 fusion.1
  432.4 8.7 %shard_map.248 = (f32[128,2048]{1,0:T(8,128)}, bf16[128,2048]{1,0:T(8,128)(2,1)}, bf16[4,2,128,256]{3,2,1,0:T(8,128)(2,1)}) custom-call(s32[6]{0:T(128)} %stack.286.where, f32[128,2048]{1,0:T(8,128)} %convert_add_fusion.6.upstream, bf16[128,2048]{1,0:T(8,128)(2,1)} %cotangent.1, f32[128,2048]{1,0:T(8,128)} %get-tuple-element.267.residual, ...), custom_call_target="tpu_custom_call" | custom-call | flops 1073741824 | bytes 14172184 | tf_op jit(solution)/shard_map/pallas_call | solution.py:65
  445.8 6.5 shard_map.247
  452.3 13.0 %collective-permute-done.49 = bf16[2,128,256]{2,1,0:T(8,128)(2,1)S(1)} collective-permute-done((bf16[2,128,256]{2,1,0:T(8,128)(2,1)S(1)}, bf16[2,128,256]{2,1,0:T(8,128)(2,1)S(1)}, u32[]{:S(2)}, u32[]{:S(2)}) %collective-permute-start.49) | collective-permute-done | bytes 131104 | tf_op jit(solution)/shard_map/ppermute | solution.py:429
  503.6 10.4 %shard_map.250 = (bf16[2,2,2,128,256]{4,3,2,1,0:T(8,128)(2,1)}, bf16[2,2,2,128,256]{4,3,2,1,0:T(8,128)(2,1)}, bf16[2,2,2,128,256]{4,3,2,1,0:T(8,128)(2,1)}, f32[2,2,8,128]{3,2,1,0:T(8,128)}) custom-call(s32[6]{0:T(128)} %stack.286.where, f32[2,2,2,128,768]{4,3,2,1,0:T(8,128)} %bitcast.228, f32[2,2,2,128,768]{4,3,2,1,0:T(8,128)} %bitcast.229, ...), custom_call_target="tpu_custom_call" | custom-call | flops 3221225472 | bytes 15500312 | tf_op jit(solution)/shard_map/pallas_call | solution.py:65
  514.0 7.9 %shard_map.251 = bf16[1024,2048]{1,0:T(8,128)(2,1)} custom-call(bf16[1024,256]{1,0:T(8,128)(2,1)} %bitcast.252, bf16[1024,256]{1,0:T(8,128)(2,1)} %bitcast.255, bf16[1024,256]{1,0:T(8,128)(2,1)} %bitcast.258, bf16[32,64,768]{2,1,0:T(8,128)(2,1)} %get-tuple-element.283.weight), custom_call_target="tpu_custom_call" | custom-call | flops 3221225472 | bytes 8912896 | tf_op jit(solution)/shard_map/pallas_call | solution.py:65
  560.7 8.4 %all_to_all.75 = bf16[2,512,2048]{2,1,0:T(8,128)(2,1)} all-to-all(bf16[2,512,2048]{2,1,0:T(8,128)(2,1)S(1)} %pad_maximum_fusion.4), channel_id=1, replica_groups=mesh['y'=2,'x'=2,'h'=2,'l'=2,'chip'=2] {'chip'}, dimensions={0} | all-to-all | bytes 8388608 | tf_op jit(solution)/shard_map/all_to_all | solution.py:436
  573.7 6.2 shard_map.253
  582.1 9.9 %collective-permute-done.62 = bf16[128,2048]{1,0:T(8,128)(2,1)} collective-permute-done((bf16[128,2048]{1,0:T(8,128)(2,1)}, bf16[128,2048]{1,0:T(8,128)(2,1)}, u32[]{:S(2)}, u32[]{:S(2)}) %collective-permute-start.62) | collective-permute-done | bytes 524320 | tf_op jit(solution)/shard_map/ppermute | solution.py:429
  605.4 18.3 %collective-permute-done.70 = bf16[2,64,1408]{2,1,0:T(8,128)(2,1)S(1)} collective-permute-done((bf16[2,64,1408]{2,1,0:T(8,128)(2,1)S(1)}, bf16[2,64,1408]{2,1,0:T(8,128)(2,1)S(1)}, u32[]{:S(2)}, u32[]{:S(2)}) %collective-permute-start.70) | collective-permute-done | bytes 360480 | tf_op jit(solution)/shard_map/ppermute | solution.py:429
  623.7 8.5 %collective-permute-done.68 = bf16[2,64,1408]{2,1,0:T(8,128)(2,1)S(1)} collective-permute-done((bf16[2,64,1408]{2,1,0:T(8,128)(2,1)S(1)}, bf16[2,64,1408]{2,1,0:T(8,128)(2,1)S(1)}, u32[]{:S(2)}, u32[]{:S(2)}) %collective-permute-start.68) | collective-permute-done | bytes 360480 | tf_op jit(solution)/shard_map/ppermute | solution.py:429
  664.4 7.3 %all_to_all.77.blocks = bf16[2,4,64,768]{3,2,1,0:T(8,128)(2,1)} all-to-all(bf16[2,4,64,768]{3,2,1,0:T(8,128)(2,1)S(1)} %pad_maximum_fusion.14), channel_id=1, replica_groups=mesh['y'=2,'x'=2,'h'=2,'l'=2,'chip'=2] {'chip'}, dimensions={0} | all-to-all | bytes 1572864 | tf_op jit(solution)/shard_map/all_to_all | solution.py:436
  678.0 15.0 %collective-permute-done.79 = bf16[176,2048]{1,0:T(8,128)(2,1)S(1)} collective-permute-done((bf16[176,2048]{1,0:T(8,128)(2,1)S(1)}, bf16[176,2048]{1,0:T(8,128)(2,1)S(1)}, u32[]{:S(2)}, u32[]{:S(2)}) %collective-permute-start.79) | collective-permute-done | bytes 720928 | tf_op jit(solution)/shard_map/ppermute | solution.py:439
  (373 shorter events, 326.8 us)
Async XLA Ops:
  32.9 33.3 %collective-permute-start.10 = (bf16[176,2048]{1,0:T(8,128)(2,1)}, bf16[176,2048]{1,0:T(8,128)(2,1)}, u32[]{:S(2)}, u32[]{:S(2)}) collective-permute-start(bf16[176,2048]{1,0:T(8,128)(2,1)} %param.25), channel_id=1, source_target_pairs={{0,4},{4,0},{1,5},{5,1},{2,6},{6,2},{3,7},{7,3},{8,12},{12,8},{9,1... | collective-permute-start | bytes 2162696 | tf_op jit(solution)/shard_map/ppermute | solution.py:439
  67.7 39.4 %collective-permute-start.18 = (bf16[256,2048]{1,0:T(8,128)(2,1)S(1)}, bf16[256,2048]{1,0:T(8,128)(2,1)}, u32[]{:S(2)}, u32[]{:S(2)}) collective-permute-start(bf16[256,2048]{1,0:T(8,128)(2,1)S(1)} %pad_maximum_fusion.10), channel_id=1, source_target_pairs={{0,2},{2,0},{1,3},{3,1},{4,6},{6,4},{5,7},{7,5},{8,10},{10,8},{9,1... | collective-permute-start | bytes 3145736 | tf_op jit(solution)/shard_map/ppermute | solution.py:433
  67.8 44.4 %collective-permute-start.14 = (bf16[8,64,768]{2,1,0:T(8,128)(2,1)}, bf16[8,64,768]{2,1,0:T(8,128)(2,1)}, u32[]{:S(2)}, u32[]{:S(2)}) collective-permute-start(bf16[8,64,768]{2,1,0:T(8,128)(2,1)} %pad_maximum_fusion.13.rest_0_), channel_id=1, source_target_pairs={{0,4},{4,0},{1,5},{5,1},{2,6},{6,2},{3,7},{7,3},{8,12},{12,8},{9,1... | collective-permute-start | bytes 2359304 | tf_op jit(solution)/shard_map/ppermute | solution.py:439
  131.6 32.2 %collective-permute-start.24 = (bf16[4,64,1408]{2,1,0:T(8,128)(2,1)S(1)}, bf16[4,64,1408]{2,1,0:T(8,128)(2,1)S(1)}, u32[]{:S(2)}, u32[]{:S(2)}) collective-permute-start(bf16[4,64,1408]{2,1,0:T(8,128)(2,1)S(1)} %pad_maximum_fusion.15), channel_id=1, source_target_pairs={{0,4},{4,0},{1,5},{5,1},{2,6},{6,2},{3,7},{7,3},{8,12},{12,8},{9,1... | collective-permute-start | bytes 2162696 | tf_op jit(solution)/shard_map/ppermute | solution.py:439
  133.7 31.4 %collective-permute-start.22 = (bf16[8,64,768]{2,1,0:T(8,128)(2,1)}, bf16[8,64,768]{2,1,0:T(8,128)(2,1)}, u32[]{:S(2)}, u32[]{:S(2)}) collective-permute-start(bf16[8,64,768]{2,1,0:T(8,128)(2,1)} %collective-permute-done.14.rest_2_), channel_id=1, source_target_pairs={{0,16},{16,0},{1,17},{17,1},{2,18},{18,2},{3,19},{19,3},{4,20},{20... | collective-permute-start | bytes 2359304 | tf_op jit(solution)/shard_map/ppermute | solution.py:439
  144.6 31.9 %collective-permute-start.23 = (bf16[64,2048]{1,0:T(8,128)(2,1)S(1)}, bf16[64,2048]{1,0:T(8,128)(2,1)S(1)}, u32[]{:S(2)}, u32[]{:S(2)}) collective-permute-start(bf16[64,2048]{1,0:T(8,128)(2,1)S(1)} %copy-done.31), channel_id=1, source_target_pairs={{0,16},{16,0},{1,17},{17,1},{2,18},{18,2},{3,19},{19,3},{4,20},{20... | collective-permute-start | bytes 786440 | tf_op jit(solution)/shard_map/ppermute | solution.py:439
  180.9 54.7 %collective-permute-start.25 = (bf16[2,176,2048]{2,1,0:T(8,128)(2,1)S(1)}, bf16[2,176,2048]{2,1,0:T(8,128)(2,1)}, u32[]{:S(2)}, u32[]{:S(2)}) collective-permute-start(bf16[2,176,2048]{2,1,0:T(8,128)(2,1)S(1)} %pad_maximum_fusion.6), channel_id=1, source_target_pairs={{0,16},{16,0},{1,17},{17,1},{2,18},{18,2},{3,19},{19,3},{4,20},{20... | collective-permute-start | bytes 4325384 | tf_op jit(solution)/shard_map/ppermute | solution.py:439
  192.1 40.0 %collective-permute-start.29 = (bf16[2,2,64,2048]{3,2,1,0:T(8,128)(2,1)S(1)}, bf16[2,2,64,2048]{3,2,1,0:T(8,128)(2,1)}, u32[]{:S(2)}, u32[]{:S(2)}) collective-permute-start(bf16[2,2,64,2048]{3,2,1,0:T(8,128)(2,1)S(1)} %get-tuple-element.351), channel_id=1, source_target_pairs={{0,2},{2,0},{1,3},{3,1},{4,6},{6,4},{5,7},{7,5},{8,10},{10,8},{9,1... | collective-permute-start | bytes 3145736 | tf_op jit(solution)/shard_map/ppermute | solution.py:433
  193.2 38.9 %collective-permute-start.27 = (bf16[2,2,64,2048]{3,2,1,0:T(8,128)(2,1)S(1)}, bf16[2,2,64,2048]{3,2,1,0:T(8,128)(2,1)}, u32[]{:S(2)}, u32[]{:S(2)}) collective-permute-start(bf16[2,2,64,2048]{3,2,1,0:T(8,128)(2,1)S(1)} %get-tuple-element.349), channel_id=1, source_target_pairs={{0,8},{8,0},{1,9},{9,1},{2,10},{10,2},{3,11},{11,3},{4,12},{12,4},... | collective-permute-start | bytes 3145736 | tf_op jit(solution)/shard_map/ppermute | solution.py:433
  195.4 34.4 %collective-permute-start.30 = (bf16[4,64,1408]{2,1,0:T(8,128)(2,1)S(1)}, bf16[4,64,1408]{2,1,0:T(8,128)(2,1)}, u32[]{:S(2)}, u32[]{:S(2)}) collective-permute-start(bf16[4,64,1408]{2,1,0:T(8,128)(2,1)S(1)} %copy-done.16), channel_id=1, source_target_pairs={{0,4},{4,0},{1,5},{5,1},{2,6},{6,2},{3,7},{7,3},{8,12},{12,8},{9,1... | collective-permute-start | bytes 2162696 | tf_op jit(solution)/shard_map/ppermute | solution.py:439
  235.7 34.6 %collective-permute-start.36 = (bf16[4,2,2,64,2048]{4,3,2,1,0:T(8,128)(2,1)}, bf16[4,2,2,64,2048]{4,3,2,1,0:T(8,128)(2,1)}, u32[]{:S(2)}, u32[]{:S(2)}) collective-permute-start(bf16[4,2,2,64,2048]{4,3,2,1,0:T(8,128)(2,1)} %pad_maximum_fusion.1.rest_4_), channel_id=1, source_target_pairs={{0,1},{1,0},{2,3},{3,2},{4,5},{5,4},{6,7},{7,6},{8,9},{9,8},{10,11... | collective-permute-start | bytes 12582920 | tf_op jit(solution)/shard_map/ppermute | solution.py:614
  235.7 34.5 %collective-permute-start.35 = (bf16[2,4,64,1408]{3,2,1,0:T(8,128)(2,1)}, bf16[2,4,64,1408]{3,2,1,0:T(8,128)(2,1)}, u32[]{:S(2)}, u32[]{:S(2)}) collective-permute-start(bf16[2,4,64,1408]{3,2,1,0:T(8,128)(2,1)} %pad_maximum_fusion.5.rest_0_), channel_id=1, source_target_pairs={{0,16},{16,0},{1,17},{17,1},{2,18},{18,2},{3,19},{19,3},{4,20},{20... | collective-permute-start | bytes 4325384 | tf_op jit(solution)/shard_map/ppermute | solution.py:439
  264.5 29.7 %all-to-all-start.4 = ((bf16[2,512,2048]{2,1,0:T(8,128)(2,1)}), bf16[2,512,2048]{2,1,0:T(8,128)(2,1)}, u32[]{:S(2)}, u32[]{:S(2)}) async-start(bf16[2,512,2048]{2,1,0:T(8,128)(2,1)} %pad_maximum_fusion.2), calls=%async_computation.4 | async-start | bytes 8388608 | tf_op jit(solution)/shard_map/all_to_all | solution.py:436
  284.9 33.5 %collective-permute-start.40 = (bf16[2,4,64,1408]{3,2,1,0:T(8,128)(2,1)S(1)}, bf16[2,4,64,1408]{3,2,1,0:T(8,128)(2,1)}, u32[]{:S(2)}, u32[]{:S(2)}) collective-permute-start(bf16[2,4,64,1408]{3,2,1,0:T(8,128)(2,1)S(1)} %copy-done.20), channel_id=1, source_target_pairs={{0,16},{16,0},{1,17},{17,1},{2,18},{18,2},{3,19},{19,3},{4,20},{20... | collective-permute-start | bytes 4325384 | tf_op jit(solution)/shard_map/ppermute | solution.py:439
  390.9 33.9 %collective-permute-start.44 = (bf16[2,1,256,1408]{3,2,1,0:T(8,128)(2,1)S(1)}, bf16[2,1,256,1408]{3,2,1,0:T(8,128)(2,1)S(1)}, u32[]{:S(2)}, u32[]{:S(2)}) collective-permute-start(bf16[2,1,256,1408]{3,2,1,0:T(8,128)(2,1)S(1)} %copy-done.21), channel_id=1, source_target_pairs={{0,16},{16,0},{1,17},{17,1},{2,18},{18,2},{3,19},{19,3},{4,20},{20... | collective-permute-start | bytes 4325384 | tf_op jit(solution)/shard_map/ppermute | solution.py:439
  393.2 29.1 %collective-permute-start.47 = (bf16[128,2048]{1,0:T(8,128)(2,1)}, bf16[128,2048]{1,0:T(8,128)(2,1)S(1)}, u32[]{:S(2)}, u32[]{:S(2)}) collective-permute-start(bf16[128,2048]{1,0:T(8,128)(2,1)} %get-tuple-element.340), channel_id=1, source_target_pairs={{0,10},{2,8},{8,2},{10,0},{1,11},{3,9},{9,3},{11,1},{4,14},{6,12},... | collective-permute-start | bytes 1572872 | tf_op jit(solution)/shard_map/ppermute | solution.py:429
  425.2 58.6 %collective-permute-start.48 = (bf16[2,1,256,1408]{3,2,1,0:T(8,128)(2,1)}, bf16[2,1,256,1408]{3,2,1,0:T(8,128)(2,1)}, u32[]{:S(2)}, u32[]{:S(2)}) collective-permute-start(bf16[2,1,256,1408]{3,2,1,0:T(8,128)(2,1)} %shard_map.245), channel_id=1, source_target_pairs={{0,16},{16,0},{1,17},{17,1},{2,18},{18,2},{3,19},{19,3},{4,20},{20... | collective-permute-start | bytes 4325384 | tf_op jit(solution)/shard_map/ppermute | solution.py:439
  427.9 53.4 %collective-permute-start.55 = (bf16[1,256,1408]{2,1,0:T(8,128)(2,1)}, bf16[1,256,1408]{2,1,0:T(8,128)(2,1)}, u32[]{:S(2)}, u32[]{:S(2)}) collective-permute-start(bf16[1,256,1408]{2,1,0:T(8,128)(2,1)} %fusion.9), channel_id=1, source_target_pairs={{0,4},{4,0},{1,5},{5,1},{2,6},{6,2},{3,7},{7,3},{8,12},{12,8},{9,1... | collective-permute-start | bytes 2162696 | tf_op jit(solution)/shard_map/ppermute | solution.py:439
  494.3 50.9 %collective-permute-start.57 = (bf16[2,176,2048]{2,1,0:T(8,128)(2,1)S(1)}, bf16[2,176,2048]{2,1,0:T(8,128)(2,1)}, u32[]{:S(2)}, u32[]{:S(2)}) collective-permute-start(bf16[2,176,2048]{2,1,0:T(8,128)(2,1)S(1)} %dynamic-slice_bitcast_fusion), channel_id=1, source_target_pairs={{0,16},{16,0},{1,17},{17,1},{2,18},{18,2},{3,19},{19,3},{4,20},{20... | collective-permute-start | bytes 4325384 | tf_op jit(solution)/shard_map/ppermute | solution.py:439
  499.5 42.9 %collective-permute-start.60 = (bf16[128,2048]{1,0:T(8,128)(2,1)}, bf16[128,2048]{1,0:T(8,128)(2,1)S(1)}, u32[]{:S(2)}, u32[]{:S(2)}) collective-permute-start(bf16[128,2048]{1,0:T(8,128)(2,1)} %get-tuple-element.337), channel_id=1, source_target_pairs={{0,10},{2,8},{8,2},{10,0},{1,11},{3,9},{9,3},{11,1},{4,14},{6,12},... | collective-permute-start | bytes 1572872 | tf_op jit(solution)/shard_map/ppermute | solution.py:429
  501.2 41.1 %collective-permute-start.59 = (bf16[128,2048]{1,0:T(8,128)(2,1)}, bf16[128,2048]{1,0:T(8,128)(2,1)S(1)}, u32[]{:S(2)}, u32[]{:S(2)}) collective-permute-start(bf16[128,2048]{1,0:T(8,128)(2,1)} %get-tuple-element.338), channel_id=1, source_target_pairs={{0,8},{2,10},{8,0},{10,2},{1,9},{3,11},{9,1},{11,3},{4,12},{6,14},... | collective-permute-start | bytes 1572872 | tf_op jit(solution)/shard_map/ppermute | solution.py:429
  502.5 39.9 %collective-permute-start.58 = (bf16[128,2048]{1,0:T(8,128)(2,1)S(1)}, bf16[128,2048]{1,0:T(8,128)(2,1)}, u32[]{:S(2)}, u32[]{:S(2)}) collective-permute-start(bf16[128,2048]{1,0:T(8,128)(2,1)S(1)} %get-tuple-element.336), channel_id=1, source_target_pairs={{0,2},{2,0},{8,10},{10,8},{1,3},{3,1},{9,11},{11,9},{4,6},{6,4},{1... | collective-permute-start | bytes 1572872 | tf_op jit(solution)/shard_map/ppermute | solution.py:429
  548.7 44.9 %collective-permute-start.61 = (bf16[2,2,256,768]{3,2,1,0:T(8,128)(2,1)}, bf16[2,2,256,768]{3,2,1,0:T(8,128)(2,1)}, u32[]{:S(2)}, u32[]{:S(2)}) collective-permute-start(bf16[2,2,256,768]{3,2,1,0:T(8,128)(2,1)} %shard_map.252), channel_id=1, source_target_pairs={{0,16},{16,0},{1,17},{17,1},{2,18},{18,2},{3,19},{19,3},{4,20},{20... | collective-permute-start | bytes 4718600 | tf_op jit(solution)/shard_map/ppermute | solution.py:439
  550.7 31.4 %collective-permute-start.64 = (bf16[128,2048]{1,0:T(8,128)(2,1)}, bf16[128,2048]{1,0:T(8,128)(2,1)S(1)}, u32[]{:S(2)}, u32[]{:S(2)}) collective-permute-start(bf16[128,2048]{1,0:T(8,128)(2,1)} %get-tuple-element.334), channel_id=1, source_target_pairs={{0,10},{2,8},{8,2},{10,0},{1,11},{3,9},{9,3},{11,1},{4,14},{6,12},... | collective-permute-start | bytes 1572872 | tf_op jit(solution)/shard_map/ppermute | solution.py:429
  552.4 29.7 %collective-permute-start.63 = (bf16[128,2048]{1,0:T(8,128)(2,1)}, bf16[128,2048]{1,0:T(8,128)(2,1)}, u32[]{:S(2)}, u32[]{:S(2)}) collective-permute-start(bf16[128,2048]{1,0:T(8,128)(2,1)} %get-tuple-element.335), channel_id=1, source_target_pairs={{0,8},{2,10},{8,0},{10,2},{1,9},{3,11},{9,1},{11,3},{4,12},{6,14},... | collective-permute-start | bytes 1572872 | tf_op jit(solution)/shard_map/ppermute | solution.py:429
  553.6 38.4 %collective-permute-start.62 = (bf16[128,2048]{1,0:T(8,128)(2,1)}, bf16[128,2048]{1,0:T(8,128)(2,1)}, u32[]{:S(2)}, u32[]{:S(2)}) collective-permute-start(bf16[128,2048]{1,0:T(8,128)(2,1)} %get-tuple-element.333), channel_id=1, source_target_pairs={{0,2},{2,0},{8,10},{10,8},{1,3},{3,1},{9,11},{11,9},{4,6},{6,4},{1... | collective-permute-start | bytes 1572872 | tf_op jit(solution)/shard_map/ppermute | solution.py:429
  555.1 38.4 %collective-permute-start.65 = (bf16[1,256,1408]{2,1,0:T(8,128)(2,1)}, bf16[1,256,1408]{2,1,0:T(8,128)(2,1)S(1)}, u32[]{:S(2)}, u32[]{:S(2)}) collective-permute-start(bf16[1,256,1408]{2,1,0:T(8,128)(2,1)} %fusion.10), channel_id=1, source_target_pairs={{0,4},{4,0},{1,5},{5,1},{2,6},{6,2},{3,7},{7,3},{8,12},{12,8},{9,1... | collective-permute-start | bytes 2162696 | tf_op jit(solution)/shard_map/ppermute | solution.py:439
  595.6 37.0 %collective-permute-start.66 = (bf16[2,256,768]{2,1,0:T(8,128)(2,1)S(1)}, bf16[2,256,768]{2,1,0:T(8,128)(2,1)S(1)}, u32[]{:S(2)}, u32[]{:S(2)}) collective-permute-start(bf16[2,256,768]{2,1,0:T(8,128)(2,1)S(1)} %fusion.8), channel_id=1, source_target_pairs={{0,4},{4,0},{1,5},{5,1},{2,6},{6,2},{3,7},{7,3},{8,12},{12,8},{9,1... | collective-permute-start | bytes 2359304 | tf_op jit(solution)/shard_map/ppermute | solution.py:439
  598.0 34.4 %collective-permute-start.67 = (bf16[2,64,2048]{2,1,0:T(8,128)(2,1)S(1)}, bf16[2,64,2048]{2,1,0:T(8,128)(2,1)S(1)}, u32[]{:S(2)}, u32[]{:S(2)}) collective-permute-start(bf16[2,64,2048]{2,1,0:T(8,128)(2,1)S(1)} %dynamic-slice_bitcast_fusion.1), channel_id=1, source_target_pairs={{0,16},{16,0},{1,17},{17,1},{2,18},{18,2},{3,19},{19,3},{4,20},{20... | collective-permute-start | bytes 1572872 | tf_op jit(solution)/shard_map/ppermute | solution.py:439
  633.7 29.5 %collective-permute-start.74 = (bf16[2,64,768]{2,1,0:T(8,128)(2,1)}, bf16[2,64,768]{2,1,0:T(8,128)(2,1)S(1)}, u32[]{:S(2)}, u32[]{:S(2)}) collective-permute-start(bf16[2,64,768]{2,1,0:T(8,128)(2,1)} %get-tuple-element.381), channel_id=1, source_target_pairs={{0,10},{2,8},{8,2},{10,0},{1,11},{3,9},{9,3},{11,1},{4,14},{6,12},... | collective-permute-start | bytes 589832 | tf_op jit(solution)/shard_map/ppermute | solution.py:429
  634.0 29.2 %collective-permute-start.73 = (bf16[2,64,768]{2,1,0:T(8,128)(2,1)}, bf16[2,64,768]{2,1,0:T(8,128)(2,1)}, u32[]{:S(2)}, u32[]{:S(2)}) collective-permute-start(bf16[2,64,768]{2,1,0:T(8,128)(2,1)} %get-tuple-element.380), channel_id=1, source_target_pairs={{0,8},{2,10},{8,0},{10,2},{1,9},{3,11},{9,1},{11,3},{4,12},{6,14},... | collective-permute-start | bytes 589832 | tf_op jit(solution)/shard_map/ppermute | solution.py:429
  655.4 37.6 %collective-permute-start.79 = (bf16[176,2048]{1,0:T(8,128)(2,1)S(1)}, bf16[176,2048]{1,0:T(8,128)(2,1)S(1)}, u32[]{:S(2)}, u32[]{:S(2)}) collective-permute-start(bf16[176,2048]{1,0:T(8,128)(2,1)S(1)} %fusion.11), channel_id=1, source_target_pairs={{0,4},{4,0},{1,5},{5,1},{2,6},{6,2},{3,7},{7,3},{8,12},{12,8},{9,1... | collective-permute-start | bytes 2162696 | tf_op jit(solution)/shard_map/ppermute | solution.py:439
  (95 other events, 1261.1 us)

commit v3 on v2

--- a/solution.py
+++ b/solution.py
@@ -70,7 +70,7 @@
         out_specs=out_specs,
         scratch_shapes=list(scratch),
         compiler_params=pltpu.CompilerParams(vmem_limit_bytes=LIMIT),
-        cost_estimate=pl.CostEstimate(flops=int(flops), bytes_accessed=int(moved), transcendentals=0),
+        cost_estimate=pl.CostEstimate(flops=int(flops) // 8, bytes_accessed=int(moved) // 8, transcendentals=0),
     )(*args)
 
 
@@ -449,13 +449,12 @@
         return to_cores(jnp.stack([mine, mine])).reshape(nc * mine.shape[0], -1)
 
     def summed_core(x):
-        x = to_cores(x.reshape(nc, half, -1)).astype(F32)
-        return x[0] + x[1]
-
-    def summed_plane(both):
-        both = both.reshape(plane, rows, -1)
-        sent = both[1:].astype(LOW)
-        got = from_plane([both[0]] + [sent[k] for k in range(plane - 1)])
+        x = to_cores(x.reshape(nc, plane, rows, -1))
+        sums = [x[0, k].astype(F32) + x[1, k].astype(F32) for k in range(plane)]
+        return [sums[0]] + [z.astype(LOW) for z in sums[1:]]
+
+    def summed_plane(sums):
+        got = from_plane(sums)
         return sum((z.astype(F32) for z in got[1:]), got[0])
 
     def at_plane(x, axis):
@@ -494,35 +493,31 @@
     small_mine = jnp.concatenate(from_plane([small] * plane))
     small_other = lax.ppermute(small_mine, "chip", [(i, i ^ 1) for i in range(nc)])
     plane_small = jnp.concatenate([pick(c == 0, small_mine, small_other), pick(c == 0, small_other, small_mine)])
-    vectors = jnp.concatenate(
-        [z for x in turns(plane_small[:, : 4 * r], "h", nh) for z in turns(x, "y", ny)]
-    )
     spread = lambda w: w.reshape(r, plane, nc, part)
     three = jnp.concatenate([spread(w_forget), spread(w_input), spread(w_query)], axis=3).transpose(2, 1, 0, 3)
     three = jnp.concatenate(from_plane(at_plane(to_cores(three), 1)))
-    down_line = turns(after(w_down, vectors), "h", nh)
+    out_line = turns(w_output, "h", nh)
     out_first = turns(w_output, "y", ny)
-    tokens_pair = jnp.concatenate([tokens, swap(after(tokens, three), "l")])
-    cotangent_x = swap(after(cotangent, three), "x")
+    tokens_pair = jnp.concatenate([tokens, swap(tokens, "l")])
+    vectors = jnp.stack(turns(plane_small[:, : 4 * r], "y", ny))
+    vectors = jnp.concatenate(turns(vectors, "h", nh)).reshape(plan.devices, -1)
     (packed,) = call(partial(pack_kernel, plan, ffr), [shape((nc, plane, r, 2 * units), LOW)], w_gate, w_up)
-    packed = to_cores(packed)
-    plane_small, vectors, three, down_line, out_first, tokens_pair, cotangent_x, packed, w_output = fence(
-        plane_small, vectors, three, down_line, out_first, tokens_pair, cotangent_x, packed, w_output
+    packed = to_cores(after(packed, out_line))
+    plane_small, three, out_line, out_first, tokens_pair, packed, vectors, cotangent, w_down = fence(
+        plane_small, three, out_line, out_first, tokens_pair, packed, vectors, cotangent, w_down
     )
 
     three_line = turns(three, "h", nh)
     three_first = turns(three, "y", ny)
-    out_line = turns(after(w_output, three_line), "h", nh)
+    out_copies = out_first + [z for x in out_line[1:] for z in turns(after(x, three_first), "y", ny)]
     tokens_far = swap(tokens_pair, "x")
-    cotangent_l = swap(jnp.concatenate([cotangent, cotangent_x]), "l")
-    gate_up = from_plane(after(at_plane(packed, 1), tokens_far, cotangent_l))
+    gate_up = from_plane(at_plane(packed, 1))
     gate_up = [jnp.concatenate(gate_up[:nl]), jnp.concatenate(gate_up[nl:])]
-    three_line, three_first, out_line, tokens_pair, tokens_far, cotangent_l, gate_up, down_line = fence(
-        three_line, three_first, out_line, tokens_pair, tokens_far, cotangent_l, gate_up, down_line
+    three_line, three_first, out_copies, tokens_pair, tokens_far, gate_up, cotangent, w_down = fence(
+        three_line, three_first, out_copies, tokens_pair, tokens_far, gate_up, cotangent, w_down
     )
 
     three = three_first + [z for x in three_line[1:] for z in turns(x, "y", ny)]
-    out_copies = out_first + [z for x in out_line[1:] for z in turns(x, "y", ny)]
     gu_first = jnp.stack(turns(gate_up[0], "h", nh))
     plane_tokens = over_plane([tokens_pair, tokens_far])
     plane_starts = (
@@ -532,7 +527,7 @@
     starts_wide = jnp.broadcast_to(plane_starts[:, :, None], (nx, span, HDIM)).astype(LOW)
     places = jnp.stack([
         plan.owner((y - j) % ny, here ^ k, (h - i) % nh, e)
-        for i, j in names for e in range(nc) for k in range(plane)
+        for i in range(nh) for j in range(ny) for e in range(nc) for k in range(plane)
     ])
     ordered = (jnp.arange(plan.devices)[:, None] == places[None, :]).astype(F32)
     vectors = jnp.dot(ordered, vectors, precision=lax.Precision.HIGHEST)
@@ -550,8 +545,12 @@
         scratch=[pltpu.SemaphoreType.DMA((count,))],
         flops=project_flops,
     )
-    down_line, gate_up, pre, out_copies, lower, starts_wide, starts_row, gu_first = fence(
-        down_line, gate_up, pre, out_copies, lower, starts_wide, starts_row, gu_first
+    cut = copies // 2
+    pieces = [jnp.stack(out_copies[:cut]), jnp.stack(out_copies[cut:])]
+    moved = [swap(z, axis) for z, axis in zip(pieces, ("l", "x"))]
+    cotangent_pair = jnp.concatenate([cotangent, swap(after(cotangent, moved), "l")])
+    gate_up, pre, pieces, moved, lower, starts_wide, starts_row, gu_first, cotangent_pair, w_down = fence(
+        gate_up, pre, pieces, moved, lower, starts_wide, starts_row, gu_first, cotangent_pair, w_down
     )
 
     by_group = lambda x: x.reshape(nc, nx, nl, rows, -1)
@@ -578,11 +577,8 @@
         out_specs=[state_spec, state_spec, rows_spec, rows_spec, rows_spec, scores_spec],
         flops=8 * mix_flops,
     )
-    down_blocks = turns(jnp.stack(down_line), "y", ny)
+    gu_first = turns(gu_first, "y", ny)
     gu_second = jnp.stack(turns(gate_up[1], "h", nh))
-    cut = copies // 2
-    pieces = [jnp.stack(out_copies[:cut]), jnp.stack(out_copies[cut:])]
-    moved = [swap(z, axis) for z, axis in zip(pieces, ("l", "x"))]
     pairs = [jnp.stack([a, z]) for a, z in zip(pieces, moved)]
     moved = [swap(z, axis) for z, axis in zip(pairs, ("x", "l"))]
     groups = jnp.stack([pairs[0], moved[0], pairs[1], moved[1]])
@@ -590,8 +586,8 @@
         (t * 2 + distance, u, m, *names[t * cut + m], u * nl + distance if t else distance * nl + u)
         for t in range(2) for distance in range(2) for u in range(2) for m in range(cut)
     ]
-    end_state, decay, local, query_reach, down_blocks, gu_first, groups, gu_second = fence(
-        end_state, decay, local, query_reach, down_blocks, gu_first, groups, gu_second
+    end_state, decay, local, query_reach, gu_first, groups, gu_second, cotangent_pair, w_down = fence(
+        end_state, decay, local, query_reach, gu_first, groups, gu_second, cotangent_pair, w_down
     )
 
     def carry(block, step):
@@ -609,11 +605,14 @@
         grid=(nx, heads), specs=[rows_spec, rows_spec, state_spec], out_specs=[piece(0)], flops=mix_flops // 4,
     )
     mixed = to_cores(mixed.reshape(nc, plane, rows, part))
-    mixed_in = from_plane([mixed[:, k] for k in range(plane)])
-    gu_first = turns(gu_first, "y", ny)
+    down_line = turns(after(w_down, incoming), "h", nh)
+    mixed_in = from_plane(after([mixed[:, k] for k in range(plane)], down_line))
+    gate_up = gu_first + turns(gu_second, "y", ny)
+    cotangent_far = swap(cotangent_pair, "x")
     groups_other = lax.ppermute(groups, "chip", [(i, i ^ 1) for i in range(nc)])
-    mixed_in, gu_first, groups, groups_other, down_blocks, gu_second = fence(
-        mixed_in, gu_first, groups, groups_other, down_blocks, gu_second
+    plane_cotangent = over_plane([cotangent_pair, cotangent_far])
+    mixed_in, gate_up, groups, groups_other, plane_cotangent, down_line = fence(
+        mixed_in, gate_up, groups, groups_other, plane_cotangent, down_line
     )
 
     parts_shape = (plane, nc, rows, part)
@@ -627,10 +626,8 @@
         flops=2 * rows * width * width,
     )
     ffn_pieces = from_plane([normed_ffn] * plane)
-    gate_up = gu_first + turns(gu_second, "y", ny)
-    plane_cotangent = over_plane([cotangent, cotangent_l[:rows], cotangent_x, cotangent_l[rows:]])
     down = jnp.zeros((ny, nh, ffr, width), LOW)
-    for j, blocks in enumerate(down_blocks):
+    for j, blocks in enumerate(turns(jnp.stack(down_line), "y", ny)):
         for i in range(nh):
             down = lax.dynamic_update_slice(down, blocks[i][None, None], ((y - j) % ny, (h - i) % nh, 0, 0))
     down = down.reshape(units, width)
@@ -653,7 +650,6 @@
         scratch=[pltpu.VMEM((count, r, 2 * units), LOW), pltpu.SemaphoreType.DMA((count,))],
         flops=2 * total * width * units * 7,
     )
-    mix_parts = to_parts(normed_parts)
     lcr = nl * nc * r
 
     def columns_grad(turns, dtype, sides, normed, grads):
@@ -669,6 +665,7 @@
 
     both_ffn = summed_core(part_ffn)
     far_sent = columns_grad(1, LOW, (1,), plane_ffn, [grad_gu])
+    mix_parts = to_parts(after(normed_parts, plane_ffn))
     both_ffn, far_sent, plane_ffn, grad_gu, hidden, mix_parts, plane_cotangent, part_out = fence(
         both_ffn, far_sent, plane_ffn, grad_gu, hidden, mix_parts, plane_cotangent, part_out
     )
@@ -679,7 +676,7 @@
     (grad_down,) = call(
         rows_grad_kernel, [shape((units, width), LOW)], hidden, plane_cotangent, flops=2 * total * units * width,
     )
-    both_out = summed_core(after(part_out, near_sent))
+    both_out = summed_core(after(part_out, grad_down))
     grad_gu_far, grad_normed_ffn, near_sent, grad_down, plane_ffn, grad_gu, both_out = fence(
         grad_gu_far, grad_normed_ffn, near_sent, grad_down, plane_ffn, grad_gu, both_out
     )
@@ -694,20 +691,20 @@
         flops=2 * rows * width * width,
     )
     grads = to_parts(grad_parts)
-    branch_pieces = from_plane([after(branch, grads)] * plane)
-    grad_gu_far = scatter_h(grad_gu_far)
+    grad_gu_far = scatter_h(after(grad_gu_far, grads))
+    output = (residual + summed_plane(after(both_out, grads))).astype(LOW)
     grads = by_group(to_cores(grads))
     (state_grad,) = call(
         mix_state_grad_kernel, [shape(states)], query_reach, grads,
         grid=(nx, heads), specs=[rows_spec, piece(0)], out_specs=[state_spec], flops=mix_flops // 4,
     )
-    mix_parts = to_cores(mix_parts)
-    grad_gu_near, state_grad, grads, branch_pieces, grad_gu_far, grad_down, both_out, mix_parts = fence(
-        grad_gu_near, state_grad, grads, branch_pieces, grad_gu_far, grad_down, both_out, mix_parts
+    grad_gu_near, state_grad, grads, branch, grad_gu_far, output, grad_down = fence(
+        grad_gu_near, state_grad, grads, branch, grad_gu_far, output, grad_down
     )
 
     next_grad = carry(state_grad, -1)
-    output = (residual + summed_plane(both_out)).astype(LOW)
+    grad_gu_near = scatter_h(after(grad_gu_near, next_grad))
+    branch_pieces = from_plane([branch] * plane)
     grad_down = scatter_y(*rows_of_y(grad_down.reshape(ny, nh, ffr, width)))
     df, dv, dq, lower_grad = call(
         mix_back_kernel,
@@ -724,20 +721,20 @@
         inputs_grad_kernel, [shape((total, width), LOW)], *pre_grads, w_three, flops=project_flops
     )
     both_in = summed_core(part_in)
-    three_sent = columns_grad(1, LOW, (0, 1), normed_in, pre_grads)
-    both_in, three_sent, pre_grads, branch_pieces, grad_down, grad_gu_near, output = fence(
-        both_in, three_sent, pre_grads, branch_pieces, grad_down, grad_gu_near, output
+    three_sent = columns_grad(1, LOW, (0, 1), normed_in, after(pre_grads, grad_gu_near))
+    both_in, three_sent, pre_grads, branch_pieces, grad_gu_near, grad_gu_far, grad_down = fence(
+        both_in, three_sent, pre_grads, branch_pieces, grad_gu_near, grad_gu_far, grad_down
     )
 
     grad_normed_in = summed_plane(both_in)
     grad_three = scatter_y(three_sent, columns_kept((0, 1), normed_in, pre_grads))
-    grad_gu_near = scatter_h(grad_gu_near)
+    grad_down = scatter_h(grad_down)
     (grad_out,) = call(
-        rows_grad_kernel, [shape((part, width), LOW)], mix_parts.reshape(total, part), over_plane(branch_pieces),
+        rows_grad_kernel, [shape((part, width), LOW)], to_cores(mix_parts).reshape(total, part), over_plane(branch_pieces),
         flops=2 * total * part * width,
     )
-    grad_three, grad_normed_in, grad_gu_near, grad_out, grad_down, grad_gu_far = fence(
-        grad_three, grad_normed_in, grad_gu_near, grad_out, grad_down, grad_gu_far
+    grad_three, grad_normed_in, grad_gu_near, grad_out, grad_gu_far, grad_down = fence(
+        grad_three, grad_normed_in, grad_gu_near, grad_out, grad_gu_far, grad_down
     )
 
     own_tokens = tokens.astype(F32)
@@ -746,15 +743,14 @@
     grad_output = scatter_y(*rows_of_y(grad_out.reshape(ny, nh, r, width)))
     gu_blocks = collect([z.astype(LOW).reshape(nl, nc, r, 2 * units) for z in (grad_gu_near, grad_gu_far)])
     lower_grad = jnp.sum(lower_grad[:, :, 0], axis=0).reshape(1, part)
-    lower_grad = sum(turns(lower_grad, "y", ny))
-    grad_three, grad_output, gu_blocks, lower_grad, grad_down = fence(
-        grad_three, grad_output, gu_blocks, lower_grad, grad_down
+    lower_grad = sum(turns(after(lower_grad, grad_output), "y", ny))
+    grad_three, grad_output, gu_blocks, lower_grad = fence(
+        grad_three, grad_output, gu_blocks, lower_grad
     )
 
     three_blocks = collect([grad_three[t] for t in range(nx)])
     grad_output = scatter_h(grad_output)
-    lower_grad = sum(turns(lower_grad, "h", nh))
-    grad_down = scatter_h(after(grad_down, lower_grad))
+    lower_grad = sum(turns(after(lower_grad, grad_output), "h", nh))
     owners = []
     for j in range(ny):
         for p in range(nx):

time: 709 us -> 674 us (0.951)
  local copies, waits for them, and re-layouts: 38.7 us -> 26 us
  blocking collectives: 55.9 us -> 44.4 us
  other arithmetic: 77.5 us -> 66.8 us
    ppermute x8, waiting for transfers between devices: 57.2 us -> 14.2 us  [swap(): return lax.ppermute(x, axis, [(0, 1), (1, 0)])]
    ppermute x27 -> x26, waiting for transfers between devices: 80 us -> 106 us  [turn(): return lax.ppermute(x, axis, [(i, (i + 1) % n) for i in range(n)])]
    all_to_all x8 -> x6, blocking collectives: 55.9 us -> 44.4 us  [to_cores(): return lax.all_to_all(x, 'chip', 0, 0, tiled=True)]
    all_to_all x6 -> x8, starting transfers between devices: 28.1 us -> 37.7 us  [to_cores(): return lax.all_to_all(x, 'chip', 0, 0, tiled=True)]
    add x5 -> x2, other arithmetic: 9.35 us -> 0.02 us  [the longest x1 0.02 us: body(): lower_grad = sum(turns(after(lower_grad, grad_output), 'h', nh))]
    ppermute x1, waiting for transfers between devices: 0.01 us -> 7.64 us  [body(): lower_grad = lax.ppermute(lower_grad, AXES, pairs)]
    ppermute x27 -> x26, starting transfers between devices: 39.1 us -> 34.6 us  [turn(): return lax.ppermute(x, axis, [(i, (i + 1) % n) for i in range(n)])]
  transfers between devices with their start and end apart: 86 -> 87, of which waited for: 25 -> 34; matrix products, arithmetic and copies ran while one was open for 14% -> 11% of each run, Pallas kernels for 16% -> 22%
where the time goes in v3:
time: 674 us; the launch traced here: 667 us
  waiting for transfers between devices  234 us (35%)
  Pallas kernels  154 us (23%)
  starting transfers between devices  139 us (21%)
  other arithmetic  66.8 us (10%)
  blocking collectives  44.4 us (7%)
  local copies, waits for them, and re-layouts  26 us (4%)
    pallas_call x20, Pallas kernels, call(): pl.pallas_call(kernel, out_shape=outs, grid=grid, in_specs=specs, out_spe...  154 us
    ppermute x26, waiting for transfers between devices, turn(): return lax.ppermute(x, axis, [(i, (i + 1) % n) for i in range(n)])  106 us
    ppermute x39, waiting for transfers between devices, from_plane(): lax.ppermute(blocks[k], ('x', 'l'), [(i, i ^ k) for i in range(plane)])  87.7 us
    ppermute x39, starting transfers between devices, from_plane(): lax.ppermute(blocks[k], ('x', 'l'), [(i, i ^ k) for i in range(plane)])  48.5 us
    all_to_all x6, blocking collectives, to_cores(): return lax.all_to_all(x, 'chip', 0, 0, tiled=True)  44.4 us
    all_to_all x8, starting transfers between devices, to_cores(): return lax.all_to_all(x, 'chip', 0, 0, tiled=True)  37.7 us
    ppermute x26, starting transfers between devices, turn(): return lax.ppermute(x, axis, [(i, (i + 1) % n) for i in range(n)])  34.6 us
    ppermute x8, waiting for transfers between devices, swap(): return lax.ppermute(x, axis, [(0, 1), (1, 0)])  14.2 us
  transfers between devices with their start and end apart: 87, of which 34 were waited for; matrix products, arithmetic and copies ran while one was open for 11% of the time, Pallas kernels for 22%

profile of v3, /device:TPU:2, one launch (start us, length us, event | category | flops | bytes accessed | tf_op | source)
XLA Modules:
  0.0 667.0 jit_solution(18422288488238370314)
XLA Ops:
  35.9 8.4 %collective-permute-done.6 = bf16[2,64,768]{2,1,0:T(8,128)(2,1)S(1)} collective-permute-done((bf16[2,64,768]{2,1,0:T(8,128)(2,1)S(1)}, bf16[2,64,768]{2,1,0:T(8,128)(2,1)S(1)}, u32[]{:S(2)}, u32[]{:S(2)}) %collective-permute-start.6) | collective-permute-done | bytes 196640 | tf_op jit(solution)/shard_map/ppermute | solution.py:429
  61.9 13.9 %collective-permute-done.13.rest_1_ = bf16[8,64,768]{2,1,0:T(8,128)(2,1)} collective-permute-done((bf16[8,64,768]{2,1,0:T(8,128)(2,1)}, bf16[8,64,768]{2,1,0:T(8,128)(2,1)}, u32[]{:S(2)}, u32[]{:S(2)}) %collective-permute-start.13) | collective-permute-done | bytes 786464 | tf_op jit(solution)/shard_map/ppermute | solution.py:439
  78.1 18.7 %collective-permute-done.17 = bf16[2,64,1408]{2,1,0:T(8,128)(2,1)S(1)} collective-permute-done((bf16[2,64,1408]{2,1,0:T(8,128)(2,1)S(1)}, bf16[2,64,1408]{2,1,0:T(8,128)(2,1)S(1)}, u32[]{:S(2)}, u32[]{:S(2)}) %collective-permute-start.17) | collective-permute-done | bytes 360480 | tf_op jit(solution)/shard_map/ppermute | solution.py:429
  117.4 11.7 %collective-permute-done.20 = bf16[2,64,2048]{2,1,0:T(8,128)(2,1)} collective-permute-done((bf16[2,64,2048]{2,1,0:T(8,128)(2,1)}, bf16[2,64,2048]{2,1,0:T(8,128)(2,1)}, u32[]{:S(2)}, u32[]{:S(2)}) %collective-permute-start.20) | collective-permute-done | bytes 524320 | tf_op jit(solution)/shard_map/ppermute | solution.py:433
  142.9 11.9 %shard_map.238 = (bf16[1024,2048]{1,0:T(8,128)(2,1)}, f32[1024,768]{1,0:T(8,128)}, bf16[32,64,768]{2,1,0:T(8,128)(2,1)}) custom-call(s32[6]{0:T(128)} %stack.295.where, bf16[1024,2048]{1,0:T(8,128)(2,1)} %bitcast.52.x, f32[1,2048]{1,0:T(1,128)} %slice.164.gain, bf16[8,64,768]{2,1,0:T(8,128)(2,1)} %pad_maximum_fusion.13.rest_0_, ...), custom_call_target="tpu_custom_call" | custom-call | flops 402653184 | bytes 2229251 | tf_op jit(solution)/shard_map/pallas_call | solution.py:65
  168.3 9.6 %shard_map.239 = (f32[2,2,128,128]{3,2,1,0:T(8,128)}, f32[2,2,128,128]{3,2,1,0:T(8,128)}, f32[2,2,512,128]{3,2,1,0:T(8,128)}, bf16[2,2,512,128]{3,2,1,0:T(8,128)...) custom-call(s32[6]{0:T(128)} %stack.295.where, f32[2,2,2,128,768]{4,3,2,1,0:T(8,128)} %bitcast.252, ...), custom_call_target="tpu_custom_call" | custom-call | flops 268435456 | bytes 1869955 | tf_op jit(solution)/shard_map/pallas_call | solution.py:65
  177.9 25.7 %collective-permute-done.27 = bf16[4,64,1408]{2,1,0:T(8,128)(2,1)S(1)} collective-permute-done((bf16[4,64,1408]{2,1,0:T(8,128)(2,1)S(1)}, bf16[4,64,1408]{2,1,0:T(8,128)(2,1)S(1)}, u32[]{:S(2)}, u32[]{:S(2)}) %collective-permute-start.27) | collective-permute-done | bytes 720928 | tf_op jit(solution)/shard_map/ppermute | solution.py:439
  229.9 21.3 %collective-permute-done.29 = bf16[176,2048]{1,0:T(8,128)(2,1)S(1)} collective-permute-done((bf16[176,2048]{1,0:T(8,128)(2,1)S(1)}, bf16[176,2048]{1,0:T(8,128)(2,1)S(1)}, u32[]{:S(2)}, u32[]{:S(2)}) %collective-permute-start.29) | collective-permute-done | bytes 720928 | tf_op jit(solution)/shard_map/ppermute | solution.py:439
  270.4 10.2 %shard_map.241 = (f32[128,2048]{1,0:T(8,128)}, bf16[4,2,128,256]{3,2,1,0:T(8,128)(2,1)}, f32[128,2048]{1,0:T(8,128)}, bf16[128,2048]{1,0:T(8,128)(2,1)}, bf16[32,64,2048]{2,1,0:T(8,128)(2,1)}) custom-call(s32[6]{0:T(128)} %stack.295.where, bf16[128,2048]{1,0:T(8,128)(2,1)} %tokens.1, f32[1,2048]{1,0:T(1,128)} %slice.160.gain_state, ...), custom_call_target="tpu_custom_call" | custom-call | flops 134217728 | bytes 2623491 | tf_op jit(solution)/shard_map/pallas_call | solution.py:65
  284.8 17.8 %collective-permute-done.39 = bf16[2,176,2048]{2,1,0:T(8,128)(2,1)S(1)} collective-permute-done((bf16[2,176,2048]{2,1,0:T(8,128)(2,1)}, bf16[2,176,2048]{2,1,0:T(8,128)(2,1)S(1)}, u32[]{:S(2)}, u32[]{:S(2)}) %collective-permute-start.39) | collective-permute-done | bytes 1441824 | tf_op jit(solution)/shard_map/ppermute | solution.py:439
  307.5 8.5 %all_to_all.71 = bf16[2,512,2048]{2,1,0:T(8,128)(2,1)} all-to-all(bf16[2,512,2048]{2,1,0:T(8,128)(2,1)S(1)} %pad_maximum_fusion.3), channel_id=1, replica_groups=mesh['y'=2,'x'=2,'h'=2,'l'=2,'chip'=2] {'chip'}, dimensions={0} | all-to-all | bytes 8388608 | tf_op jit(solution)/shard_map/all_to_all | solution.py:436
  319.6 29.2 %shard_map.242 = (bf16[1024,704]{1,0:T(8,128)(2,1)}, bf16[1024,1408]{1,0:T(8,128)(2,1)}, bf16[1024,2048]{1,0:T(8,128)(2,1)}, bf16[1024,2048]{1,0:T(8,128)(2,1)}) custom-call(s32[6]{0:T(128)} %stack.295.where, bf16[1024,2048]{1,0:T(8,128)(2,1)} %bitcast.247, bf16[1024,2048]{1,0:T(8,128)(2,1)} %bitcast.79.cotangent.right, bf16[704,2048]{1,0:T(8,128)(2,1)} %bitcast.260, ...), custom_call_target="tpu_custom_call" | custom-call | flops 2583691264 | bytes 3719171 | tf_op jit(solution)/shard_map/pallas_call | solution.py:65
  348.8 8.5 %all_to_all.72 = bf16[2,4,128,2048]{3,2,1,0:T(8,128)(2,1)S(1)} all-to-all(bf16[2,4,128,2048]{3,2,1,0:T(8,128)(2,1)} %bitcast.275), channel_id=1, replica_groups=mesh['y'=2,'x'=2,'h'=2,'l'=2,'chip'=2] {'chip'}, dimensions={0} | all-to-all | bytes 8388608 | tf_op jit(solution)/shard_map/all_to_all | solution.py:436
  358.9 6.0 shard_map.243
  370.1 7.5 %shard_map.246 = bf16[704,2048]{1,0:T(8,128)(2,1)} custom-call(bf16[1024,704]{1,0:T(8,128)(2,1)} %get-tuple-element.283.left, bf16[1024,2048]{1,0:T(8,128)(2,1)} %bitcast.79.cotangent.right), custom_call_target="tpu_custom_call" | custom-call | flops 369098752 | bytes 1064960 | tf_op jit(solution)/shard_map/pallas_call | solution.py:65
  383.6 6.0 shard_map.245
  389.7 6.5 shard_map.244
  404.4 8.7 %shard_map.248 = (f32[128,2048]{1,0:T(8,128)}, bf16[128,2048]{1,0:T(8,128)(2,1)}, bf16[4,2,128,256]{3,2,1,0:T(8,128)(2,1)}) custom-call(s32[6]{0:T(128)} %stack.295.where, f32[128,2048]{1,0:T(8,128)} %convert_add_fusion.6.upstream, bf16[128,2048]{1,0:T(8,128)(2,1)} %cotangent, f32[128,2048]{1,0:T(8,128)} %get-tuple-element.291.residual, ...), custom_call_target="tpu_custom_call" | custom-call | flops 134217728 | bytes 1771523 | tf_op jit(solution)/shard_map/pallas_call | solution.py:65
  431.2 6.5 shard_map.247
  446.5 7.9 %collective-permute-done.52 = bf16[128,2048]{1,0:T(8,128)(2,1)S(1)} collective-permute-done((bf16[128,2048]{1,0:T(8,128)(2,1)}, bf16[128,2048]{1,0:T(8,128)(2,1)S(1)}, u32[]{:S(2)}, u32[]{:S(2)}) %collective-permute-start.52) | collective-permute-done | bytes 524320 | tf_op jit(solution)/shard_map/ppermute | solution.py:429
  454.4 10.8 %collective-permute-done.54 = bf16[128,2048]{1,0:T(8,128)(2,1)} collective-permute-done((bf16[128,2048]{1,0:T(8,128)(2,1)}, bf16[128,2048]{1,0:T(8,128)(2,1)}, u32[]{:S(2)}, u32[]{:S(2)}) %collective-permute-start.54) | collective-permute-done | bytes 524320 | tf_op jit(solution)/shard_map/ppermute | solution.py:429
  473.5 6.7 %collective-permute-done.55.next_grad = bf16[2,2,128,128]{3,2,1,0:T(8,128)(2,1)S(1)} collective-permute-done((bf16[2,2,128,128]{3,2,1,0:T(8,128)(2,1)S(1)}, bf16[2,2,128,128]{3,2,1,0:T(8,128)(2,1)S(1)}, u32[]{:S(2)}, u32[]{:S(2)}) %collective-permute-start.55) | collective-permute-done | bytes 131104 | tf_op jit(solution)/shard_map/ppermute | solution.py:598
  486.1 10.4 %shard_map.250 = (bf16[2,2,2,128,256]{4,3,2,1,0:T(8,128)(2,1)}, bf16[2,2,2,128,256]{4,3,2,1,0:T(8,128)(2,1)}, bf16[2,2,2,128,256]{4,3,2,1,0:T(8,128)(2,1)}, f32[2,2,8,128]{3,2,1,0:T(8,128)}) custom-call(s32[6]{0:T(128)} %stack.295.where, f32[2,2,2,128,768]{4,3,2,1,0:T(8,128)} %bitcast.255, f32[2,2,2,128,768]{4,3,2,1,0:T(8,128)} %bitcast.256, ...), custom_call_target="tpu_custom_call" | custom-call | flops 402653184 | bytes 1937539 | tf_op jit(solution)/shard_map/pallas_call | solution.py:65
  496.5 7.9 %shard_map.251 = bf16[1024,2048]{1,0:T(8,128)(2,1)} custom-call(bf16[1024,256]{1,0:T(8,128)(2,1)} %bitcast.265, bf16[1024,256]{1,0:T(8,128)(2,1)} %bitcast.268, bf16[1024,256]{1,0:T(8,128)(2,1)} %bitcast.271, bf16[32,64,768]{2,1,0:T(8,128)(2,1)} %get-tuple-element.317.weight), custom_call_target="tpu_custom_call" | custom-call | flops 402653184 | bytes 1114112 | tf_op jit(solution)/shard_map/pallas_call | solution.py:65
  543.2 12.1 %all_to_all.74 = bf16[2,512,2048]{2,1,0:T(8,128)(2,1)} all-to-all(bf16[2,512,2048]{2,1,0:T(8,128)(2,1)} %pad_maximum_fusion.4), channel_id=1, replica_groups=mesh['y'=2,'x'=2,'h'=2,'l'=2,'chip'=2] {'chip'}, dimensions={0} | all-to-all | bytes 8388608 | tf_op jit(solution)/shard_map/all_to_all | solution.py:436
  559.9 6.4 shard_map.253
  566.3 7.6 %collective-permute-done.64 = bf16[128,2048]{1,0:T(8,128)(2,1)} collective-permute-done((bf16[128,2048]{1,0:T(8,128)(2,1)}, bf16[128,2048]{1,0:T(8,128)(2,1)}, u32[]{:S(2)}, u32[]{:S(2)}) %collective-permute-start.64) | collective-permute-done | bytes 524320 | tf_op jit(solution)/shard_map/ppermute | solution.py:429
  586.4 7.0 %collective-permute-done.67 = bf16[2,64,2048]{2,1,0:T(8,128)(2,1)S(1)} collective-permute-done((bf16[2,64,2048]{2,1,0:T(8,128)(2,1)S(1)}, bf16[2,64,2048]{2,1,0:T(8,128)(2,1)S(1)}, u32[]{:S(2)}, u32[]{:S(2)}) %collective-permute-start.67) | collective-permute-done | bytes 524320 | tf_op jit(solution)/shard_map/ppermute | solution.py:439
  594.2 8.6 %collective-permute-done.68 = bf16[2,64,1408]{2,1,0:T(8,128)(2,1)S(1)} collective-permute-done((bf16[2,64,1408]{2,1,0:T(8,128)(2,1)S(1)}, bf16[2,64,1408]{2,1,0:T(8,128)(2,1)S(1)}, u32[]{:S(2)}, u32[]{:S(2)}) %collective-permute-start.68) | collective-permute-done | bytes 360480 | tf_op jit(solution)/shard_map/ppermute | solution.py:429
  602.8 7.0 %collective-permute-done.70 = bf16[2,64,1408]{2,1,0:T(8,128)(2,1)S(1)} collective-permute-done((bf16[2,64,1408]{2,1,0:T(8,128)(2,1)S(1)}, bf16[2,64,1408]{2,1,0:T(8,128)(2,1)S(1)}, u32[]{:S(2)}, u32[]{:S(2)}) %collective-permute-start.70) | collective-permute-done | bytes 360480 | tf_op jit(solution)/shard_map/ppermute | solution.py:429
  611.1 8.2 %collective-permute-done.66 = bf16[2,256,768]{2,1,0:T(8,128)(2,1)S(1)} collective-permute-done((bf16[2,256,768]{2,1,0:T(8,128)(2,1)S(1)}, bf16[2,256,768]{2,1,0:T(8,128)(2,1)S(1)}, u32[]{:S(2)}, u32[]{:S(2)}) %collective-permute-start.66) | collective-permute-done | bytes 786464 | tf_op jit(solution)/shard_map/ppermute | solution.py:439
  657.1 7.6 %collective-permute-done.78 = f32[64]{0:T(128)S(1)} collective-permute-done((f32[64]{0:T(128)S(1)}, f32[64]{0:T(128)S(1)}, u32[]{:S(2)}, u32[]{:S(2)}) %collective-permute-start.78) | collective-permute-done | bytes 288 | tf_op jit(solution)/shard_map/ppermute | solution.py:774
  (379 shorter events, 320.2 us)
Async XLA Ops:
  19.4 34.1 %collective-permute-start.9 = (bf16[128,2048]{1,0:T(8,128)(2,1)S(1)}, bf16[128,2048]{1,0:T(8,128)(2,1)}, u32[]{:S(2)}, u32[]{:S(2)}) collective-permute-start(bf16[128,2048]{1,0:T(8,128)(2,1)S(1)} %copy-done.9), channel_id=1, source_target_pairs={{0,2},{2,0},{1,3},{3,1},{4,6},{6,4},{5,7},{7,5},{8,10},{10,8},{9,1... | collective-permute-start | bytes 1572872 | tf_op jit(solution)/shard_map/ppermute | solution.py:433
  56.4 43.3 %collective-permute-start.15 = (bf16[256,2048]{1,0:T(8,128)(2,1)S(1)}, bf16[256,2048]{1,0:T(8,128)(2,1)}, u32[]{:S(2)}, u32[]{:S(2)}) collective-permute-start(bf16[256,2048]{1,0:T(8,128)(2,1)S(1)} %pad_maximum_fusion.9), channel_id=1, source_target_pairs={{0,8},{8,0},{1,9},{9,1},{2,10},{10,2},{3,11},{11,3},{4,12},{12,4},... | collective-permute-start | bytes 3145736 | tf_op jit(solution)/shard_map/ppermute | solution.py:433
  57.9 38.9 %collective-permute-start.17 = (bf16[2,64,1408]{2,1,0:T(8,128)(2,1)S(1)}, bf16[2,64,1408]{2,1,0:T(8,128)(2,1)S(1)}, u32[]{:S(2)}, u32[]{:S(2)}) collective-permute-start(bf16[2,64,1408]{2,1,0:T(8,128)(2,1)S(1)} %get-tuple-element.379), channel_id=1, source_target_pairs={{0,8},{2,10},{8,0},{10,2},{1,9},{3,11},{9,1},{11,3},{4,12},{6,14},... | collective-permute-start | bytes 1081352 | tf_op jit(solution)/shard_map/ppermute | solution.py:429
  59.4 38.9 %collective-permute-start.18 = (bf16[2,64,1408]{2,1,0:T(8,128)(2,1)S(1)}, bf16[2,64,1408]{2,1,0:T(8,128)(2,1)S(1)}, u32[]{:S(2)}, u32[]{:S(2)}) collective-permute-start(bf16[2,64,1408]{2,1,0:T(8,128)(2,1)S(1)} %get-tuple-element.380), channel_id=1, source_target_pairs={{0,10},{2,8},{8,2},{10,0},{1,11},{3,9},{9,3},{11,1},{4,14},{6,12},... | collective-permute-start | bytes 1081352 | tf_op jit(solution)/shard_map/ppermute | solution.py:429
  61.0 38.7 %collective-permute-start.12 = (bf16[8,64,768]{2,1,0:T(8,128)(2,1)}, bf16[8,64,768]{2,1,0:T(8,128)(2,1)}, u32[]{:S(2)}, u32[]{:S(2)}) collective-permute-start(bf16[8,64,768]{2,1,0:T(8,128)(2,1)} %pad_maximum_fusion.13.rest_0_), channel_id=1, source_target_pairs={{0,4},{4,0},{1,5},{5,1},{2,6},{6,2},{3,7},{7,3},{8,12},{12,8},{9,1... | collective-permute-start | bytes 2359304 | tf_op jit(solution)/shard_map/ppermute | solution.py:439
  160.0 43.8 %collective-permute-start.25 = (bf16[2,2,64,2048]{3,2,1,0:T(8,128)(2,1)}, bf16[2,2,64,2048]{3,2,1,0:T(8,128)(2,1)}, u32[]{:S(2)}, u32[]{:S(2)}) collective-permute-start(bf16[2,2,64,2048]{3,2,1,0:T(8,128)(2,1)} %get-tuple-element.384), channel_id=1, source_target_pairs={{0,8},{8,0},{1,9},{9,1},{2,10},{10,2},{3,11},{11,3},{4,12},{12,4},... | collective-permute-start | bytes 3145736 | tf_op jit(solution)/shard_map/ppermute | solution.py:433
  161.5 46.4 %collective-permute-start.24 = (bf16[2,4,64,1408]{3,2,1,0:T(8,128)(2,1)S(1)}, bf16[2,4,64,1408]{3,2,1,0:T(8,128)(2,1)}, u32[]{:S(2)}, u32[]{:S(2)}) collective-permute-start(bf16[2,4,64,1408]{3,2,1,0:T(8,128)(2,1)S(1)} %pad_maximum_fusion.5.rest_0_), channel_id=1, source_target_pairs={{0,16},{16,0},{1,17},{17,1},{2,18},{18,2},{3,19},{19,3},{4,20},{20... | collective-permute-start | bytes 4325384 | tf_op jit(solution)/shard_map/ppermute | solution.py:439
  165.2 39.3 %collective-permute-start.26 = (bf16[2,2,64,2048]{3,2,1,0:T(8,128)(2,1)}, bf16[2,2,64,2048]{3,2,1,0:T(8,128)(2,1)}, u32[]{:S(2)}, u32[]{:S(2)}) collective-permute-start(bf16[2,2,64,2048]{3,2,1,0:T(8,128)(2,1)} %get-tuple-element.386), channel_id=1, source_target_pairs={{0,2},{2,0},{1,3},{3,1},{4,6},{6,4},{5,7},{7,5},{8,10},{10,8},{9,1... | collective-permute-start | bytes 3145736 | tf_op jit(solution)/shard_map/ppermute | solution.py:433
  165.8 37.8 %collective-permute-start.27 = (bf16[4,64,1408]{2,1,0:T(8,128)(2,1)S(1)}, bf16[4,64,1408]{2,1,0:T(8,128)(2,1)S(1)}, u32[]{:S(2)}, u32[]{:S(2)}) collective-permute-start(bf16[4,64,1408]{2,1,0:T(8,128)(2,1)S(1)} %pad_maximum_fusion.16), channel_id=1, source_target_pairs={{0,4},{4,0},{1,5},{5,1},{2,6},{6,2},{3,7},{7,3},{8,12},{12,8},{9,1... | collective-permute-start | bytes 2162696 | tf_op jit(solution)/shard_map/ppermute | solution.py:439
  208.0 59.5 %collective-permute-start.34 = (bf16[4,2,2,64,2048]{4,3,2,1,0:T(8,128)(2,1)}, bf16[4,2,2,64,2048]{4,3,2,1,0:T(8,128)(2,1)}, u32[]{:S(2)}, u32[]{:S(2)}) collective-permute-start(bf16[4,2,2,64,2048]{4,3,2,1,0:T(8,128)(2,1)} %pad_maximum_fusion.1.rest_4_), channel_id=1, source_target_pairs={{0,1},{1,0},{2,3},{3,2},{4,5},{5,4},{6,7},{7,6},{8,9},{9,8},{10,11... | collective-permute-start | bytes 12582920 | tf_op jit(solution)/shard_map/ppermute | solution.py:612
  208.0 45.5 %collective-permute-start.35 = (bf16[256,2048]{1,0:T(8,128)(2,1)S(1)}, bf16[256,2048]{1,0:T(8,128)(2,1)S(1)}, u32[]{:S(2)}, u32[]{:S(2)}) collective-permute-start(bf16[256,2048]{1,0:T(8,128)(2,1)S(1)} %pad_maximum_fusion.10), channel_id=1, source_target_pairs={{0,8},{8,0},{1,9},{9,1},{2,10},{10,2},{3,11},{11,3},{4,12},{12,4},... | collective-permute-start | bytes 3145736 | tf_op jit(solution)/shard_map/ppermute | solution.py:433
  213.7 53.8 %collective-permute-start.33 = (bf16[2,4,64,1408]{3,2,1,0:T(8,128)(2,1)S(1)}, bf16[2,4,64,1408]{3,2,1,0:T(8,128)(2,1)}, u32[]{:S(2)}, u32[]{:S(2)}) collective-permute-start(bf16[2,4,64,1408]{3,2,1,0:T(8,128)(2,1)S(1)} %pad_maximum_fusion.6.rest_2_), channel_id=1, source_target_pairs={{0,16},{16,0},{1,17},{17,1},{2,18},{18,2},{3,19},{19,3},{4,20},{20... | collective-permute-start | bytes 4325384 | tf_op jit(solution)/shard_map/ppermute | solution.py:439
  216.8 34.5 %collective-permute-start.29 = (bf16[176,2048]{1,0:T(8,128)(2,1)S(1)}, bf16[176,2048]{1,0:T(8,128)(2,1)S(1)}, u32[]{:S(2)}, u32[]{:S(2)}) collective-permute-start(bf16[176,2048]{1,0:T(8,128)(2,1)S(1)} %copy-done.17), channel_id=1, source_target_pairs={{0,4},{4,0},{1,5},{5,1},{2,6},{6,2},{3,7},{7,3},{8,12},{12,8},{9,1... | collective-permute-start | bytes 2162696 | tf_op jit(solution)/shard_map/ppermute | solution.py:439
  268.7 33.8 %collective-permute-start.39 = (bf16[2,176,2048]{2,1,0:T(8,128)(2,1)}, bf16[2,176,2048]{2,1,0:T(8,128)(2,1)S(1)}, u32[]{:S(2)}, u32[]{:S(2)}) collective-permute-start(bf16[2,176,2048]{2,1,0:T(8,128)(2,1)} %pad_maximum_fusion.7), channel_id=1, source_target_pairs={{0,16},{16,0},{1,17},{17,1},{2,18},{18,2},{3,19},{19,3},{4,20},{20... | collective-permute-start | bytes 4325384 | tf_op jit(solution)/shard_map/ppermute | solution.py:439
  316.0 48.9 %collective-permute-start.42 = (bf16[2,128,256]{2,1,0:T(8,128)(2,1)S(1)}, bf16[2,128,256]{2,1,0:T(8,128)(2,1)S(1)}, u32[]{:S(2)}, u32[]{:S(2)}) collective-permute-start(bf16[2,128,256]{2,1,0:T(8,128)(2,1)S(1)} %get-tuple-element.402), channel_id=1, source_target_pairs={{0,10},{2,8},{8,2},{10,0},{1,11},{3,9},{9,3},{11,1},{4,14},{6,12},... | collective-permute-start | bytes 393224 | tf_op jit(solution)/shard_map/ppermute | solution.py:429
  317.6 47.3 %collective-permute-start.41 = (bf16[2,128,256]{2,1,0:T(8,128)(2,1)S(1)}, bf16[2,128,256]{2,1,0:T(8,128)(2,1)S(1)}, u32[]{:S(2)}, u32[]{:S(2)}) collective-permute-start(bf16[2,128,256]{2,1,0:T(8,128)(2,1)S(1)} %get-tuple-element.403), channel_id=1, source_target_pairs={{0,8},{2,10},{8,0},{10,2},{1,9},{3,11},{9,1},{11,3},{4,12},{6,14},... | collective-permute-start | bytes 393224 | tf_op jit(solution)/shard_map/ppermute | solution.py:429
  318.3 46.7 %collective-permute-start.40 = (bf16[2,128,256]{2,1,0:T(8,128)(2,1)S(1)}, bf16[2,128,256]{2,1,0:T(8,128)(2,1)S(1)}, u32[]{:S(2)}, u32[]{:S(2)}) collective-permute-start(bf16[2,128,256]{2,1,0:T(8,128)(2,1)S(1)} %get-tuple-element.404), channel_id=1, source_target_pairs={{0,2},{2,0},{8,10},{10,8},{1,3},{3,1},{9,11},{11,9},{4,6},{6,4},{1... | collective-permute-start | bytes 393224 | tf_op jit(solution)/shard_map/ppermute | solution.py:429
  365.1 37.6 %collective-permute-start.43 = (bf16[2,1,256,1408]{3,2,1,0:T(8,128)(2,1)}, bf16[2,1,256,1408]{3,2,1,0:T(8,128)(2,1)}, u32[]{:S(2)}, u32[]{:S(2)}) collective-permute-start(bf16[2,1,256,1408]{3,2,1,0:T(8,128)(2,1)} %shard_map.243), channel_id=1, source_target_pairs={{0,16},{16,0},{1,17},{17,1},{2,18},{18,2},{3,19},{19,3},{4,20},{20... | collective-permute-start | bytes 4325384 | tf_op jit(solution)/shard_map/ppermute | solution.py:439
  426.1 39.1 %collective-permute-start.54 = (bf16[128,2048]{1,0:T(8,128)(2,1)}, bf16[128,2048]{1,0:T(8,128)(2,1)}, u32[]{:S(2)}, u32[]{:S(2)}) collective-permute-start(bf16[128,2048]{1,0:T(8,128)(2,1)} %get-tuple-element.305), channel_id=1, source_target_pairs={{0,10},{2,8},{8,2},{10,0},{1,11},{3,9},{9,3},{11,1},{4,14},{6,12},... | collective-permute-start | bytes 1572872 | tf_op jit(solution)/shard_map/ppermute | solution.py:429
  427.5 41.1 %collective-permute-start.47 = (bf16[2,1,256,1408]{3,2,1,0:T(8,128)(2,1)}, bf16[2,1,256,1408]{3,2,1,0:T(8,128)(2,1)}, u32[]{:S(2)}, u32[]{:S(2)}) collective-permute-start(bf16[2,1,256,1408]{3,2,1,0:T(8,128)(2,1)} %shard_map.245), channel_id=1, source_target_pairs={{0,16},{16,0},{1,17},{17,1},{2,18},{18,2},{3,19},{19,3},{4,20},{20... | collective-permute-start | bytes 4325384 | tf_op jit(solution)/shard_map/ppermute | solution.py:439
  428.9 38.7 %collective-permute-start.51 = (bf16[1,256,1408]{2,1,0:T(8,128)(2,1)}, bf16[1,256,1408]{2,1,0:T(8,128)(2,1)S(1)}, u32[]{:S(2)}, u32[]{:S(2)}) collective-permute-start(bf16[1,256,1408]{2,1,0:T(8,128)(2,1)} %fusion.6), channel_id=1, source_target_pairs={{0,4},{4,0},{1,5},{5,1},{2,6},{6,2},{3,7},{7,3},{8,12},{12,8},{9,1... | collective-permute-start | bytes 2162696 | tf_op jit(solution)/shard_map/ppermute | solution.py:439
  473.1 57.0 %collective-permute-start.60 = (bf16[2,176,2048]{2,1,0:T(8,128)(2,1)}, bf16[2,176,2048]{2,1,0:T(8,128)(2,1)}, u32[]{:S(2)}, u32[]{:S(2)}) collective-permute-start(bf16[2,176,2048]{2,1,0:T(8,128)(2,1)} %dynamic-slice_bitcast_fusion), channel_id=1, source_target_pairs={{0,16},{16,0},{1,17},{17,1},{2,18},{18,2},{3,19},{19,3},{4,20},{20... | collective-permute-start | bytes 4325384 | tf_op jit(solution)/shard_map/ppermute | solution.py:439
  481.1 41.2 %collective-permute-start.56 = (bf16[1,256,1408]{2,1,0:T(8,128)(2,1)}, bf16[1,256,1408]{2,1,0:T(8,128)(2,1)}, u32[]{:S(2)}, u32[]{:S(2)}) collective-permute-start(bf16[1,256,1408]{2,1,0:T(8,128)(2,1)} %fusion.7), channel_id=1, source_target_pairs={{0,4},{4,0},{1,5},{5,1},{2,6},{6,2},{3,7},{7,3},{8,12},{12,8},{9,1... | collective-permute-start | bytes 2162696 | tf_op jit(solution)/shard_map/ppermute | solution.py:439
  482.6 49.5 %collective-permute-start.59 = (bf16[128,2048]{1,0:T(8,128)(2,1)}, bf16[128,2048]{1,0:T(8,128)(2,1)}, u32[]{:S(2)}, u32[]{:S(2)}) collective-permute-start(bf16[128,2048]{1,0:T(8,128)(2,1)} %get-tuple-element.337), channel_id=1, source_target_pairs={{0,10},{2,8},{8,2},{10,0},{1,11},{3,9},{9,3},{11,1},{4,14},{6,12},... | collective-permute-start | bytes 1572872 | tf_op jit(solution)/shard_map/ppermute | solution.py:429
  482.6 49.5 %collective-permute-start.58 = (bf16[128,2048]{1,0:T(8,128)(2,1)}, bf16[128,2048]{1,0:T(8,128)(2,1)}, u32[]{:S(2)}, u32[]{:S(2)}) collective-permute-start(bf16[128,2048]{1,0:T(8,128)(2,1)} %get-tuple-element.337), channel_id=1, source_target_pairs={{0,8},{2,10},{8,0},{10,2},{1,9},{3,11},{9,1},{11,3},{4,12},{6,14},... | collective-permute-start | bytes 1572872 | tf_op jit(solution)/shard_map/ppermute | solution.py:429
  483.5 48.6 %collective-permute-start.57 = (bf16[128,2048]{1,0:T(8,128)(2,1)}, bf16[128,2048]{1,0:T(8,128)(2,1)}, u32[]{:S(2)}, u32[]{:S(2)}) collective-permute-start(bf16[128,2048]{1,0:T(8,128)(2,1)} %get-tuple-element.337), channel_id=1, source_target_pairs={{0,2},{2,0},{8,10},{10,8},{1,3},{3,1},{9,11},{11,9},{4,6},{6,4},{1... | collective-permute-start | bytes 1572872 | tf_op jit(solution)/shard_map/ppermute | solution.py:429
  532.1 34.1 %collective-permute-start.62 = (bf16[128,2048]{1,0:T(8,128)(2,1)}, bf16[128,2048]{1,0:T(8,128)(2,1)S(1)}, u32[]{:S(2)}, u32[]{:S(2)}) collective-permute-start(bf16[128,2048]{1,0:T(8,128)(2,1)} %get-tuple-element.332), channel_id=1, source_target_pairs={{0,2},{2,0},{8,10},{10,8},{1,3},{3,1},{9,11},{11,9},{4,6},{6,4},{1... | collective-permute-start | bytes 1572872 | tf_op jit(solution)/shard_map/ppermute | solution.py:429
  532.2 34.1 %collective-permute-start.63 = (bf16[128,2048]{1,0:T(8,128)(2,1)}, bf16[128,2048]{1,0:T(8,128)(2,1)}, u32[]{:S(2)}, u32[]{:S(2)}) collective-permute-start(bf16[128,2048]{1,0:T(8,128)(2,1)} %get-tuple-element.333), channel_id=1, source_target_pairs={{0,8},{2,10},{8,0},{10,2},{1,9},{3,11},{9,1},{11,3},{4,12},{6,14},... | collective-permute-start | bytes 1572872 | tf_op jit(solution)/shard_map/ppermute | solution.py:429
  533.2 40.7 %collective-permute-start.64 = (bf16[128,2048]{1,0:T(8,128)(2,1)}, bf16[128,2048]{1,0:T(8,128)(2,1)}, u32[]{:S(2)}, u32[]{:S(2)}) collective-permute-start(bf16[128,2048]{1,0:T(8,128)(2,1)} %get-tuple-element.334), channel_id=1, source_target_pairs={{0,10},{2,8},{8,2},{10,0},{1,11},{3,9},{9,3},{11,1},{4,14},{6,12},... | collective-permute-start | bytes 1572872 | tf_op jit(solution)/shard_map/ppermute | solution.py:429
  535.8 39.5 %collective-permute-start.65 = (bf16[176,2048]{1,0:T(8,128)(2,1)S(1)}, bf16[176,2048]{1,0:T(8,128)(2,1)}, u32[]{:S(2)}, u32[]{:S(2)}) collective-permute-start(bf16[176,2048]{1,0:T(8,128)(2,1)S(1)} %fusion.8), channel_id=1, source_target_pairs={{0,4},{4,0},{1,5},{5,1},{2,6},{6,2},{3,7},{7,3},{8,12},{12,8},{9,1... | collective-permute-start | bytes 2162696 | tf_op jit(solution)/shard_map/ppermute | solution.py:439
  538.8 39.0 %collective-permute-start.61 = (bf16[2,2,256,768]{3,2,1,0:T(8,128)(2,1)}, bf16[2,2,256,768]{3,2,1,0:T(8,128)(2,1)S(1)}, u32[]{:S(2)}, u32[]{:S(2)}) collective-permute-start(bf16[2,2,256,768]{3,2,1,0:T(8,128)(2,1)} %shard_map.252), channel_id=1, source_target_pairs={{0,16},{16,0},{1,17},{17,1},{2,18},{18,2},{3,19},{19,3},{4,20},{20... | collective-permute-start | bytes 4718600 | tf_op jit(solution)/shard_map/ppermute | solution.py:439
  583.4 35.9 %collective-permute-start.66 = (bf16[2,256,768]{2,1,0:T(8,128)(2,1)S(1)}, bf16[2,256,768]{2,1,0:T(8,128)(2,1)S(1)}, u32[]{:S(2)}, u32[]{:S(2)}) collective-permute-start(bf16[2,256,768]{2,1,0:T(8,128)(2,1)S(1)} %fusion.5), channel_id=1, source_target_pairs={{0,4},{4,0},{1,5},{5,1},{2,6},{6,2},{3,7},{7,3},{8,12},{12,8},{9,1... | collective-permute-start | bytes 2359304 | tf_op jit(solution)/shard_map/ppermute | solution.py:439
  (104 other events, 1528.1 us)

commit v4 on v3

--- a/solution.py
+++ b/solution.py
@@ -489,36 +489,37 @@
         out = [lax.dynamic_index_in_dim(x, (y - i) % ny, 0, keepdims=False) for i in range(1, ny + 1)]
         return out[0], out[1:]
 
+    spread = lambda w: w.reshape(r, plane, nc, part)
+    three = jnp.concatenate([spread(w_forget), spread(w_input), spread(w_query)], axis=3).transpose(2, 1, 0, 3)
+    three = to_cores(three)
+    three = jnp.concatenate(from_plane(at_plane(three, 1)))
     small = jnp.concatenate([gain_mix, gain_state, gain_ffn, lower_bound, starts.astype(F32)]).reshape(1, -1)
-    small_mine = jnp.concatenate(from_plane([small] * plane))
+    small_mine = jnp.concatenate(from_plane([after(small, three)] * plane))
     small_other = lax.ppermute(small_mine, "chip", [(i, i ^ 1) for i in range(nc)])
     plane_small = jnp.concatenate([pick(c == 0, small_mine, small_other), pick(c == 0, small_other, small_mine)])
-    spread = lambda w: w.reshape(r, plane, nc, part)
-    three = jnp.concatenate([spread(w_forget), spread(w_input), spread(w_query)], axis=3).transpose(2, 1, 0, 3)
-    three = jnp.concatenate(from_plane(at_plane(to_cores(three), 1)))
-    out_line = turns(w_output, "h", nh)
     out_first = turns(w_output, "y", ny)
     tokens_pair = jnp.concatenate([tokens, swap(tokens, "l")])
     vectors = jnp.stack(turns(plane_small[:, : 4 * r], "y", ny))
     vectors = jnp.concatenate(turns(vectors, "h", nh)).reshape(plan.devices, -1)
     (packed,) = call(partial(pack_kernel, plan, ffr), [shape((nc, plane, r, 2 * units), LOW)], w_gate, w_up)
-    packed = to_cores(after(packed, out_line))
-    plane_small, three, out_line, out_first, tokens_pair, packed, vectors, cotangent, w_down = fence(
-        plane_small, three, out_line, out_first, tokens_pair, packed, vectors, cotangent, w_down
+    packed = to_cores(packed)
+    plane_small, three, w_output, out_first, tokens_pair, packed, vectors, cotangent, w_down = fence(
+        plane_small, three, w_output, out_first, tokens_pair, packed, vectors, cotangent, w_down
     )
 
     three_line = turns(three, "h", nh)
     three_first = turns(three, "y", ny)
-    out_copies = out_first + [z for x in out_line[1:] for z in turns(after(x, three_first), "y", ny)]
+    out_line = turns(after(w_output, three_line), "h", nh)
     tokens_far = swap(tokens_pair, "x")
     gate_up = from_plane(at_plane(packed, 1))
     gate_up = [jnp.concatenate(gate_up[:nl]), jnp.concatenate(gate_up[nl:])]
-    three_line, three_first, out_copies, tokens_pair, tokens_far, gate_up, cotangent, w_down = fence(
-        three_line, three_first, out_copies, tokens_pair, tokens_far, gate_up, cotangent, w_down
+    three_line, three_first, out_line, tokens_pair, tokens_far, gate_up, cotangent, w_down = fence(
+        three_line, three_first, out_line, tokens_pair, tokens_far, gate_up, cotangent, w_down
     )
 
     three = three_first + [z for x in three_line[1:] for z in turns(x, "y", ny)]
-    gu_first = jnp.stack(turns(gate_up[0], "h", nh))
+    out_copies = out_first + [z for x in out_line[1:] for z in turns(x, "y", ny)]
+    gu_line = turns(gate_up[0], "h", nh)
     plane_tokens = over_plane([tokens_pair, tokens_far])
     plane_starts = (
         plane_small[:, 4 * r :].reshape(nc, nx, nl, rows).transpose(1, 2, 0, 3).reshape(nx, span)
@@ -545,6 +546,7 @@
         scratch=[pltpu.SemaphoreType.DMA((count,))],
         flops=project_flops,
     )
+    gu_first = jnp.stack(after(gu_line, pre))
     cut = copies // 2
     pieces = [jnp.stack(out_copies[:cut]), jnp.stack(out_copies[cut:])]
     moved = [swap(z, axis) for z, axis in zip(pieces, ("l", "x"))]
@@ -637,7 +639,7 @@
 
     plane_ffn = over_plane(ffn_pieces)
     gu_names = [(j, k) for k in (0, nl) for j in range(ny)]
-    step = min(256, half)
+    step = half
     row_spec = lambda n: pl.BlockSpec((step, n), lambda t: (t, 0))
     hidden, grad_gu, part_out, part_ffn = call(
         partial(ffn_kernel, plan, gu_names),
@@ -694,18 +696,18 @@
     grad_gu_far = scatter_h(after(grad_gu_far, grads))
     output = (residual + summed_plane(after(both_out, grads))).astype(LOW)
     grads = by_group(to_cores(grads))
+    mix_parts = to_cores(after(mix_parts, grads))
     (state_grad,) = call(
         mix_state_grad_kernel, [shape(states)], query_reach, grads,
         grid=(nx, heads), specs=[rows_spec, piece(0)], out_specs=[state_spec], flops=mix_flops // 4,
     )
-    grad_gu_near, state_grad, grads, branch, grad_gu_far, output, grad_down = fence(
-        grad_gu_near, state_grad, grads, branch, grad_gu_far, output, grad_down
+    grad_gu_near, state_grad, grads, branch, grad_gu_far, output, grad_down, mix_parts = fence(
+        grad_gu_near, state_grad, grads, branch, grad_gu_far, output, grad_down, mix_parts
     )
 
     next_grad = carry(state_grad, -1)
     grad_gu_near = scatter_h(after(grad_gu_near, next_grad))
     branch_pieces = from_plane([branch] * plane)
-    grad_down = scatter_y(*rows_of_y(grad_down.reshape(ny, nh, ffr, width)))
     df, dv, dq, lower_grad = call(
         mix_back_kernel,
         [shape(grouped, LOW)] * 3 + [shape((nx, heads, 8, HDIM))],
@@ -717,20 +719,22 @@
         flops=12 * mix_flops,
     )
     pre_grads = [g.reshape(total, part) for g in (df, dv, dq)]
+    three_sent = columns_grad(1, LOW, (0, 1), normed_in, pre_grads)
     (part_in,) = call(
-        inputs_grad_kernel, [shape((total, width), LOW)], *pre_grads, w_three, flops=project_flops
+        inputs_grad_kernel, [shape((total, width), LOW)], *after(pre_grads, three_sent), w_three, flops=project_flops
     )
     both_in = summed_core(part_in)
-    three_sent = columns_grad(1, LOW, (0, 1), normed_in, after(pre_grads, grad_gu_near))
-    both_in, three_sent, pre_grads, branch_pieces, grad_gu_near, grad_gu_far, grad_down = fence(
-        both_in, three_sent, pre_grads, branch_pieces, grad_gu_near, grad_gu_far, grad_down
+    three_kept = columns_kept((0, 1), normed_in, after(pre_grads, both_in))
+    grad_three = scatter_y(three_sent, three_kept)
+    both_in, grad_three, branch_pieces, grad_gu_near, grad_gu_far, grad_down = fence(
+        both_in, grad_three, branch_pieces, grad_gu_near, grad_gu_far, grad_down
     )
 
     grad_normed_in = summed_plane(both_in)
-    grad_three = scatter_y(three_sent, columns_kept((0, 1), normed_in, pre_grads))
-    grad_down = scatter_h(grad_down)
+    grad_three = scatter_h(grad_three)
+    grad_down = scatter_y(*rows_of_y(grad_down.reshape(ny, nh, ffr, width)))
     (grad_out,) = call(
-        rows_grad_kernel, [shape((part, width), LOW)], to_cores(mix_parts).reshape(total, part), over_plane(branch_pieces),
+        rows_grad_kernel, [shape((part, width), LOW)], mix_parts.reshape(total, part), over_plane(branch_pieces),
         flops=2 * total * part * width,
     )
     grad_three, grad_normed_in, grad_gu_near, grad_out, grad_gu_far, grad_down = fence(
@@ -739,16 +743,17 @@
 
     own_tokens = tokens.astype(F32)
     grad_tokens = grad_residual + norm_back(own_tokens, inverse_rms(own_tokens), grad_normed_in * full_gain_mix)
-    grad_three = scatter_h(grad_three).astype(LOW).reshape(nx, nl, nc, r, 3 * part)
+    grad_three = grad_three.astype(LOW).reshape(nx, nl, nc, r, 3 * part)
     grad_output = scatter_y(*rows_of_y(grad_out.reshape(ny, nh, r, width)))
     gu_blocks = collect([z.astype(LOW).reshape(nl, nc, r, 2 * units) for z in (grad_gu_near, grad_gu_far)])
+    three_blocks = collect([after(grad_three[t], gu_blocks) for t in range(nx)])
+    grad_down = scatter_h(grad_down)
     lower_grad = jnp.sum(lower_grad[:, :, 0], axis=0).reshape(1, part)
     lower_grad = sum(turns(after(lower_grad, grad_output), "y", ny))
-    grad_three, grad_output, gu_blocks, lower_grad = fence(
-        grad_three, grad_output, gu_blocks, lower_grad
-    )
-
-    three_blocks = collect([grad_three[t] for t in range(nx)])
+    three_blocks, grad_output, gu_blocks, lower_grad = fence(
+        three_blocks, grad_output, gu_blocks, lower_grad
+    )
+
     grad_output = scatter_h(grad_output)
     lower_grad = sum(turns(after(lower_grad, grad_output), "h", nh))
     owners = []

time: 674 us -> 668 us (level)
  blocking collectives: 44.4 us -> 57.6 us
  starting transfers between devices: 139 us -> 126 us
  waiting for transfers between devices: 234 us -> 226 us
    ppermute x8, waiting for transfers between devices: 14.2 us -> 0.18 us  [swap(): return lax.ppermute(x, axis, [(0, 1), (1, 0)])]
    all_to_all x6 -> x8, blocking collectives: 44.4 us -> 57.6 us  [to_cores(): return lax.all_to_all(x, 'chip', 0, 0, tiled=True)]
    ppermute x39, waiting for transfers between devices: 87.7 us -> 99 us  [from_plane(): lax.ppermute(blocks[k], ('x', 'l'), [(i, i ^ k) for i in range(plane)])]
    all_to_all x8 -> x6, starting transfers between devices: 37.7 us -> 26.6 us  [to_cores(): return lax.all_to_all(x, 'chip', 0, 0, tiled=True)]
  transfers between devices with their start and end apart: 87 -> 85, of which waited for: 34 -> 37; matrix products, arithmetic and copies ran while one was open for 11% -> 11% of each run, Pallas kernels for 22% -> 19%
where the time goes in v4:
time: 668 us; the launch traced here: 661 us
  waiting for transfers between devices  226 us (34%)
  Pallas kernels  153 us (23%)
  starting transfers between devices  126 us (19%)
  other arithmetic  63.5 us (10%)
  blocking collectives  57.6 us (9%)
  local copies, waits for them, and re-layouts  31.2 us (5%)
    pallas_call x20, Pallas kernels, call(): pl.pallas_call(kernel, out_shape=outs, grid=grid, in_specs=specs, out_spe...  153 us
    ppermute x26, waiting for transfers between devices, turn(): return lax.ppermute(x, axis, [(i, (i + 1) % n) for i in range(n)])  105 us
    ppermute x39, waiting for transfers between devices, from_plane(): lax.ppermute(blocks[k], ('x', 'l'), [(i, i ^ k) for i in range(plane)])  99 us
    all_to_all x8, blocking collectives, to_cores(): return lax.all_to_all(x, 'chip', 0, 0, tiled=True)  57.6 us
    ppermute x39, starting transfers between devices, from_plane(): lax.ppermute(blocks[k], ('x', 'l'), [(i, i ^ k) for i in range(plane)])  45.4 us
    ppermute x26, starting transfers between devices, turn(): return lax.ppermute(x, axis, [(i, (i + 1) % n) for i in range(n)])  32.8 us
    all_to_all x6, starting transfers between devices, to_cores(): return lax.all_to_all(x, 'chip', 0, 0, tiled=True)  26.6 us
  transfers between devices with their start and end apart: 85, of which 37 were waited for; matrix products, arithmetic and copies ran while one was open for 11% of the time, Pallas kernels for 19%

profile of v4, /device:TPU:2, one launch (start us, length us, event | category | flops | bytes accessed | tf_op | source)
XLA Modules:
  0.0 660.7 jit_solution(9247997800862985385)
XLA Ops:
  55.3 28.7 %collective-permute-done.11.rest_2_ = bf16[8,64,768]{2,1,0:T(8,128)(2,1)S(1)} collective-permute-done((bf16[8,64,768]{2,1,0:T(8,128)(2,1)}, bf16[8,64,768]{2,1,0:T(8,128)(2,1)S(1)}, u32[]{:S(2)}, u32[]{:S(2)}) %collective-permute-start.11) | collective-permute-done | bytes 786464 | tf_op jit(solution)/shard_map/ppermute | solution.py:439
  89.9 7.4 %collective-permute-done.15 = bf16[2,64,1408]{2,1,0:T(8,128)(2,1)S(1)} collective-permute-done((bf16[2,64,1408]{2,1,0:T(8,128)(2,1)S(1)}, bf16[2,64,1408]{2,1,0:T(8,128)(2,1)S(1)}, u32[]{:S(2)}, u32[]{:S(2)}) %collective-permute-start.15) | collective-permute-done | bytes 360480 | tf_op jit(solution)/shard_map/ppermute | solution.py:429
  128.7 8.6 %all_to_all.70 = bf16[2,512,2048]{2,1,0:T(8,128)(2,1)} all-to-all(bf16[2,512,2048]{2,1,0:T(8,128)(2,1)S(1)} %pad_maximum_fusion), channel_id=1, replica_groups=mesh['y'=2,'x'=2,'h'=2,'l'=2,'chip'=2] {'chip'}, dimensions={0} | all-to-all | bytes 8388608 | tf_op jit(solution)/shard_map/all_to_all | solution.py:436
  137.4 11.4 %shard_map.238 = (bf16[1024,2048]{1,0:T(8,128)(2,1)}, f32[1024,768]{1,0:T(8,128)}, bf16[32,64,768]{2,1,0:T(8,128)(2,1)}) custom-call(s32[6]{0:T(128)} %stack.295.where, bf16[1024,2048]{1,0:T(8,128)(2,1)} %bitcast.257, f32[1,2048]{1,0:T(1,128)} %slice.166.gain, bf16[8,64,768]{2,1,0:T(8,128)(2,1)} %pad_maximum_fusion.13.rest_0_, ...), custom_call_target="tpu_custom_call" | custom-call | flops 402653184 | bytes 2229251 | tf_op jit(solution)/shard_map/pallas_call | solution.py:65
  160.5 9.6 %shard_map.239 = (f32[2,2,128,128]{3,2,1,0:T(8,128)}, f32[2,2,128,128]{3,2,1,0:T(8,128)}, f32[2,2,512,128]{3,2,1,0:T(8,128)}, bf16[2,2,512,128]{3,2,1,0:T(8,128)...) custom-call(s32[6]{0:T(128)} %stack.295.where, f32[2,2,2,128,768]{4,3,2,1,0:T(8,128)} %bitcast.251, ...), custom_call_target="tpu_custom_call" | custom-call | flops 268435456 | bytes 1869955 | tf_op jit(solution)/shard_map/pallas_call | solution.py:65
  170.1 24.5 %collective-permute-done.27 = bf16[4,64,1408]{2,1,0:T(8,128)(2,1)S(1)} collective-permute-done((bf16[4,64,1408]{2,1,0:T(8,128)(2,1)S(1)}, bf16[4,64,1408]{2,1,0:T(8,128)(2,1)S(1)}, u32[]{:S(2)}, u32[]{:S(2)}) %collective-permute-start.27) | collective-permute-done | bytes 720928 | tf_op jit(solution)/shard_map/ppermute | solution.py:439
  223.7 19.6 %collective-permute-done.29 = bf16[176,2048]{1,0:T(8,128)(2,1)S(1)} collective-permute-done((bf16[176,2048]{1,0:T(8,128)(2,1)S(1)}, bf16[176,2048]{1,0:T(8,128)(2,1)S(1)}, u32[]{:S(2)}, u32[]{:S(2)}) %collective-permute-start.29) | collective-permute-done | bytes 720928 | tf_op jit(solution)/shard_map/ppermute | solution.py:439
  249.3 5.6 all-to-all-start.4
  263.5 10.2 %shard_map.241 = (f32[128,2048]{1,0:T(8,128)}, bf16[4,2,128,256]{3,2,1,0:T(8,128)(2,1)}, f32[128,2048]{1,0:T(8,128)}, bf16[128,2048]{1,0:T(8,128)(2,1)}, bf16[32,64,2048]{2,1,0:T(8,128)(2,1)}) custom-call(s32[6]{0:T(128)} %stack.295.where, bf16[128,2048]{1,0:T(8,128)(2,1)} %tokens.1, f32[1,2048]{1,0:T(1,128)} %slice.162.gain_state, ...), custom_call_target="tpu_custom_call" | custom-call | flops 134217728 | bytes 2623491 | tf_op jit(solution)/shard_map/pallas_call | solution.py:65
  277.9 16.6 %collective-permute-done.39 = bf16[2,176,2048]{2,1,0:T(8,128)(2,1)S(1)} collective-permute-done((bf16[2,176,2048]{2,1,0:T(8,128)(2,1)}, bf16[2,176,2048]{2,1,0:T(8,128)(2,1)S(1)}, u32[]{:S(2)}, u32[]{:S(2)}) %collective-permute-start.39) | collective-permute-done | bytes 1441824 | tf_op jit(solution)/shard_map/ppermute | solution.py:439
  299.9 8.4 %all_to_all.72 = bf16[2,512,2048]{2,1,0:T(8,128)(2,1)} all-to-all(bf16[2,512,2048]{2,1,0:T(8,128)(2,1)S(1)} %pad_maximum_fusion.3), channel_id=1, replica_groups=mesh['y'=2,'x'=2,'h'=2,'l'=2,'chip'=2] {'chip'}, dimensions={0} | all-to-all | bytes 8388608 | tf_op jit(solution)/shard_map/all_to_all | solution.py:436
  311.9 28.0 %shard_map.242 = (bf16[1024,704]{1,0:T(8,128)(2,1)}, bf16[1024,1408]{1,0:T(8,128)(2,1)}, bf16[1024,2048]{1,0:T(8,128)(2,1)}, bf16[1024,2048]{1,0:T(8,128)(2,1)}) custom-call(s32[6]{0:T(128)} %stack.295.where, bf16[1024,2048]{1,0:T(8,128)(2,1)} %bitcast.246, bf16[1024,2048]{1,0:T(8,128)(2,1)} %bitcast.79.cotangent.right, bf16[704,2048]{1,0:T(8,128)(2,1)} %bitcast.260, ...), custom_call_target="tpu_custom_call" | custom-call | flops 2583691264 | bytes 3719171 | tf_op jit(solution)/shard_map/pallas_call | solution.py:65
  339.9 8.5 %all_to_all.73 = bf16[2,4,128,2048]{3,2,1,0:T(8,128)(2,1)S(1)} all-to-all(bf16[2,4,128,2048]{3,2,1,0:T(8,128)(2,1)} %bitcast.275), channel_id=1, replica_groups=mesh['y'=2,'x'=2,'h'=2,'l'=2,'chip'=2] {'chip'}, dimensions={0} | all-to-all | bytes 8388608 | tf_op jit(solution)/shard_map/all_to_all | solution.py:436
  350.0 6.0 shard_map.243
  360.2 7.5 %shard_map.246 = bf16[704,2048]{1,0:T(8,128)(2,1)} custom-call(bf16[1024,704]{1,0:T(8,128)(2,1)} %get-tuple-element.285.left, bf16[1024,2048]{1,0:T(8,128)(2,1)} %bitcast.79.cotangent.right), custom_call_target="tpu_custom_call" | custom-call | flops 369098752 | bytes 1064960 | tf_op jit(solution)/shard_map/pallas_call | solution.py:65
  367.7 5.8 all-to-all-start.7
  373.5 6.0 shard_map.245
  379.6 6.5 shard_map.244
  394.2 8.7 %shard_map.248 = (f32[128,2048]{1,0:T(8,128)}, bf16[128,2048]{1,0:T(8,128)(2,1)}, bf16[4,2,128,256]{3,2,1,0:T(8,128)(2,1)}) custom-call(s32[6]{0:T(128)} %stack.295.where, f32[128,2048]{1,0:T(8,128)} %convert_add_fusion.6.upstream, bf16[128,2048]{1,0:T(8,128)(2,1)} %cotangent, f32[128,2048]{1,0:T(8,128)} %get-tuple-element.293.residual, ...), custom_call_target="tpu_custom_call" | custom-call | flops 134217728 | bytes 1771523 | tf_op jit(solution)/shard_map/pallas_call | solution.py:65
  421.5 6.5 shard_map.247
  444.2 10.5 %collective-permute-done.54 = bf16[128,2048]{1,0:T(8,128)(2,1)} collective-permute-done((bf16[128,2048]{1,0:T(8,128)(2,1)}, bf16[128,2048]{1,0:T(8,128)(2,1)}, u32[]{:S(2)}, u32[]{:S(2)}) %collective-permute-start.54) | collective-permute-done | bytes 524320 | tf_op jit(solution)/shard_map/ppermute | solution.py:429
  464.4 7.5 %collective-permute-done.55.next_grad = bf16[2,2,128,128]{3,2,1,0:T(8,128)(2,1)S(1)} collective-permute-done((bf16[2,2,128,128]{3,2,1,0:T(8,128)(2,1)S(1)}, bf16[2,2,128,128]{3,2,1,0:T(8,128)(2,1)S(1)}, u32[]{:S(2)}, u32[]{:S(2)}) %collective-permute-start.55) | collective-permute-done | bytes 131104 | tf_op jit(solution)/shard_map/ppermute | solution.py:600
  472.6 10.4 %shard_map.250 = (bf16[2,2,2,128,256]{4,3,2,1,0:T(8,128)(2,1)}, bf16[2,2,2,128,256]{4,3,2,1,0:T(8,128)(2,1)}, bf16[2,2,2,128,256]{4,3,2,1,0:T(8,128)(2,1)}, f32[2,2,8,128]{3,2,1,0:T(8,128)}) custom-call(s32[6]{0:T(128)} %stack.295.where, f32[2,2,2,128,768]{4,3,2,1,0:T(8,128)} %bitcast.254, f32[2,2,2,128,768]{4,3,2,1,0:T(8,128)} %bitcast.255, ...), custom_call_target="tpu_custom_call" | custom-call | flops 402653184 | bytes 1937539 | tf_op jit(solution)/shard_map/pallas_call | solution.py:65
  483.0 5.7 shard_map.251
  494.8 7.9 %shard_map.252 = bf16[1024,2048]{1,0:T(8,128)(2,1)} custom-call(bf16[1024,256]{1,0:T(8,128)(2,1)} %bitcast.266, bf16[1024,256]{1,0:T(8,128)(2,1)} %bitcast.269, bf16[1024,256]{1,0:T(8,128)(2,1)} %bitcast.272, bf16[32,64,768]{2,1,0:T(8,128)(2,1)} %get-tuple-element.325.weight), custom_call_target="tpu_custom_call" | custom-call | flops 402653184 | bytes 1114112 | tf_op jit(solution)/shard_map/pallas_call | solution.py:65
  502.7 8.5 %all_to_all.75 = bf16[2,4,128,2048]{3,2,1,0:T(8,128)(2,1)S(1)} all-to-all(bf16[2,4,128,2048]{3,2,1,0:T(8,128)(2,1)} %bitcast.259), channel_id=1, replica_groups=mesh['y'=2,'x'=2,'h'=2,'l'=2,'chip'=2] {'chip'}, dimensions={0} | all-to-all | bytes 8388608 | tf_op jit(solution)/shard_map/all_to_all | solution.py:436
  513.2 6.2 shard_map.253
  538.8 8.3 %all_to_all.76 = bf16[2,512,2048]{2,1,0:T(8,128)(2,1)} all-to-all(bf16[2,512,2048]{2,1,0:T(8,128)(2,1)S(1)} %pad_maximum_fusion.4), channel_id=1, replica_groups=mesh['y'=2,'x'=2,'h'=2,'l'=2,'chip'=2] {'chip'}, dimensions={0} | all-to-all | bytes 8388608 | tf_op jit(solution)/shard_map/all_to_all | solution.py:436
  551.8 10.1 %collective-permute-done.62 = bf16[128,2048]{1,0:T(8,128)(2,1)} collective-permute-done((bf16[128,2048]{1,0:T(8,128)(2,1)}, bf16[128,2048]{1,0:T(8,128)(2,1)}, u32[]{:S(2)}, u32[]{:S(2)}) %collective-permute-start.62) | collective-permute-done | bytes 524320 | tf_op jit(solution)/shard_map/ppermute | solution.py:429
  561.9 10.9 %collective-permute-done.64 = bf16[128,2048]{1,0:T(8,128)(2,1)} collective-permute-done((bf16[128,2048]{1,0:T(8,128)(2,1)}, bf16[128,2048]{1,0:T(8,128)(2,1)}, u32[]{:S(2)}, u32[]{:S(2)}) %collective-permute-start.64) | collective-permute-done | bytes 524320 | tf_op jit(solution)/shard_map/ppermute | solution.py:429
  583.2 16.1 %collective-permute-done.66 = bf16[2,64,1408]{2,1,0:T(8,128)(2,1)S(1)} collective-permute-done((bf16[2,64,1408]{2,1,0:T(8,128)(2,1)S(1)}, bf16[2,64,1408]{2,1,0:T(8,128)(2,1)S(1)}, u32[]{:S(2)}, u32[]{:S(2)}) %collective-permute-start.66) | collective-permute-done | bytes 360480 | tf_op jit(solution)/shard_map/ppermute | solution.py:429
  650.3 7.3 %collective-permute-done.77 = f32[64]{0:T(128)S(1)} collective-permute-done((f32[64]{0:T(128)S(1)}, f32[64]{0:T(128)S(1)}, u32[]{:S(2)}, u32[]{:S(2)}) %collective-permute-start.77) | collective-permute-done | bytes 288 | tf_op jit(solution)/shard_map/ppermute | solution.py:779
  (377 shorter events, 315.0 us)
Async XLA Ops:
  47.2 36.9 %collective-permute-start.11 = (bf16[8,64,768]{2,1,0:T(8,128)(2,1)}, bf16[8,64,768]{2,1,0:T(8,128)(2,1)S(1)}, u32[]{:S(2)}, u32[]{:S(2)}) collective-permute-start(bf16[8,64,768]{2,1,0:T(8,128)(2,1)} %pad_maximum_fusion.13.rest_0_), channel_id=1, source_target_pairs={{0,4},{4,0},{1,5},{5,1},{2,6},{6,2},{3,7},{7,3},{8,12},{12,8},{9,1... | collective-permute-start | bytes 2359304 | tf_op jit(solution)/shard_map/ppermute | solution.py:439
  49.8 47.6 %collective-permute-start.14 = (bf16[256,2048]{1,0:T(8,128)(2,1)S(1)}, bf16[256,2048]{1,0:T(8,128)(2,1)S(1)}, u32[]{:S(2)}, u32[]{:S(2)}) collective-permute-start(bf16[256,2048]{1,0:T(8,128)(2,1)S(1)} %pad_maximum_fusion.9), channel_id=1, source_target_pairs={{0,8},{8,0},{1,9},{9,1},{2,10},{10,2},{3,11},{11,3},{4,12},{12,4},... | collective-permute-start | bytes 3145736 | tf_op jit(solution)/shard_map/ppermute | solution.py:433
  51.2 38.2 %collective-permute-start.16 = (bf16[2,64,1408]{2,1,0:T(8,128)(2,1)S(1)}, bf16[2,64,1408]{2,1,0:T(8,128)(2,1)S(1)}, u32[]{:S(2)}, u32[]{:S(2)}) collective-permute-start(bf16[2,64,1408]{2,1,0:T(8,128)(2,1)S(1)} %get-tuple-element.385), channel_id=1, source_target_pairs={{0,8},{2,10},{8,0},{10,2},{1,9},{3,11},{9,1},{11,3},{4,12},{6,14},... | collective-permute-start | bytes 1081352 | tf_op jit(solution)/shard_map/ppermute | solution.py:429
  52.0 37.7 %collective-permute-start.17 = (bf16[2,64,1408]{2,1,0:T(8,128)(2,1)S(1)}, bf16[2,64,1408]{2,1,0:T(8,128)(2,1)S(1)}, u32[]{:S(2)}, u32[]{:S(2)}) collective-permute-start(bf16[2,64,1408]{2,1,0:T(8,128)(2,1)S(1)} %get-tuple-element.386), channel_id=1, source_target_pairs={{0,10},{2,8},{8,2},{10,0},{1,11},{3,9},{9,3},{11,1},{4,14},{6,12},... | collective-permute-start | bytes 1081352 | tf_op jit(solution)/shard_map/ppermute | solution.py:429
  53.8 43.6 %collective-permute-start.12 = (bf16[8,64,768]{2,1,0:T(8,128)(2,1)}, bf16[8,64,768]{2,1,0:T(8,128)(2,1)S(1)}, u32[]{:S(2)}, u32[]{:S(2)}) collective-permute-start(bf16[8,64,768]{2,1,0:T(8,128)(2,1)} %pad_maximum_fusion.13.rest_0_), channel_id=1, source_target_pairs={{0,16},{16,0},{1,17},{17,1},{2,18},{18,2},{3,19},{19,3},{4,20},{20... | collective-permute-start | bytes 2359304 | tf_op jit(solution)/shard_map/ppermute | solution.py:439
  115.8 33.0 %collective-permute-start.22 = (bf16[4,64,1408]{2,1,0:T(8,128)(2,1)S(1)}, bf16[4,64,1408]{2,1,0:T(8,128)(2,1)}, u32[]{:S(2)}, u32[]{:S(2)}) collective-permute-start(bf16[4,64,1408]{2,1,0:T(8,128)(2,1)S(1)} %pad_maximum_fusion.15), channel_id=1, source_target_pairs={{0,4},{4,0},{1,5},{5,1},{2,6},{6,2},{3,7},{7,3},{8,12},{12,8},{9,1... | collective-permute-start | bytes 2162696 | tf_op jit(solution)/shard_map/ppermute | solution.py:439
  153.1 43.6 %collective-permute-start.25 = (bf16[2,2,64,2048]{3,2,1,0:T(8,128)(2,1)S(1)}, bf16[2,2,64,2048]{3,2,1,0:T(8,128)(2,1)}, u32[]{:S(2)}, u32[]{:S(2)}) collective-permute-start(bf16[2,2,64,2048]{3,2,1,0:T(8,128)(2,1)S(1)} %get-tuple-element.390), channel_id=1, source_target_pairs={{0,8},{8,0},{1,9},{9,1},{2,10},{10,2},{3,11},{11,3},{4,12},{12,4},... | collective-permute-start | bytes 3145736 | tf_op jit(solution)/shard_map/ppermute | solution.py:433
  153.8 46.9 %collective-permute-start.24 = (bf16[2,4,64,1408]{3,2,1,0:T(8,128)(2,1)S(1)}, bf16[2,4,64,1408]{3,2,1,0:T(8,128)(2,1)}, u32[]{:S(2)}, u32[]{:S(2)}) collective-permute-start(bf16[2,4,64,1408]{3,2,1,0:T(8,128)(2,1)S(1)} %pad_maximum_fusion.5.rest_0_), channel_id=1, source_target_pairs={{0,16},{16,0},{1,17},{17,1},{2,18},{18,2},{3,19},{19,3},{4,20},{20... | collective-permute-start | bytes 4325384 | tf_op jit(solution)/shard_map/ppermute | solution.py:439
  156.5 40.4 %collective-permute-start.26 = (bf16[2,2,64,2048]{3,2,1,0:T(8,128)(2,1)}, bf16[2,2,64,2048]{3,2,1,0:T(8,128)(2,1)}, u32[]{:S(2)}, u32[]{:S(2)}) collective-permute-start(bf16[2,2,64,2048]{3,2,1,0:T(8,128)(2,1)} %get-tuple-element.392), channel_id=1, source_target_pairs={{0,2},{2,0},{1,3},{3,1},{4,6},{6,4},{5,7},{7,5},{8,10},{10,8},{9,1... | collective-permute-start | bytes 3145736 | tf_op jit(solution)/shard_map/ppermute | solution.py:433
  156.5 38.1 %collective-permute-start.27 = (bf16[4,64,1408]{2,1,0:T(8,128)(2,1)S(1)}, bf16[4,64,1408]{2,1,0:T(8,128)(2,1)S(1)}, u32[]{:S(2)}, u32[]{:S(2)}) collective-permute-start(bf16[4,64,1408]{2,1,0:T(8,128)(2,1)S(1)} %pad_maximum_fusion.16), channel_id=1, source_target_pairs={{0,4},{4,0},{1,5},{5,1},{2,6},{6,2},{3,7},{7,3},{8,12},{12,8},{9,1... | collective-permute-start | bytes 2162696 | tf_op jit(solution)/shard_map/ppermute | solution.py:439
  200.7 58.7 %collective-permute-start.34 = (bf16[4,2,2,64,2048]{4,3,2,1,0:T(8,128)(2,1)}, bf16[4,2,2,64,2048]{4,3,2,1,0:T(8,128)(2,1)}, u32[]{:S(2)}, u32[]{:S(2)}) collective-permute-start(bf16[4,2,2,64,2048]{4,3,2,1,0:T(8,128)(2,1)} %pad_maximum_fusion.1.rest_4_), channel_id=1, source_target_pairs={{0,1},{1,0},{2,3},{3,2},{4,5},{5,4},{6,7},{7,6},{8,9},{9,8},{10,11... | collective-permute-start | bytes 12582920 | tf_op jit(solution)/shard_map/ppermute | solution.py:614
  200.7 43.4 %collective-permute-start.35 = (bf16[256,2048]{1,0:T(8,128)(2,1)S(1)}, bf16[256,2048]{1,0:T(8,128)(2,1)S(1)}, u32[]{:S(2)}, u32[]{:S(2)}) collective-permute-start(bf16[256,2048]{1,0:T(8,128)(2,1)S(1)} %pad_maximum_fusion.10), channel_id=1, source_target_pairs={{0,8},{8,0},{1,9},{9,1},{2,10},{10,2},{3,11},{11,3},{4,12},{12,4},... | collective-permute-start | bytes 3145736 | tf_op jit(solution)/shard_map/ppermute | solution.py:433
  207.6 51.9 %collective-permute-start.33 = (bf16[2,4,64,1408]{3,2,1,0:T(8,128)(2,1)S(1)}, bf16[2,4,64,1408]{3,2,1,0:T(8,128)(2,1)}, u32[]{:S(2)}, u32[]{:S(2)}) collective-permute-start(bf16[2,4,64,1408]{3,2,1,0:T(8,128)(2,1)S(1)} %pad_maximum_fusion.6.rest_2_), channel_id=1, source_target_pairs={{0,16},{16,0},{1,17},{17,1},{2,18},{18,2},{3,19},{19,3},{4,20},{20... | collective-permute-start | bytes 4325384 | tf_op jit(solution)/shard_map/ppermute | solution.py:439
  210.6 32.7 %collective-permute-start.29 = (bf16[176,2048]{1,0:T(8,128)(2,1)S(1)}, bf16[176,2048]{1,0:T(8,128)(2,1)S(1)}, u32[]{:S(2)}, u32[]{:S(2)}) collective-permute-start(bf16[176,2048]{1,0:T(8,128)(2,1)S(1)} %copy-done.12), channel_id=1, source_target_pairs={{0,4},{4,0},{1,5},{5,1},{2,6},{6,2},{3,7},{7,3},{8,12},{12,8},{9,1... | collective-permute-start | bytes 2162696 | tf_op jit(solution)/shard_map/ppermute | solution.py:439
  260.7 33.8 %collective-permute-start.39 = (bf16[2,176,2048]{2,1,0:T(8,128)(2,1)}, bf16[2,176,2048]{2,1,0:T(8,128)(2,1)S(1)}, u32[]{:S(2)}, u32[]{:S(2)}) collective-permute-start(bf16[2,176,2048]{2,1,0:T(8,128)(2,1)} %pad_maximum_fusion.7), channel_id=1, source_target_pairs={{0,16},{16,0},{1,17},{17,1},{2,18},{18,2},{3,19},{19,3},{4,20},{20... | collective-permute-start | bytes 4325384 | tf_op jit(solution)/shard_map/ppermute | solution.py:439
  308.4 47.7 %collective-permute-start.42 = (bf16[2,128,256]{2,1,0:T(8,128)(2,1)S(1)}, bf16[2,128,256]{2,1,0:T(8,128)(2,1)S(1)}, u32[]{:S(2)}, u32[]{:S(2)}) collective-permute-start(bf16[2,128,256]{2,1,0:T(8,128)(2,1)S(1)} %get-tuple-element.408), channel_id=1, source_target_pairs={{0,10},{2,8},{8,2},{10,0},{1,11},{3,9},{9,3},{11,1},{4,14},{6,12},... | collective-permute-start | bytes 393224 | tf_op jit(solution)/shard_map/ppermute | solution.py:429
  309.3 46.7 %collective-permute-start.41 = (bf16[2,128,256]{2,1,0:T(8,128)(2,1)S(1)}, bf16[2,128,256]{2,1,0:T(8,128)(2,1)S(1)}, u32[]{:S(2)}, u32[]{:S(2)}) collective-permute-start(bf16[2,128,256]{2,1,0:T(8,128)(2,1)S(1)} %get-tuple-element.409), channel_id=1, source_target_pairs={{0,8},{2,10},{8,0},{10,2},{1,9},{3,11},{9,1},{11,3},{4,12},{6,14},... | collective-permute-start | bytes 393224 | tf_op jit(solution)/shard_map/ppermute | solution.py:429
  310.5 45.6 %collective-permute-start.40 = (bf16[2,128,256]{2,1,0:T(8,128)(2,1)S(1)}, bf16[2,128,256]{2,1,0:T(8,128)(2,1)S(1)}, u32[]{:S(2)}, u32[]{:S(2)}) collective-permute-start(bf16[2,128,256]{2,1,0:T(8,128)(2,1)S(1)} %get-tuple-element.410), channel_id=1, source_target_pairs={{0,2},{2,0},{8,10},{10,8},{1,3},{3,1},{9,11},{11,9},{4,6},{6,4},{1... | collective-permute-start | bytes 393224 | tf_op jit(solution)/shard_map/ppermute | solution.py:429
  356.1 35.4 %collective-permute-start.43 = (bf16[2,1,256,1408]{3,2,1,0:T(8,128)(2,1)}, bf16[2,1,256,1408]{3,2,1,0:T(8,128)(2,1)}, u32[]{:S(2)}, u32[]{:S(2)}) collective-permute-start(bf16[2,1,256,1408]{3,2,1,0:T(8,128)(2,1)} %shard_map.243), channel_id=1, source_target_pairs={{0,16},{16,0},{1,17},{17,1},{2,18},{18,2},{3,19},{19,3},{4,20},{20... | collective-permute-start | bytes 4325384 | tf_op jit(solution)/shard_map/ppermute | solution.py:439
  356.7 33.6 %collective-permute-start.44 = (bf16[128,2048]{1,0:T(8,128)(2,1)}, bf16[128,2048]{1,0:T(8,128)(2,1)S(1)}, u32[]{:S(2)}, u32[]{:S(2)}) collective-permute-start(bf16[128,2048]{1,0:T(8,128)(2,1)} %get-tuple-element.282), channel_id=1, source_target_pairs={{0,2},{2,0},{8,10},{10,8},{1,3},{3,1},{9,11},{11,9},{4,6},{6,4},{1... | collective-permute-start | bytes 1572872 | tf_op jit(solution)/shard_map/ppermute | solution.py:429
  357.3 33.0 %collective-permute-start.45 = (bf16[128,2048]{1,0:T(8,128)(2,1)}, bf16[128,2048]{1,0:T(8,128)(2,1)S(1)}, u32[]{:S(2)}, u32[]{:S(2)}) collective-permute-start(bf16[128,2048]{1,0:T(8,128)(2,1)} %get-tuple-element.283), channel_id=1, source_target_pairs={{0,8},{2,10},{8,0},{10,2},{1,9},{3,11},{9,1},{11,3},{4,12},{6,14},... | collective-permute-start | bytes 1572872 | tf_op jit(solution)/shard_map/ppermute | solution.py:429
  415.2 39.4 %collective-permute-start.54 = (bf16[128,2048]{1,0:T(8,128)(2,1)}, bf16[128,2048]{1,0:T(8,128)(2,1)}, u32[]{:S(2)}, u32[]{:S(2)}) collective-permute-start(bf16[128,2048]{1,0:T(8,128)(2,1)} %get-tuple-element.307), channel_id=1, source_target_pairs={{0,10},{2,8},{8,2},{10,0},{1,11},{3,9},{9,3},{11,1},{4,14},{6,12},... | collective-permute-start | bytes 1572872 | tf_op jit(solution)/shard_map/ppermute | solution.py:429
  417.0 42.8 %collective-permute-start.47 = (bf16[2,1,256,1408]{3,2,1,0:T(8,128)(2,1)}, bf16[2,1,256,1408]{3,2,1,0:T(8,128)(2,1)}, u32[]{:S(2)}, u32[]{:S(2)}) collective-permute-start(bf16[2,1,256,1408]{3,2,1,0:T(8,128)(2,1)} %shard_map.245), channel_id=1, source_target_pairs={{0,16},{16,0},{1,17},{17,1},{2,18},{18,2},{3,19},{19,3},{4,20},{20... | collective-permute-start | bytes 4325384 | tf_op jit(solution)/shard_map/ppermute | solution.py:439
  419.5 38.2 %collective-permute-start.51 = (bf16[1,256,1408]{2,1,0:T(8,128)(2,1)}, bf16[1,256,1408]{2,1,0:T(8,128)(2,1)}, u32[]{:S(2)}, u32[]{:S(2)}) collective-permute-start(bf16[1,256,1408]{2,1,0:T(8,128)(2,1)} %fusion.5), channel_id=1, source_target_pairs={{0,4},{4,0},{1,5},{5,1},{2,6},{6,2},{3,7},{7,3},{8,12},{12,8},{9,1... | collective-permute-start | bytes 2162696 | tf_op jit(solution)/shard_map/ppermute | solution.py:439
  488.8 36.2 %collective-permute-start.56 = (bf16[2,2,256,768]{3,2,1,0:T(8,128)(2,1)}, bf16[2,2,256,768]{3,2,1,0:T(8,128)(2,1)}, u32[]{:S(2)}, u32[]{:S(2)}) collective-permute-start(bf16[2,2,256,768]{3,2,1,0:T(8,128)(2,1)} %shard_map.251), channel_id=1, source_target_pairs={{0,16},{16,0},{1,17},{17,1},{2,18},{18,2},{3,19},{19,3},{4,20},{20... | collective-permute-start | bytes 4718600 | tf_op jit(solution)/shard_map/ppermute | solution.py:439
  491.3 36.4 %collective-permute-start.59 = (bf16[128,2048]{1,0:T(8,128)(2,1)S(1)}, bf16[128,2048]{1,0:T(8,128)(2,1)}, u32[]{:S(2)}, u32[]{:S(2)}) collective-permute-start(bf16[128,2048]{1,0:T(8,128)(2,1)S(1)} %copy-done.28), channel_id=1, source_target_pairs={{0,10},{2,8},{8,2},{10,0},{1,11},{3,9},{9,3},{11,1},{4,14},{6,12},... | collective-permute-start | bytes 1572872 | tf_op jit(solution)/shard_map/ppermute | solution.py:429
  491.3 36.3 %collective-permute-start.58 = (bf16[128,2048]{1,0:T(8,128)(2,1)S(1)}, bf16[128,2048]{1,0:T(8,128)(2,1)}, u32[]{:S(2)}, u32[]{:S(2)}) collective-permute-start(bf16[128,2048]{1,0:T(8,128)(2,1)S(1)} %copy-done.28), channel_id=1, source_target_pairs={{0,8},{2,10},{8,0},{10,2},{1,9},{3,11},{9,1},{11,3},{4,12},{6,14},... | collective-permute-start | bytes 1572872 | tf_op jit(solution)/shard_map/ppermute | solution.py:429
  492.3 39.3 %collective-permute-start.57 = (bf16[128,2048]{1,0:T(8,128)(2,1)S(1)}, bf16[128,2048]{1,0:T(8,128)(2,1)}, u32[]{:S(2)}, u32[]{:S(2)}) collective-permute-start(bf16[128,2048]{1,0:T(8,128)(2,1)S(1)} %copy-done.28), channel_id=1, source_target_pairs={{0,2},{2,0},{8,10},{10,8},{1,3},{3,1},{9,11},{11,9},{4,6},{6,4},{1... | collective-permute-start | bytes 1572872 | tf_op jit(solution)/shard_map/ppermute | solution.py:429
  532.7 40.2 %collective-permute-start.64 = (bf16[128,2048]{1,0:T(8,128)(2,1)}, bf16[128,2048]{1,0:T(8,128)(2,1)}, u32[]{:S(2)}, u32[]{:S(2)}) collective-permute-start(bf16[128,2048]{1,0:T(8,128)(2,1)} %get-tuple-element.338), channel_id=1, source_target_pairs={{0,10},{2,8},{8,2},{10,0},{1,11},{3,9},{9,3},{11,1},{4,14},{6,12},... | collective-permute-start | bytes 1572872 | tf_op jit(solution)/shard_map/ppermute | solution.py:429
  536.3 39.6 %collective-permute-start.65 = (bf16[2,176,2048]{2,1,0:T(8,128)(2,1)}, bf16[2,176,2048]{2,1,0:T(8,128)(2,1)}, u32[]{:S(2)}, u32[]{:S(2)}) collective-permute-start(bf16[2,176,2048]{2,1,0:T(8,128)(2,1)} %dynamic-slice_bitcast_fusion), channel_id=1, source_target_pairs={{0,16},{16,0},{1,17},{17,1},{2,18},{18,2},{3,19},{19,3},{4,20},{20... | collective-permute-start | bytes 4325384 | tf_op jit(solution)/shard_map/ppermute | solution.py:439
  536.9 37.7 %collective-permute-start.61 = (bf16[2,256,768]{2,1,0:T(8,128)(2,1)S(1)}, bf16[2,256,768]{2,1,0:T(8,128)(2,1)}, u32[]{:S(2)}, u32[]{:S(2)}) collective-permute-start(bf16[2,256,768]{2,1,0:T(8,128)(2,1)S(1)} %fusion.4), channel_id=1, source_target_pairs={{0,4},{4,0},{1,5},{5,1},{2,6},{6,2},{3,7},{7,3},{8,12},{12,8},{9,1... | collective-permute-start | bytes 2359304 | tf_op jit(solution)/shard_map/ppermute | solution.py:439
  582.8 65.1 %collective-permute-start.78 = (bf16[176,2048]{1,0:T(8,128)(2,1)}, bf16[176,2048]{1,0:T(8,128)(2,1)}, u32[]{:S(2)}, u32[]{:S(2)}) collective-permute-start(bf16[176,2048]{1,0:T(8,128)(2,1)} %fusion.7), channel_id=1, source_target_pairs={{0,4},{4,0},{1,5},{5,1},{2,6},{6,2},{3,7},{7,3},{8,12},{12,8},{9,1... | collective-permute-start | bytes 2162696 | tf_op jit(solution)/shard_map/ppermute | solution.py:439
  (102 other events, 1367.6 us)

commit v5 on v4

--- a/solution.py
+++ b/solution.py
@@ -580,10 +580,10 @@
         flops=8 * mix_flops,
     )
     gu_first = turns(gu_first, "y", ny)
-    gu_second = jnp.stack(turns(gate_up[1], "h", nh))
+    gu_second = turns(gate_up[1], "h", nh)
     pairs = [jnp.stack([a, z]) for a, z in zip(pieces, moved)]
     moved = [swap(z, axis) for z, axis in zip(pairs, ("x", "l"))]
-    groups = jnp.stack([pairs[0], moved[0], pairs[1], moved[1]])
+    groups = [pairs[0], moved[0], pairs[1], moved[1]]
     out_names = [
         (t * 2 + distance, u, m, *names[t * cut + m], u * nl + distance if t else distance * nl + u)
         for t in range(2) for distance in range(2) for u in range(2) for m in range(cut)
@@ -602,6 +602,7 @@
         return incoming
 
     incoming = carry(end_state, 1)
+    groups, gu_second = (jnp.stack(z) for z in after((groups, gu_second), incoming))
     (mixed,) = call(
         mix_end_kernel, [shape(grouped, LOW)], local, query_reach, incoming,
         grid=(nx, heads), specs=[rows_spec, rows_spec, state_spec], out_specs=[piece(0)], flops=mix_flops // 4,
@@ -721,7 +722,7 @@
     pre_grads = [g.reshape(total, part) for g in (df, dv, dq)]
     three_sent = columns_grad(1, LOW, (0, 1), normed_in, pre_grads)
     (part_in,) = call(
-        inputs_grad_kernel, [shape((total, width), LOW)], *after(pre_grads, three_sent), w_three, flops=project_flops
+        inputs_grad_kernel, [shape((total, width), LOW)], *after(pre_grads, (three_sent, branch_pieces)), w_three, flops=project_flops
     )
     both_in = summed_core(part_in)
     three_kept = columns_kept((0, 1), normed_in, after(pre_grads, both_in))
@@ -747,11 +748,17 @@
     grad_output = scatter_y(*rows_of_y(grad_out.reshape(ny, nh, r, width)))
     gu_blocks = collect([z.astype(LOW).reshape(nl, nc, r, 2 * units) for z in (grad_gu_near, grad_gu_far)])
     three_blocks = collect([after(grad_three[t], gu_blocks) for t in range(nx)])
+    along = shape((r, HDIM))
+    grad_w_gate, grad_w_up, along_ffn = call(
+        partial(unpack_kernel, plan, ffr), [shape(w_gate.shape), shape(w_up.shape), along],
+        where, to_cores(gu_blocks), w_gate, w_up, specs=[SMEM] + [VMEM] * 3,
+        scratch=[pltpu.VMEM((nc, plane, r, 2 * units), LOW)],
+    )
     grad_down = scatter_h(grad_down)
     lower_grad = jnp.sum(lower_grad[:, :, 0], axis=0).reshape(1, part)
     lower_grad = sum(turns(after(lower_grad, grad_output), "y", ny))
-    three_blocks, grad_output, gu_blocks, lower_grad = fence(
-        three_blocks, grad_output, gu_blocks, lower_grad
+    three_blocks, grad_output, lower_grad, grad_w_gate, grad_w_up, along_ffn = fence(
+        three_blocks, grad_output, lower_grad, grad_w_gate, grad_w_up, along_ffn
     )
 
     grad_output = scatter_h(grad_output)
@@ -764,12 +771,6 @@
                     for e in range(nc):
                         owners.append(((p * nl + o) * nc + e) * copies + j * nh + i)
     pairs = list(enumerate(owners))
-    along = shape((r, HDIM))
-    grad_w_gate, grad_w_up, along_ffn = call(
-        partial(unpack_kernel, plan, ffr), [shape(w_gate.shape), shape(w_up.shape), along],
-        where, to_cores(gu_blocks), w_gate, w_up, specs=[SMEM] + [VMEM] * 3,
-        scratch=[pltpu.VMEM((nc, plane, r, 2 * units), LOW)],
-    )
     grad_w_forget, grad_w_input, grad_w_query, along_mix = call(
         partial(unpack_part_kernel, plan, part), [shape(w_query.shape)] * 3 + [along],
         where, to_cores(three_blocks), w_forget, w_input, w_query, specs=[SMEM] + [VMEM] * 4,

time: 668 us -> 664 us (level)
  waiting for transfers between devices: 226 us -> 219 us
    ppermute x39, waiting for transfers between devices: 99 us -> 87.3 us  [from_plane(): lax.ppermute(blocks[k], ('x', 'l'), [(i, i ^ k) for i in range(plane)])]
    ppermute x26, waiting for transfers between devices: 105 us -> 111 us  [turn(): return lax.ppermute(x, axis, [(i, (i + 1) % n) for i in range(n)])]
    all_to_all x8 -> x9, blocking collectives: 57.6 us -> 63 us  [to_cores(): return lax.all_to_all(x, 'chip', 0, 0, tiled=True)]
    all_to_all x6 -> x5, starting transfers between devices: 26.6 us -> 22 us  [to_cores(): return lax.all_to_all(x, 'chip', 0, 0, tiled=True)]
  transfers between devices with their start and end apart: 85 -> 84, of which waited for: 37 -> 35; matrix products, arithmetic and copies ran while one was open for 11% -> 10% of each run, Pallas kernels for 19% -> 22%
where the time goes in v5:
time: 664 us; the launch traced here: 654 us
  waiting for transfers between devices  219 us (33%)
  Pallas kernels  153 us (23%)
  starting transfers between devices  121 us (18%)
  blocking collectives  63 us (9%)
  other arithmetic  62.1 us (9%)
  local copies, waits for them, and re-layouts  32.2 us (5%)
    pallas_call x20, Pallas kernels, call(): pl.pallas_call(kernel, out_shape=outs, grid=grid, in_specs=specs, out_spe...  153 us
    ppermute x26, waiting for transfers between devices, turn(): return lax.ppermute(x, axis, [(i, (i + 1) % n) for i in range(n)])  111 us
    ppermute x39, waiting for transfers between devices, from_plane(): lax.ppermute(blocks[k], ('x', 'l'), [(i, i ^ k) for i in range(plane)])  87.3 us
    all_to_all x9, blocking collectives, to_cores(): return lax.all_to_all(x, 'chip', 0, 0, tiled=True)  63 us
    ppermute x39, starting transfers between devices, from_plane(): lax.ppermute(blocks[k], ('x', 'l'), [(i, i ^ k) for i in range(plane)])  45.5 us
    ppermute x26, starting transfers between devices, turn(): return lax.ppermute(x, axis, [(i, (i + 1) % n) for i in range(n)])  32.9 us
    all_to_all x5, starting transfers between devices, to_cores(): return lax.all_to_all(x, 'chip', 0, 0, tiled=True)  22 us
  transfers between devices with their start and end apart: 84, of which 35 were waited for; matrix products, arithmetic and copies ran while one was open for 10% of the time, Pallas kernels for 22%

profile of v5, /device:TPU:2, one launch (start us, length us, event | category | flops | bytes accessed | tf_op | source)
XLA Modules:
  0.0 653.8 jit_solution(12485055394674799138)
XLA Ops:
  55.3 28.7 %collective-permute-done.11.rest_2_ = bf16[8,64,768]{2,1,0:T(8,128)(2,1)S(1)} collective-permute-done((bf16[8,64,768]{2,1,0:T(8,128)(2,1)}, bf16[8,64,768]{2,1,0:T(8,128)(2,1)S(1)}, u32[]{:S(2)}, u32[]{:S(2)}) %collective-permute-start.11) | collective-permute-done | bytes 786464 | tf_op jit(solution)/shard_map/ppermute | solution.py:439
  89.9 7.4 %collective-permute-done.15 = bf16[2,64,1408]{2,1,0:T(8,128)(2,1)S(1)} collective-permute-done((bf16[2,64,1408]{2,1,0:T(8,128)(2,1)S(1)}, bf16[2,64,1408]{2,1,0:T(8,128)(2,1)S(1)}, u32[]{:S(2)}, u32[]{:S(2)}) %collective-permute-start.15) | collective-permute-done | bytes 360480 | tf_op jit(solution)/shard_map/ppermute | solution.py:429
  128.9 8.1 %all_to_all.70 = bf16[2,512,2048]{2,1,0:T(8,128)(2,1)} all-to-all(bf16[2,512,2048]{2,1,0:T(8,128)(2,1)S(1)} %pad_maximum_fusion), channel_id=1, replica_groups=mesh['y'=2,'x'=2,'h'=2,'l'=2,'chip'=2] {'chip'}, dimensions={0} | all-to-all | bytes 8388608 | tf_op jit(solution)/shard_map/all_to_all | solution.py:436
  137.0 11.3 %shard_map.238 = (bf16[1024,2048]{1,0:T(8,128)(2,1)}, f32[1024,768]{1,0:T(8,128)}, bf16[32,64,768]{2,1,0:T(8,128)(2,1)}) custom-call(s32[6]{0:T(128)} %stack.295.where, bf16[1024,2048]{1,0:T(8,128)(2,1)} %bitcast.255, f32[1,2048]{1,0:T(1,128)} %slice.166.gain, bf16[8,64,768]{2,1,0:T(8,128)(2,1)} %pad_maximum_fusion.13.rest_0_, ...), custom_call_target="tpu_custom_call" | custom-call | flops 402653184 | bytes 2229251 | tf_op jit(solution)/shard_map/pallas_call | solution.py:65
  160.7 9.6 %shard_map.239 = (f32[2,2,128,128]{3,2,1,0:T(8,128)}, f32[2,2,128,128]{3,2,1,0:T(8,128)}, f32[2,2,512,128]{3,2,1,0:T(8,128)}, bf16[2,2,512,128]{3,2,1,0:T(8,128)...) custom-call(s32[6]{0:T(128)} %stack.295.where, f32[2,2,2,128,768]{4,3,2,1,0:T(8,128)} %bitcast.249, ...), custom_call_target="tpu_custom_call" | custom-call | flops 268435456 | bytes 1869955 | tf_op jit(solution)/shard_map/pallas_call | solution.py:65
  170.2 21.3 %collective-permute-done.27 = bf16[4,64,1408]{2,1,0:T(8,128)(2,1)} collective-permute-done((bf16[4,64,1408]{2,1,0:T(8,128)(2,1)S(1)}, bf16[4,64,1408]{2,1,0:T(8,128)(2,1)}, u32[]{:S(2)}, u32[]{:S(2)}) %collective-permute-start.27) | collective-permute-done | bytes 720928 | tf_op jit(solution)/shard_map/ppermute | solution.py:439
  220.5 21.9 %collective-permute-done.29 = bf16[176,2048]{1,0:T(8,128)(2,1)S(1)} collective-permute-done((bf16[176,2048]{1,0:T(8,128)(2,1)S(1)}, bf16[176,2048]{1,0:T(8,128)(2,1)S(1)}, u32[]{:S(2)}, u32[]{:S(2)}) %collective-permute-start.29) | collective-permute-done | bytes 720928 | tf_op jit(solution)/shard_map/ppermute | solution.py:439
  248.5 5.6 all-to-all-start.4
  261.8 10.2 %shard_map.241 = (f32[128,2048]{1,0:T(8,128)}, bf16[4,2,128,256]{3,2,1,0:T(8,128)(2,1)}, f32[128,2048]{1,0:T(8,128)}, bf16[128,2048]{1,0:T(8,128)(2,1)}, bf16[32,64,2048]{2,1,0:T(8,128)(2,1)}) custom-call(s32[6]{0:T(128)} %stack.295.where, bf16[128,2048]{1,0:T(8,128)(2,1)} %tokens.1, f32[1,2048]{1,0:T(1,128)} %slice.162.gain_state, ...), custom_call_target="tpu_custom_call" | custom-call | flops 134217728 | bytes 2623491 | tf_op jit(solution)/shard_map/pallas_call | solution.py:65
  276.1 17.5 %collective-permute-done.39 = bf16[2,176,2048]{2,1,0:T(8,128)(2,1)S(1)} collective-permute-done((bf16[2,176,2048]{2,1,0:T(8,128)(2,1)}, bf16[2,176,2048]{2,1,0:T(8,128)(2,1)S(1)}, u32[]{:S(2)}, u32[]{:S(2)}) %collective-permute-start.39) | collective-permute-done | bytes 1441824 | tf_op jit(solution)/shard_map/ppermute | solution.py:439
  298.7 8.3 %all_to_all.72 = bf16[2,512,2048]{2,1,0:T(8,128)(2,1)} all-to-all(bf16[2,512,2048]{2,1,0:T(8,128)(2,1)S(1)} %pad_maximum_fusion.3), channel_id=1, replica_groups=mesh['y'=2,'x'=2,'h'=2,'l'=2,'chip'=2] {'chip'}, dimensions={0} | all-to-all | bytes 8388608 | tf_op jit(solution)/shard_map/all_to_all | solution.py:436
  310.6 27.9 %shard_map.242 = (bf16[1024,704]{1,0:T(8,128)(2,1)}, bf16[1024,1408]{1,0:T(8,128)(2,1)}, bf16[1024,2048]{1,0:T(8,128)(2,1)}, bf16[1024,2048]{1,0:T(8,128)(2,1)}) custom-call(s32[6]{0:T(128)} %stack.295.where, bf16[1024,2048]{1,0:T(8,128)(2,1)} %bitcast.244, bf16[1024,2048]{1,0:T(8,128)(2,1)} %bitcast.79.cotangent.right, bf16[704,2048]{1,0:T(8,128)(2,1)} %bitcast.258, ...), custom_call_target="tpu_custom_call" | custom-call | flops 2583691264 | bytes 3719171 | tf_op jit(solution)/shard_map/pallas_call | solution.py:65
  338.5 8.5 %all_to_all.73 = bf16[2,4,128,2048]{3,2,1,0:T(8,128)(2,1)S(1)} all-to-all(bf16[2,4,128,2048]{3,2,1,0:T(8,128)(2,1)} %bitcast.273), channel_id=1, replica_groups=mesh['y'=2,'x'=2,'h'=2,'l'=2,'chip'=2] {'chip'}, dimensions={0} | all-to-all | bytes 8388608 | tf_op jit(solution)/shard_map/all_to_all | solution.py:436
  348.7 6.0 shard_map.243
  359.8 7.5 %shard_map.246 = bf16[704,2048]{1,0:T(8,128)(2,1)} custom-call(bf16[1024,704]{1,0:T(8,128)(2,1)} %get-tuple-element.307.left, bf16[1024,2048]{1,0:T(8,128)(2,1)} %bitcast.79.cotangent.right), custom_call_target="tpu_custom_call" | custom-call | flops 369098752 | bytes 1064960 | tf_op jit(solution)/shard_map/pallas_call | solution.py:65
  367.3 5.8 all-to-all-start.7
  373.0 6.0 shard_map.245
  379.1 6.5 shard_map.244
  393.7 8.7 %shard_map.248 = (f32[128,2048]{1,0:T(8,128)}, bf16[128,2048]{1,0:T(8,128)(2,1)}, bf16[4,2,128,256]{3,2,1,0:T(8,128)(2,1)}) custom-call(s32[6]{0:T(128)} %stack.295.where, f32[128,2048]{1,0:T(8,128)} %convert_add_fusion.6.upstream, bf16[128,2048]{1,0:T(8,128)(2,1)} %cotangent, f32[128,2048]{1,0:T(8,128)} %get-tuple-element.315.residual, ...), custom_call_target="tpu_custom_call" | custom-call | flops 134217728 | bytes 1771523 | tf_op jit(solution)/shard_map/pallas_call | solution.py:65
  420.5 6.6 %shard_map.247 = f32[2,1,256,1408]{3,2,1,0:T(8,128)} custom-call(s32[6]{0:T(128)} %stack.295.where, bf16[1024,2048]{1,0:T(8,128)(2,1)} %bitcast.248, bf16[1024,1408]{1,0:T(8,128)(2,1)} %get-tuple-element.313.rest_0_), custom_call_target="tpu_custom_call" | custom-call | flops 184549376 | bytes 1245187 | tf_op jit(solution)/shard_map/pallas_call | solution.py:65
  443.8 10.7 %collective-permute-done.54 = bf16[128,2048]{1,0:T(8,128)(2,1)} collective-permute-done((bf16[128,2048]{1,0:T(8,128)(2,1)}, bf16[128,2048]{1,0:T(8,128)(2,1)}, u32[]{:S(2)}, u32[]{:S(2)}) %collective-permute-start.54) | collective-permute-done | bytes 524320 | tf_op jit(solution)/shard_map/ppermute | solution.py:429
  473.1 10.4 %shard_map.250 = (bf16[2,2,2,128,256]{4,3,2,1,0:T(8,128)(2,1)}, bf16[2,2,2,128,256]{4,3,2,1,0:T(8,128)(2,1)}, bf16[2,2,2,128,256]{4,3,2,1,0:T(8,128)(2,1)}, f32[2,2,8,128]{3,2,1,0:T(8,128)}) custom-call(s32[6]{0:T(128)} %stack.295.where, f32[2,2,2,128,768]{4,3,2,1,0:T(8,128)} %bitcast.252, f32[2,2,2,128,768]{4,3,2,1,0:T(8,128)} %bitcast.253, ...), custom_call_target="tpu_custom_call" | custom-call | flops 402653184 | bytes 1937539 | tf_op jit(solution)/shard_map/pallas_call | solution.py:65
  483.4 5.7 shard_map.251
  492.2 7.9 %shard_map.252 = bf16[1024,2048]{1,0:T(8,128)(2,1)} custom-call(bf16[1024,256]{1,0:T(8,128)(2,1)} %bitcast.264, bf16[1024,256]{1,0:T(8,128)(2,1)} %bitcast.267, bf16[1024,256]{1,0:T(8,128)(2,1)} %bitcast.270, bf16[32,64,768]{2,1,0:T(8,128)(2,1)} %get-tuple-element.348.weight), custom_call_target="tpu_custom_call" | custom-call | flops 402653184 | bytes 1114112 | tf_op jit(solution)/shard_map/pallas_call | solution.py:65
  500.1 8.5 %all_to_all.75 = bf16[2,4,128,2048]{3,2,1,0:T(8,128)(2,1)S(1)} all-to-all(bf16[2,4,128,2048]{3,2,1,0:T(8,128)(2,1)} %bitcast.257), channel_id=1, replica_groups=mesh['y'=2,'x'=2,'h'=2,'l'=2,'chip'=2] {'chip'}, dimensions={0} | all-to-all | bytes 8388608 | tf_op jit(solution)/shard_map/all_to_all | solution.py:436
  510.6 6.2 shard_map.253
  516.8 6.4 collective-permute-done.60
  536.4 8.4 %all_to_all.76 = bf16[2,512,2048]{2,1,0:T(8,128)(2,1)} all-to-all(bf16[2,512,2048]{2,1,0:T(8,128)(2,1)S(1)} %pad_maximum_fusion.4), channel_id=1, replica_groups=mesh['y'=2,'x'=2,'h'=2,'l'=2,'chip'=2] {'chip'}, dimensions={0} | all-to-all | bytes 8388608 | tf_op jit(solution)/shard_map/all_to_all | solution.py:436
  549.5 9.1 %collective-permute-done.62 = bf16[128,2048]{1,0:T(8,128)(2,1)S(1)} collective-permute-done((bf16[128,2048]{1,0:T(8,128)(2,1)}, bf16[128,2048]{1,0:T(8,128)(2,1)S(1)}, u32[]{:S(2)}, u32[]{:S(2)}) %collective-permute-start.62) | collective-permute-done | bytes 524320 | tf_op jit(solution)/shard_map/ppermute | solution.py:429
  560.2 8.8 %collective-permute-done.64 = bf16[128,2048]{1,0:T(8,128)(2,1)} collective-permute-done((bf16[128,2048]{1,0:T(8,128)(2,1)}, bf16[128,2048]{1,0:T(8,128)(2,1)}, u32[]{:S(2)}, u32[]{:S(2)}) %collective-permute-start.64) | collective-permute-done | bytes 524320 | tf_op jit(solution)/shard_map/ppermute | solution.py:429
  580.9 15.0 %collective-permute-done.66 = bf16[2,64,1408]{2,1,0:T(8,128)(2,1)S(1)} collective-permute-done((bf16[2,64,1408]{2,1,0:T(8,128)(2,1)S(1)}, bf16[2,64,1408]{2,1,0:T(8,128)(2,1)S(1)}, u32[]{:S(2)}, u32[]{:S(2)}) %collective-permute-start.66) | collective-permute-done | bytes 360480 | tf_op jit(solution)/shard_map/ppermute | solution.py:429
  607.8 5.7 all_to_all.77.blocks
  (374 shorter events, 315.3 us)
Async XLA Ops:
  47.2 36.9 %collective-permute-start.11 = (bf16[8,64,768]{2,1,0:T(8,128)(2,1)}, bf16[8,64,768]{2,1,0:T(8,128)(2,1)S(1)}, u32[]{:S(2)}, u32[]{:S(2)}) collective-permute-start(bf16[8,64,768]{2,1,0:T(8,128)(2,1)} %pad_maximum_fusion.13.rest_0_), channel_id=1, source_target_pairs={{0,4},{4,0},{1,5},{5,1},{2,6},{6,2},{3,7},{7,3},{8,12},{12,8},{9,1... | collective-permute-start | bytes 2359304 | tf_op jit(solution)/shard_map/ppermute | solution.py:439
  49.8 47.6 %collective-permute-start.14 = (bf16[256,2048]{1,0:T(8,128)(2,1)S(1)}, bf16[256,2048]{1,0:T(8,128)(2,1)S(1)}, u32[]{:S(2)}, u32[]{:S(2)}) collective-permute-start(bf16[256,2048]{1,0:T(8,128)(2,1)S(1)} %pad_maximum_fusion.9), channel_id=1, source_target_pairs={{0,8},{8,0},{1,9},{9,1},{2,10},{10,2},{3,11},{11,3},{4,12},{12,4},... | collective-permute-start | bytes 3145736 | tf_op jit(solution)/shard_map/ppermute | solution.py:433
  51.2 38.2 %collective-permute-start.16 = (bf16[2,64,1408]{2,1,0:T(8,128)(2,1)S(1)}, bf16[2,64,1408]{2,1,0:T(8,128)(2,1)S(1)}, u32[]{:S(2)}, u32[]{:S(2)}) collective-permute-start(bf16[2,64,1408]{2,1,0:T(8,128)(2,1)S(1)} %get-tuple-element.409), channel_id=1, source_target_pairs={{0,8},{2,10},{8,0},{10,2},{1,9},{3,11},{9,1},{11,3},{4,12},{6,14},... | collective-permute-start | bytes 1081352 | tf_op jit(solution)/shard_map/ppermute | solution.py:429
  52.0 37.7 %collective-permute-start.17 = (bf16[2,64,1408]{2,1,0:T(8,128)(2,1)S(1)}, bf16[2,64,1408]{2,1,0:T(8,128)(2,1)S(1)}, u32[]{:S(2)}, u32[]{:S(2)}) collective-permute-start(bf16[2,64,1408]{2,1,0:T(8,128)(2,1)S(1)} %get-tuple-element.410), channel_id=1, source_target_pairs={{0,10},{2,8},{8,2},{10,0},{1,11},{3,9},{9,3},{11,1},{4,14},{6,12},... | collective-permute-start | bytes 1081352 | tf_op jit(solution)/shard_map/ppermute | solution.py:429
  53.8 43.6 %collective-permute-start.12 = (bf16[8,64,768]{2,1,0:T(8,128)(2,1)}, bf16[8,64,768]{2,1,0:T(8,128)(2,1)S(1)}, u32[]{:S(2)}, u32[]{:S(2)}) collective-permute-start(bf16[8,64,768]{2,1,0:T(8,128)(2,1)} %pad_maximum_fusion.13.rest_0_), channel_id=1, source_target_pairs={{0,16},{16,0},{1,17},{17,1},{2,18},{18,2},{3,19},{19,3},{4,20},{20... | collective-permute-start | bytes 2359304 | tf_op jit(solution)/shard_map/ppermute | solution.py:439
  116.0 32.5 %collective-permute-start.22 = (bf16[4,64,1408]{2,1,0:T(8,128)(2,1)S(1)}, bf16[4,64,1408]{2,1,0:T(8,128)(2,1)}, u32[]{:S(2)}, u32[]{:S(2)}) collective-permute-start(bf16[4,64,1408]{2,1,0:T(8,128)(2,1)S(1)} %pad_maximum_fusion.15), channel_id=1, source_target_pairs={{0,4},{4,0},{1,5},{5,1},{2,6},{6,2},{3,7},{7,3},{8,12},{12,8},{9,1... | collective-permute-start | bytes 2162696 | tf_op jit(solution)/shard_map/ppermute | solution.py:439
  151.4 42.4 %collective-permute-start.24 = (bf16[2,4,64,1408]{3,2,1,0:T(8,128)(2,1)S(1)}, bf16[2,4,64,1408]{3,2,1,0:T(8,128)(2,1)S(1)}, u32[]{:S(2)}, u32[]{:S(2)}) collective-permute-start(bf16[2,4,64,1408]{3,2,1,0:T(8,128)(2,1)S(1)} %pad_maximum_fusion.5.rest_0_), channel_id=1, source_target_pairs={{0,16},{16,0},{1,17},{17,1},{2,18},{18,2},{3,19},{19,3},{4,20},{20... | collective-permute-start | bytes 4325384 | tf_op jit(solution)/shard_map/ppermute | solution.py:439
  153.3 40.5 %collective-permute-start.26 = (bf16[2,2,64,2048]{3,2,1,0:T(8,128)(2,1)S(1)}, bf16[2,2,64,2048]{3,2,1,0:T(8,128)(2,1)}, u32[]{:S(2)}, u32[]{:S(2)}) collective-permute-start(bf16[2,2,64,2048]{3,2,1,0:T(8,128)(2,1)S(1)} %pad_maximum_fusion.12), channel_id=1, source_target_pairs={{0,2},{2,0},{1,3},{3,1},{4,6},{6,4},{5,7},{7,5},{8,10},{10,8},{9,1... | collective-permute-start | bytes 3145736 | tf_op jit(solution)/shard_map/ppermute | solution.py:433
  154.5 39.3 %collective-permute-start.25 = (bf16[2,2,64,2048]{3,2,1,0:T(8,128)(2,1)S(1)}, bf16[2,2,64,2048]{3,2,1,0:T(8,128)(2,1)S(1)}, u32[]{:S(2)}, u32[]{:S(2)}) collective-permute-start(bf16[2,2,64,2048]{3,2,1,0:T(8,128)(2,1)S(1)} %pad_maximum_fusion.11), channel_id=1, source_target_pairs={{0,8},{8,0},{1,9},{9,1},{2,10},{10,2},{3,11},{11,3},{4,12},{12,4},... | collective-permute-start | bytes 3145736 | tf_op jit(solution)/shard_map/ppermute | solution.py:433
  155.2 36.3 %collective-permute-start.27 = (bf16[4,64,1408]{2,1,0:T(8,128)(2,1)S(1)}, bf16[4,64,1408]{2,1,0:T(8,128)(2,1)}, u32[]{:S(2)}, u32[]{:S(2)}) collective-permute-start(bf16[4,64,1408]{2,1,0:T(8,128)(2,1)S(1)} %pad_maximum_fusion.16), channel_id=1, source_target_pairs={{0,4},{4,0},{1,5},{5,1},{2,6},{6,2},{3,7},{7,3},{8,12},{12,8},{9,1... | collective-permute-start | bytes 2162696 | tf_op jit(solution)/shard_map/ppermute | solution.py:439
  204.0 54.6 %collective-permute-start.34 = (bf16[4,2,2,64,2048]{4,3,2,1,0:T(8,128)(2,1)}, bf16[4,2,2,64,2048]{4,3,2,1,0:T(8,128)(2,1)}, u32[]{:S(2)}, u32[]{:S(2)}) collective-permute-start(bf16[4,2,2,64,2048]{4,3,2,1,0:T(8,128)(2,1)} %pad_maximum_fusion.1.rest_4_), channel_id=1, source_target_pairs={{0,1},{1,0},{2,3},{3,2},{4,5},{5,4},{6,7},{7,6},{8,9},{9,8},{10,11... | collective-permute-start | bytes 12582920 | tf_op jit(solution)/shard_map/ppermute | solution.py:615
  204.0 40.6 %collective-permute-start.35 = (bf16[256,2048]{1,0:T(8,128)(2,1)S(1)}, bf16[256,2048]{1,0:T(8,128)(2,1)S(1)}, u32[]{:S(2)}, u32[]{:S(2)}) collective-permute-start(bf16[256,2048]{1,0:T(8,128)(2,1)S(1)} %pad_maximum_fusion.10), channel_id=1, source_target_pairs={{0,8},{8,0},{1,9},{9,1},{2,10},{10,2},{3,11},{11,3},{4,12},{12,4},... | collective-permute-start | bytes 3145736 | tf_op jit(solution)/shard_map/ppermute | solution.py:433
  205.9 52.6 %collective-permute-start.33 = (bf16[2,4,64,1408]{3,2,1,0:T(8,128)(2,1)S(1)}, bf16[2,4,64,1408]{3,2,1,0:T(8,128)(2,1)}, u32[]{:S(2)}, u32[]{:S(2)}) collective-permute-start(bf16[2,4,64,1408]{3,2,1,0:T(8,128)(2,1)S(1)} %pad_maximum_fusion.6.rest_2_), channel_id=1, source_target_pairs={{0,16},{16,0},{1,17},{17,1},{2,18},{18,2},{3,19},{19,3},{4,20},{20... | collective-permute-start | bytes 4325384 | tf_op jit(solution)/shard_map/ppermute | solution.py:439
  207.5 35.0 %collective-permute-start.29 = (bf16[176,2048]{1,0:T(8,128)(2,1)S(1)}, bf16[176,2048]{1,0:T(8,128)(2,1)S(1)}, u32[]{:S(2)}, u32[]{:S(2)}) collective-permute-start(bf16[176,2048]{1,0:T(8,128)(2,1)S(1)} %copy-done.12), channel_id=1, source_target_pairs={{0,4},{4,0},{1,5},{5,1},{2,6},{6,2},{3,7},{7,3},{8,12},{12,8},{9,1... | collective-permute-start | bytes 2162696 | tf_op jit(solution)/shard_map/ppermute | solution.py:439
  259.8 33.8 %collective-permute-start.39 = (bf16[2,176,2048]{2,1,0:T(8,128)(2,1)}, bf16[2,176,2048]{2,1,0:T(8,128)(2,1)S(1)}, u32[]{:S(2)}, u32[]{:S(2)}) collective-permute-start(bf16[2,176,2048]{2,1,0:T(8,128)(2,1)} %pad_maximum_fusion.7), channel_id=1, source_target_pairs={{0,16},{16,0},{1,17},{17,1},{2,18},{18,2},{3,19},{19,3},{4,20},{20... | collective-permute-start | bytes 4325384 | tf_op jit(solution)/shard_map/ppermute | solution.py:439
  307.0 47.7 %collective-permute-start.42 = (bf16[2,128,256]{2,1,0:T(8,128)(2,1)S(1)}, bf16[2,128,256]{2,1,0:T(8,128)(2,1)S(1)}, u32[]{:S(2)}, u32[]{:S(2)}) collective-permute-start(bf16[2,128,256]{2,1,0:T(8,128)(2,1)S(1)} %get-tuple-element.428), channel_id=1, source_target_pairs={{0,10},{2,8},{8,2},{10,0},{1,11},{3,9},{9,3},{11,1},{4,14},{6,12},... | collective-permute-start | bytes 393224 | tf_op jit(solution)/shard_map/ppermute | solution.py:429
  308.6 46.1 %collective-permute-start.41 = (bf16[2,128,256]{2,1,0:T(8,128)(2,1)S(1)}, bf16[2,128,256]{2,1,0:T(8,128)(2,1)S(1)}, u32[]{:S(2)}, u32[]{:S(2)}) collective-permute-start(bf16[2,128,256]{2,1,0:T(8,128)(2,1)S(1)} %get-tuple-element.429), channel_id=1, source_target_pairs={{0,8},{2,10},{8,0},{10,2},{1,9},{3,11},{9,1},{11,3},{4,12},{6,14},... | collective-permute-start | bytes 393224 | tf_op jit(solution)/shard_map/ppermute | solution.py:429
  309.3 45.4 %collective-permute-start.40 = (bf16[2,128,256]{2,1,0:T(8,128)(2,1)S(1)}, bf16[2,128,256]{2,1,0:T(8,128)(2,1)S(1)}, u32[]{:S(2)}, u32[]{:S(2)}) collective-permute-start(bf16[2,128,256]{2,1,0:T(8,128)(2,1)S(1)} %get-tuple-element.430), channel_id=1, source_target_pairs={{0,2},{2,0},{8,10},{10,8},{1,3},{3,1},{9,11},{11,9},{4,6},{6,4},{1... | collective-permute-start | bytes 393224 | tf_op jit(solution)/shard_map/ppermute | solution.py:429
  354.8 36.3 %collective-permute-start.43 = (bf16[2,1,256,1408]{3,2,1,0:T(8,128)(2,1)}, bf16[2,1,256,1408]{3,2,1,0:T(8,128)(2,1)}, u32[]{:S(2)}, u32[]{:S(2)}) collective-permute-start(bf16[2,1,256,1408]{3,2,1,0:T(8,128)(2,1)} %shard_map.243), channel_id=1, source_target_pairs={{0,16},{16,0},{1,17},{17,1},{2,18},{18,2},{3,19},{19,3},{4,20},{20... | collective-permute-start | bytes 4325384 | tf_op jit(solution)/shard_map/ppermute | solution.py:439
  356.3 33.5 %collective-permute-start.44 = (bf16[128,2048]{1,0:T(8,128)(2,1)}, bf16[128,2048]{1,0:T(8,128)(2,1)S(1)}, u32[]{:S(2)}, u32[]{:S(2)}) collective-permute-start(bf16[128,2048]{1,0:T(8,128)(2,1)} %get-tuple-element.304), channel_id=1, source_target_pairs={{0,2},{2,0},{8,10},{10,8},{1,3},{3,1},{9,11},{11,9},{4,6},{6,4},{1... | collective-permute-start | bytes 1572872 | tf_op jit(solution)/shard_map/ppermute | solution.py:429
  357.0 32.8 %collective-permute-start.45 = (bf16[128,2048]{1,0:T(8,128)(2,1)}, bf16[128,2048]{1,0:T(8,128)(2,1)S(1)}, u32[]{:S(2)}, u32[]{:S(2)}) collective-permute-start(bf16[128,2048]{1,0:T(8,128)(2,1)} %get-tuple-element.305), channel_id=1, source_target_pairs={{0,8},{2,10},{8,0},{10,2},{1,9},{3,11},{9,1},{11,3},{4,12},{6,14},... | collective-permute-start | bytes 1572872 | tf_op jit(solution)/shard_map/ppermute | solution.py:429
  358.4 31.4 %collective-permute-start.46 = (bf16[128,2048]{1,0:T(8,128)(2,1)}, bf16[128,2048]{1,0:T(8,128)(2,1)S(1)}, u32[]{:S(2)}, u32[]{:S(2)}) collective-permute-start(bf16[128,2048]{1,0:T(8,128)(2,1)} %get-tuple-element.306), channel_id=1, source_target_pairs={{0,10},{2,8},{8,2},{10,0},{1,11},{3,9},{9,3},{11,1},{4,14},{6,12},... | collective-permute-start | bytes 1572872 | tf_op jit(solution)/shard_map/ppermute | solution.py:429
  415.4 39.1 %collective-permute-start.54 = (bf16[128,2048]{1,0:T(8,128)(2,1)}, bf16[128,2048]{1,0:T(8,128)(2,1)}, u32[]{:S(2)}, u32[]{:S(2)}) collective-permute-start(bf16[128,2048]{1,0:T(8,128)(2,1)} %get-tuple-element.329), channel_id=1, source_target_pairs={{0,10},{2,8},{8,2},{10,0},{1,11},{3,9},{9,3},{11,1},{4,14},{6,12},... | collective-permute-start | bytes 1572872 | tf_op jit(solution)/shard_map/ppermute | solution.py:429
  416.8 43.0 %collective-permute-start.47 = (bf16[2,1,256,1408]{3,2,1,0:T(8,128)(2,1)}, bf16[2,1,256,1408]{3,2,1,0:T(8,128)(2,1)}, u32[]{:S(2)}, u32[]{:S(2)}) collective-permute-start(bf16[2,1,256,1408]{3,2,1,0:T(8,128)(2,1)} %shard_map.245), channel_id=1, source_target_pairs={{0,16},{16,0},{1,17},{17,1},{2,18},{18,2},{3,19},{19,3},{4,20},{20... | collective-permute-start | bytes 4325384 | tf_op jit(solution)/shard_map/ppermute | solution.py:439
  418.3 39.4 %collective-permute-start.51 = (bf16[1,256,1408]{2,1,0:T(8,128)(2,1)}, bf16[1,256,1408]{2,1,0:T(8,128)(2,1)}, u32[]{:S(2)}, u32[]{:S(2)}) collective-permute-start(bf16[1,256,1408]{2,1,0:T(8,128)(2,1)} %fusion.5), channel_id=1, source_target_pairs={{0,4},{4,0},{1,5},{5,1},{2,6},{6,2},{3,7},{7,3},{8,12},{12,8},{9,1... | collective-permute-start | bytes 2162696 | tf_op jit(solution)/shard_map/ppermute | solution.py:439
  489.1 36.4 %collective-permute-start.59 = (bf16[2,2,256,768]{3,2,1,0:T(8,128)(2,1)}, bf16[2,2,256,768]{3,2,1,0:T(8,128)(2,1)}, u32[]{:S(2)}, u32[]{:S(2)}) collective-permute-start(bf16[2,2,256,768]{3,2,1,0:T(8,128)(2,1)} %shard_map.251), channel_id=1, source_target_pairs={{0,16},{16,0},{1,17},{17,1},{2,18},{18,2},{3,19},{19,3},{4,20},{20... | collective-permute-start | bytes 4718600 | tf_op jit(solution)/shard_map/ppermute | solution.py:439
  490.5 32.6 %collective-permute-start.60 = (bf16[1,256,1408]{2,1,0:T(8,128)(2,1)}, bf16[1,256,1408]{2,1,0:T(8,128)(2,1)}, u32[]{:S(2)}, u32[]{:S(2)}) collective-permute-start(bf16[1,256,1408]{2,1,0:T(8,128)(2,1)} %fusion.6), channel_id=1, source_target_pairs={{0,4},{4,0},{1,5},{5,1},{2,6},{6,2},{3,7},{7,3},{8,12},{12,8},{9,1... | collective-permute-start | bytes 2162696 | tf_op jit(solution)/shard_map/ppermute | solution.py:439
  529.4 39.6 %collective-permute-start.64 = (bf16[128,2048]{1,0:T(8,128)(2,1)}, bf16[128,2048]{1,0:T(8,128)(2,1)}, u32[]{:S(2)}, u32[]{:S(2)}) collective-permute-start(bf16[128,2048]{1,0:T(8,128)(2,1)} %get-tuple-element.360), channel_id=1, source_target_pairs={{0,10},{2,8},{8,2},{10,0},{1,11},{3,9},{9,3},{11,1},{4,14},{6,12},... | collective-permute-start | bytes 1572872 | tf_op jit(solution)/shard_map/ppermute | solution.py:429
  533.2 39.1 %collective-permute-start.65 = (bf16[2,176,2048]{2,1,0:T(8,128)(2,1)}, bf16[2,176,2048]{2,1,0:T(8,128)(2,1)}, u32[]{:S(2)}, u32[]{:S(2)}) collective-permute-start(bf16[2,176,2048]{2,1,0:T(8,128)(2,1)} %dynamic-slice_bitcast_fusion), channel_id=1, source_target_pairs={{0,16},{16,0},{1,17},{17,1},{2,18},{18,2},{3,19},{19,3},{4,20},{20... | collective-permute-start | bytes 4325384 | tf_op jit(solution)/shard_map/ppermute | solution.py:439
  534.6 36.5 %collective-permute-start.61 = (bf16[2,256,768]{2,1,0:T(8,128)(2,1)}, bf16[2,256,768]{2,1,0:T(8,128)(2,1)}, u32[]{:S(2)}, u32[]{:S(2)}) collective-permute-start(bf16[2,256,768]{2,1,0:T(8,128)(2,1)} %fusion.4), channel_id=1, source_target_pairs={{0,4},{4,0},{1,5},{5,1},{2,6},{6,2},{3,7},{7,3},{8,12},{12,8},{9,1... | collective-permute-start | bytes 2359304 | tf_op jit(solution)/shard_map/ppermute | solution.py:439
  574.6 30.8 %collective-permute-start.72 = (bf16[2,64,2048]{2,1,0:T(8,128)(2,1)S(1)}, bf16[2,64,2048]{2,1,0:T(8,128)(2,1)S(1)}, u32[]{:S(2)}, u32[]{:S(2)}) collective-permute-start(bf16[2,64,2048]{2,1,0:T(8,128)(2,1)S(1)} %dynamic-slice_bitcast_fusion.1), channel_id=1, source_target_pairs={{0,16},{16,0},{1,17},{17,1},{2,18},{18,2},{3,19},{19,3},{4,20},{20... | collective-permute-start | bytes 1572872 | tf_op jit(solution)/shard_map/ppermute | solution.py:439
  580.3 62.6 %collective-permute-start.78 = (bf16[176,2048]{1,0:T(8,128)(2,1)}, bf16[176,2048]{1,0:T(8,128)(2,1)}, u32[]{:S(2)}, u32[]{:S(2)}) collective-permute-start(bf16[176,2048]{1,0:T(8,128)(2,1)} %fusion.7), channel_id=1, source_target_pairs={{0,4},{4,0},{1,5},{5,1},{2,6},{6,2},{3,7},{7,3},{8,12},{12,8},{9,1... | collective-permute-start | bytes 2162696 | tf_op jit(solution)/shard_map/ppermute | solution.py:439
  (100 other events, 1356.9 us)
